TPU v7x, 512 devices: a whole 4x8x8 slice. The times are simulated.
512 devices in a mesh: grp: 16 (over x, y_lo), blk: 32 (over y_hi, z, core).
Axes of the slice: x: 4, y: 8 (y_hi: 2, y_lo: 4; y = y_hi * 4 + y_lo), z: 8, core: 2. Of those that a mesh axis runs over, the one named last changes fastest.
Arguments:
- image_emb: bfloat16 [131072, 1152], P(('grp', 'blk')), may hold values from -0.1796875 to 0.1796875
- text_emb: bfloat16 [131072, 1152], P(('grp', 'blk')), may hold values from -0.1796875 to 0.1796875
- image_pair_index: int32 [131072], P(('grp', 'blk')), may hold values from 0 to 1023
- text_ids: int32 [131072], P(('grp', 'blk')), may hold values from 0 to 1023
- exponent_sharpness: float32 [1], replicated, may hold values from 1.5 to 2.5
- additive_offset: float32 [1], replicated, may hold values from -3 to -1
- objective_adjoint: float32 [1], replicated, may hold values from 64 to 256
Outputs:
- grad_image: float32 [131072, 1152], P(('grp', 'blk'))
- grad_text: float32 [131072, 1152], P(('grp', 'blk'))
All inputs are finite; a program needn't handle non-finite values.
Results may differ from a plain program's by a relative error of at most 0.0044.
Values may be sent and summed in bfloat16 or wider, within the bound.
A program may use at most 64 MiB of HBM per device.

v0:
```python
import jax
import jax.numpy as jnp
from jax import lax
from jax.sharding import PartitionSpec as P

SPAN = 4
HOPS = 2


EPSILON = 1e-06


def from_behind(block, axis, distance):
    devices = range(lax.axis_size(axis))
    route = [((i - distance) % len(devices), i) for i in devices]
    return lax.ppermute(block, axis, route)


def normalize(rows):
    wide = rows.astype(jnp.float32)
    inverse = lax.rsqrt(jnp.sum(wide * wide, axis=-1, keepdims=True) + EPSILON)
    unit = wide * inverse
    return (inverse, unit, unit.astype(jnp.bfloat16))


def finish(inverse, unit, grad_unit):
    return inverse * (grad_unit - unit * jnp.sum(unit * grad_unit, axis=-1, keepdims=True))


def loss_coefficient_matrix(
    normalized_left,
    normalized_right,
    left_pair_label,
    right_pair_label,
    sharpness_factor,
    shift_term_value,
    weighting_factor,
):
    embedding_inner_grid = lax.dot_general(
        normalized_left,
        normalized_right,
        (((1,), (1,)), ((), ())),
        preferred_element_type=jnp.float32,
    )
    match_score = sharpness_factor * embedding_inner_grid + shift_term_value
    sign = jnp.where(left_pair_label[:, None] == right_pair_label[None, :], 1.0, -1.0).astype(
        jnp.float32
    )
    return (weighting_factor * sign * jax.nn.sigmoid(-sign * match_score)).astype(jnp.bfloat16)


def transpose_product(coef, rows):
    return lax.dot_general(coef, rows, (((0,), (0,)), ((), ())), preferred_element_type=jnp.float32)


def body(
    image_emb,
    text_emb,
    image_pair_index,
    text_ids,
    exponent_sharpness,
    additive_offset,
    objective_adjoint,
):
    batch_height = image_emb.shape[0]
    inv_image, unit_image, normalized_image = normalize(image_emb)
    inv_text, unit_text, text_hat = normalize(text_emb)
    sharpness_factor = jnp.exp(exponent_sharpness[0])
    shift_term_value = additive_offset[0]
    weighting_factor = -(objective_adjoint[0] * sharpness_factor / batch_height)
    d_image = jnp.zeros(unit_image.shape, jnp.float32)
    carried = jnp.zeros(unit_text.shape, jnp.float32)
    incoming_visitor = text_hat
    visual_label = text_ids
    for hop_index in range(HOPS):
        if hop_index > 0:
            incoming_visitor, visual_label = from_behind((incoming_visitor, visual_label), "grp", 1)
            carried = from_behind(carried, "grp", 1)
        for cycle_index in range(SPAN):
            if cycle_index > 0:
                incoming_visitor, visual_label = from_behind(
                    (incoming_visitor, visual_label), "blk", 1
                )
                carried = from_behind(carried, "blk", 1)
            coef = loss_coefficient_matrix(
                normalized_image,
                incoming_visitor,
                image_pair_index,
                visual_label,
                sharpness_factor,
                shift_term_value,
                weighting_factor,
            )
            d_image = d_image + jnp.dot(coef, incoming_visitor, preferred_element_type=jnp.float32)
            carried = carried + transpose_product(coef, normalized_image)
    d_text = from_behind(carried, "blk", -((SPAN - 1) * HOPS))
    d_text = from_behind(d_text, "grp", -(HOPS - 1))
    grad_image = finish(inv_image, unit_image, d_image)
    grad_text = finish(inv_text, unit_text, d_text)
    return (grad_image, grad_text)


def solution(mesh):
    placed = (
        P(("grp", "blk"), None),
        P(("grp", "blk"), None),
        P(("grp", "blk")),
        P(("grp", "blk")),
        P(),
        P(),
        P(),
    )
    return jax.shard_map(
        body,
        mesh=mesh,
        in_specs=placed,
        out_specs=(P(("grp", "blk"), None), P(("grp", "blk"), None)),
        check_vma=False,
    )
```

profile of v0, /device:TPU:462, one launch (start us, length us, event | category | flops | bytes accessed | tf_op | source)
XLA Modules:
  0.0 458.9 jit_solution(17377089008888750737)
XLA Ops:
  6.4 1.9 collective-permute-start.14
  8.3 1.9 collective-permute-start.1
  10.2 1.9 collective-permute-start
  12.1 18.1 %collective-permute-done.1 = bf16[256,1152]{1,0:T(8,128)(2,1)S(1)} collective-permute-done((bf16[256,1152]{1,0:T(8,128)(2,1)S(1)}, bf16[256,1152]{1,0:T(8,128)(2,1)S(1)}, u32[]{:S(2)}, u32[]{:S(2)}) %collective-permute-start.1) | collective-permute-done | bytes 589856 | tf_op jit(solution)/shard_map/ppermute | solution.py:16
  31.1 18.2 %collective-permute-start.15 = (f32[256,1152]{1,0:T(8,128)S(1)}, f32[256,1152]{1,0:T(8,128)S(1)}, u32[]{:S(2)}, u32[]{:S(2)}) collective-permute-start(f32[256,1152]{1,0:T(8,128)S(1)} %convolution_add_fusion), channel_id=1, source_target_pairs={{31,0},{0,1},{1,2},{2,3},{3,4},{4,5},{5,6},{6,7},{7,8},{8,9},{9,10... | collective-permute-start | bytes 3538952 | tf_op jit(solution)/shard_map/ppermute | solution.py:16
  49.4 10.4 %collective-permute-start.3 = (bf16[256,1152]{1,0:T(8,128)(2,1)S(1)}, bf16[256,1152]{1,0:T(8,128)(2,1)S(1)}, u32[]{:S(2)}, u32[]{:S(2)}) collective-permute-start(bf16[256,1152]{1,0:T(8,128)(2,1)S(1)} %collective-permute-done.1), channel_id=1, source_target_pairs={{31,0},{0,1},{1,2},{2,3},{3,4},{4,5},{5,6},{6,7},{7,8},{8,9},{9,10... | collective-permute-start | bytes 1769480 | tf_op jit(solution)/shard_map/ppermute | solution.py:16
  59.8 1.9 collective-permute-start.2
  62.1 2.6 collective-permute-done.2
  65.2 33.7 %collective-permute-start.16 = (f32[256,1152]{1,0:T(8,128)S(1)}, f32[256,1152]{1,0:T(8,128)S(1)}, u32[]{:S(2)}, u32[]{:S(2)}) collective-permute-start(f32[256,1152]{1,0:T(8,128)S(1)} %fusion.111), channel_id=1, source_target_pairs={{31,0},{0,1},{1,2},{2,3},{3,4},{4,5},{5,6},{6,7},{7,8},{8,9},{9,10... | collective-permute-start | bytes 3538952 | tf_op jit(solution)/shard_map/ppermute | solution.py:16
  99.0 10.4 %collective-permute-start.5 = (bf16[256,1152]{1,0:T(8,128)(2,1)S(1)}, bf16[256,1152]{1,0:T(8,128)(2,1)S(1)}, u32[]{:S(2)}, u32[]{:S(2)}) collective-permute-start(bf16[256,1152]{1,0:T(8,128)(2,1)S(1)} %collective-permute-done.3), channel_id=1, source_target_pairs={{31,0},{0,1},{1,2},{2,3},{3,4},{4,5},{5,6},{6,7},{7,8},{8,9},{9,10... | collective-permute-start | bytes 1769480 | tf_op jit(solution)/shard_map/ppermute | solution.py:16
  109.4 1.9 collective-permute-start.4
  111.7 2.6 collective-permute-done.4
  114.8 1.9 collective-permute-start.17
  116.7 1.9 collective-permute-start.7
  118.6 1.9 collective-permute-start.6
  120.6 32.7 %collective-permute-done.7 = bf16[256,1152]{1,0:T(8,128)(2,1)S(1)} collective-permute-done((bf16[256,1152]{1,0:T(8,128)(2,1)S(1)}, bf16[256,1152]{1,0:T(8,128)(2,1)S(1)}, u32[]{:S(2)}, u32[]{:S(2)}) %collective-permute-start.7) | collective-permute-done | bytes 589856 | tf_op jit(solution)/shard_map/ppermute | solution.py:16
  154.3 18.1 %collective-permute-start.18 = (f32[256,1152]{1,0:T(8,128)S(1)}, f32[256,1152]{1,0:T(8,128)S(1)}, u32[]{:S(2)}, u32[]{:S(2)}) collective-permute-start(f32[256,1152]{1,0:T(8,128)S(1)} %fusion.99), channel_id=1, source_target_pairs={{31,0},{0,1},{1,2},{2,3},{3,4},{4,5},{5,6},{6,7},{7,8},{8,9},{9,10... | collective-permute-start | bytes 3538952 | tf_op jit(solution)/shard_map/ppermute | solution.py:16
  172.3 11.6 %collective-permute-start.9 = (bf16[256,1152]{1,0:T(8,128)(2,1)S(1)}, bf16[256,1152]{1,0:T(8,128)(2,1)S(1)}, u32[]{:S(2)}, u32[]{:S(2)}) collective-permute-start(bf16[256,1152]{1,0:T(8,128)(2,1)S(1)} %collective-permute-done.7), channel_id=1, source_target_pairs={{31,0},{0,1},{1,2},{2,3},{3,4},{4,5},{5,6},{6,7},{7,8},{8,9},{9,10... | collective-permute-start | bytes 1769480 | tf_op jit(solution)/shard_map/ppermute | solution.py:16
  183.9 1.9 collective-permute-start.8
  186.2 2.6 collective-permute-done.8
  189.3 15.1 %collective-permute-start.19 = (f32[256,1152]{1,0:T(8,128)S(1)}, f32[256,1152]{1,0:T(8,128)S(1)}, u32[]{:S(2)}, u32[]{:S(2)}) collective-permute-start(f32[256,1152]{1,0:T(8,128)S(1)} %fusion.93), channel_id=1, source_target_pairs={{31,0},{0,1},{1,2},{2,3},{3,4},{4,5},{5,6},{6,7},{7,8},{8,9},{9,10... | collective-permute-start | bytes 3538952 | tf_op jit(solution)/shard_map/ppermute | solution.py:16
  204.4 10.4 %collective-permute-start.11 = (bf16[256,1152]{1,0:T(8,128)(2,1)S(1)}, bf16[256,1152]{1,0:T(8,128)(2,1)S(1)}, u32[]{:S(2)}, u32[]{:S(2)}) collective-permute-start(bf16[256,1152]{1,0:T(8,128)(2,1)S(1)} %collective-permute-done.9), channel_id=1, source_target_pairs={{31,0},{0,1},{1,2},{2,3},{3,4},{4,5},{5,6},{6,7},{7,8},{8,9},{9,10... | collective-permute-start | bytes 1769480 | tf_op jit(solution)/shard_map/ppermute | solution.py:16
  214.9 1.9 collective-permute-start.10
  217.2 2.6 collective-permute-done.10
  220.3 45.8 %collective-permute-start.20 = (f32[256,1152]{1,0:T(8,128)S(1)}, f32[256,1152]{1,0:T(8,128)S(1)}, u32[]{:S(2)}, u32[]{:S(2)}) collective-permute-start(f32[256,1152]{1,0:T(8,128)S(1)} %fusion.87), channel_id=1, source_target_pairs={{31,0},{0,1},{1,2},{2,3},{3,4},{4,5},{5,6},{6,7},{7,8},{8,9},{9,10... | collective-permute-start | bytes 3538952 | tf_op jit(solution)/shard_map/ppermute | solution.py:16
  266.1 10.4 %collective-permute-start.13 = (bf16[256,1152]{1,0:T(8,128)(2,1)S(1)}, bf16[256,1152]{1,0:T(8,128)(2,1)S(1)}, u32[]{:S(2)}, u32[]{:S(2)}) collective-permute-start(bf16[256,1152]{1,0:T(8,128)(2,1)S(1)} %collective-permute-done.11), channel_id=1, source_target_pairs={{31,0},{0,1},{1,2},{2,3},{3,4},{4,5},{5,6},{6,7},{7,8},{8,9},{9,10... | collective-permute-start | bytes 1769480 | tf_op jit(solution)/shard_map/ppermute | solution.py:16
  276.9 1.9 collective-permute-start.12
  279.7 2.1 collective-permute-done.12
  282.3 2.1 collective-permute-start.21
  286.2 59.0 %collective-permute-done.21 = f32[256,1152]{1,0:T(8,128)S(1)} collective-permute-done((f32[256,1152]{1,0:T(8,128)S(1)}, f32[256,1152]{1,0:T(8,128)S(1)}, u32[]{:S(2)}, u32[]{:S(2)}) %collective-permute-start.21) | collective-permute-done | bytes 1179680 | tf_op jit(solution)/shard_map/ppermute | solution.py:16
  345.2 21.9 %collective-permute-start.22 = (f32[256,1152]{1,0:T(8,128)S(1)}, f32[256,1152]{1,0:T(8,128)S(1)}, u32[]{:S(2)}, u32[]{:S(2)}) collective-permute-start(f32[256,1152]{1,0:T(8,128)S(1)} %collective-permute-done.21), channel_id=1, source_target_pairs={{32,0},{64,32},{96,64},{128,96},{160,128},{192,160},{224,192},{256... | collective-permute-start | bytes 3538952 | tf_op jit(solution)/shard_map/ppermute | solution.py:16
  369.3 88.0 %collective-permute-done.22 = f32[256,1152]{1,0:T(8,128)S(1)} collective-permute-done((f32[256,1152]{1,0:T(8,128)S(1)}, f32[256,1152]{1,0:T(8,128)S(1)}, u32[]{:S(2)}, u32[]{:S(2)}) %collective-permute-start.22) | collective-permute-done | bytes 1179680 | tf_op jit(solution)/shard_map/ppermute | solution.py:16
  (54 shorter events, 16.3 us)
Async XLA Ops:
  0.6 4.8 %copy-start = (bf16[256,1152]{1,0:T(8,128)(2,1)S(1)}, bf16[256,1152]{1,0:T(8,128)(2,1)}, u32[]{:S(2)}) copy-start(bf16[256,1152]{1,0:T(8,128)(2,1)} %param.7) | copy-start | bytes 1769476
  0.6 2.7 copy-start.1
  0.7 4.8 %copy-start.3 = (s32[256]{0:T(256)S(1)}, s32[256]{0:T(256)}, u32[]{:S(2)}) copy-start(s32[256]{0:T(256)} %param.10) | copy-start | bytes 3076
  0.7 4.8 %copy-start.2 = (s32[256]{0:T(256)S(1)}, s32[256]{0:T(256)}, u32[]{:S(2)}) copy-start(s32[256]{0:T(256)} %param.9) | copy-start | bytes 3076
  6.4 24.2 %collective-permute-start.14 = (f32[256,1152]{1,0:T(8,128)S(1)}, f32[256,1152]{1,0:T(8,128)S(1)}, u32[]{:S(2)}, u32[]{:S(2)}) collective-permute-start(f32[256,1152]{1,0:T(8,128)S(1)} %fusion.207), channel_id=1, source_target_pairs={{31,0},{0,1},{1,2},{2,3},{3,4},{4,5},{5,6},{6,7},{7,8},{8,9},{9,10... | collective-permute-start | bytes 3538952 | tf_op jit(solution)/shard_map/ppermute | solution.py:16
  8.3 21.9 %collective-permute-start.1 = (bf16[256,1152]{1,0:T(8,128)(2,1)S(1)}, bf16[256,1152]{1,0:T(8,128)(2,1)S(1)}, u32[]{:S(2)}, u32[]{:S(2)}) collective-permute-start(bf16[256,1152]{1,0:T(8,128)(2,1)S(1)} %fusion.2), channel_id=1, source_target_pairs={{31,0},{0,1},{1,2},{2,3},{3,4},{4,5},{5,6},{6,7},{7,8},{8,9},{9,10... | collective-permute-start | bytes 1769480 | tf_op jit(solution)/shard_map/ppermute | solution.py:16
  10.2 20.4 %collective-permute-start = (s32[256]{0:T(256)S(1)}, s32[256]{0:T(256)S(1)}, u32[]{:S(2)}, u32[]{:S(2)}) collective-permute-start(s32[256]{0:T(256)S(1)} %copy-done.3), channel_id=1, source_target_pairs={{31,0},{0,1},{1,2},{2,3},{3,4},{4,5},{5,6},{6,7},{7,8},{8,9},{9,10... | collective-permute-start | bytes 3080 | tf_op jit(solution)/shard_map/ppermute | solution.py:16
  31.1 33.6 %collective-permute-start.15 = (f32[256,1152]{1,0:T(8,128)S(1)}, f32[256,1152]{1,0:T(8,128)S(1)}, u32[]{:S(2)}, u32[]{:S(2)}) collective-permute-start(f32[256,1152]{1,0:T(8,128)S(1)} %convolution_add_fusion), channel_id=1, source_target_pairs={{31,0},{0,1},{1,2},{2,3},{3,4},{4,5},{5,6},{6,7},{7,8},{8,9},{9,10... | collective-permute-start | bytes 3538952 | tf_op jit(solution)/shard_map/ppermute | solution.py:16
  49.4 12.3 %collective-permute-start.3 = (bf16[256,1152]{1,0:T(8,128)(2,1)S(1)}, bf16[256,1152]{1,0:T(8,128)(2,1)S(1)}, u32[]{:S(2)}, u32[]{:S(2)}) collective-permute-start(bf16[256,1152]{1,0:T(8,128)(2,1)S(1)} %collective-permute-done.1), channel_id=1, source_target_pairs={{31,0},{0,1},{1,2},{2,3},{3,4},{4,5},{5,6},{6,7},{7,8},{8,9},{9,10... | collective-permute-start | bytes 1769480 | tf_op jit(solution)/shard_map/ppermute | solution.py:16
  59.8 4.9 %collective-permute-start.2 = (s32[256]{0:T(256)S(1)}, s32[256]{0:T(256)S(1)}, u32[]{:S(2)}, u32[]{:S(2)}) collective-permute-start(s32[256]{0:T(256)S(1)} %collective-permute-done), channel_id=1, source_target_pairs={{31,0},{0,1},{1,2},{2,3},{3,4},{4,5},{5,6},{6,7},{7,8},{8,9},{9,10... | collective-permute-start | bytes 3080 | tf_op jit(solution)/shard_map/ppermute | solution.py:16
  65.2 49.0 %collective-permute-start.16 = (f32[256,1152]{1,0:T(8,128)S(1)}, f32[256,1152]{1,0:T(8,128)S(1)}, u32[]{:S(2)}, u32[]{:S(2)}) collective-permute-start(f32[256,1152]{1,0:T(8,128)S(1)} %fusion.111), channel_id=1, source_target_pairs={{31,0},{0,1},{1,2},{2,3},{3,4},{4,5},{5,6},{6,7},{7,8},{8,9},{9,10... | collective-permute-start | bytes 3538952 | tf_op jit(solution)/shard_map/ppermute | solution.py:16
  99.0 12.3 %collective-permute-start.5 = (bf16[256,1152]{1,0:T(8,128)(2,1)S(1)}, bf16[256,1152]{1,0:T(8,128)(2,1)S(1)}, u32[]{:S(2)}, u32[]{:S(2)}) collective-permute-start(bf16[256,1152]{1,0:T(8,128)(2,1)S(1)} %collective-permute-done.3), channel_id=1, source_target_pairs={{31,0},{0,1},{1,2},{2,3},{3,4},{4,5},{5,6},{6,7},{7,8},{8,9},{9,10... | collective-permute-start | bytes 1769480 | tf_op jit(solution)/shard_map/ppermute | solution.py:16
  109.4 4.9 %collective-permute-start.4 = (s32[256]{0:T(256)S(1)}, s32[256]{0:T(256)S(1)}, u32[]{:S(2)}, u32[]{:S(2)}) collective-permute-start(s32[256]{0:T(256)S(1)} %collective-permute-done.2), channel_id=1, source_target_pairs={{31,0},{0,1},{1,2},{2,3},{3,4},{4,5},{5,6},{6,7},{7,8},{8,9},{9,10... | collective-permute-start | bytes 3080 | tf_op jit(solution)/shard_map/ppermute | solution.py:16
  114.8 38.9 %collective-permute-start.17 = (f32[256,1152]{1,0:T(8,128)S(1)}, f32[256,1152]{1,0:T(8,128)S(1)}, u32[]{:S(2)}, u32[]{:S(2)}) collective-permute-start(f32[256,1152]{1,0:T(8,128)S(1)} %fusion.105), channel_id=1, source_target_pairs={{480,0},{0,32},{32,64},{64,96},{96,128},{128,160},{160,192},{192,2... | collective-permute-start | bytes 3538952 | tf_op jit(solution)/shard_map/ppermute | solution.py:16
  116.7 36.6 %collective-permute-start.7 = (bf16[256,1152]{1,0:T(8,128)(2,1)S(1)}, bf16[256,1152]{1,0:T(8,128)(2,1)S(1)}, u32[]{:S(2)}, u32[]{:S(2)}) collective-permute-start(bf16[256,1152]{1,0:T(8,128)(2,1)S(1)} %collective-permute-done.5), channel_id=1, source_target_pairs={{480,0},{0,32},{32,64},{64,96},{96,128},{128,160},{160,192},{192,2... | collective-permute-start | bytes 1769480 | tf_op jit(solution)/shard_map/ppermute | solution.py:16
  118.6 35.1 %collective-permute-start.6 = (s32[256]{0:T(256)S(1)}, s32[256]{0:T(256)S(1)}, u32[]{:S(2)}, u32[]{:S(2)}) collective-permute-start(s32[256]{0:T(256)S(1)} %collective-permute-done.4), channel_id=1, source_target_pairs={{480,0},{0,32},{32,64},{64,96},{96,128},{128,160},{160,192},{192,2... | collective-permute-start | bytes 3080 | tf_op jit(solution)/shard_map/ppermute | solution.py:16
  154.3 34.5 %collective-permute-start.18 = (f32[256,1152]{1,0:T(8,128)S(1)}, f32[256,1152]{1,0:T(8,128)S(1)}, u32[]{:S(2)}, u32[]{:S(2)}) collective-permute-start(f32[256,1152]{1,0:T(8,128)S(1)} %fusion.99), channel_id=1, source_target_pairs={{31,0},{0,1},{1,2},{2,3},{3,4},{4,5},{5,6},{6,7},{7,8},{8,9},{9,10... | collective-permute-start | bytes 3538952 | tf_op jit(solution)/shard_map/ppermute | solution.py:16
  172.3 13.5 %collective-permute-start.9 = (bf16[256,1152]{1,0:T(8,128)(2,1)S(1)}, bf16[256,1152]{1,0:T(8,128)(2,1)S(1)}, u32[]{:S(2)}, u32[]{:S(2)}) collective-permute-start(bf16[256,1152]{1,0:T(8,128)(2,1)S(1)} %collective-permute-done.7), channel_id=1, source_target_pairs={{31,0},{0,1},{1,2},{2,3},{3,4},{4,5},{5,6},{6,7},{7,8},{8,9},{9,10... | collective-permute-start | bytes 1769480 | tf_op jit(solution)/shard_map/ppermute | solution.py:16
  183.9 4.9 %collective-permute-start.8 = (s32[256]{0:T(256)S(1)}, s32[256]{0:T(256)S(1)}, u32[]{:S(2)}, u32[]{:S(2)}) collective-permute-start(s32[256]{0:T(256)S(1)} %collective-permute-done.6), channel_id=1, source_target_pairs={{31,0},{0,1},{1,2},{2,3},{3,4},{4,5},{5,6},{6,7},{7,8},{8,9},{9,10... | collective-permute-start | bytes 3080 | tf_op jit(solution)/shard_map/ppermute | solution.py:16
  189.3 30.5 %collective-permute-start.19 = (f32[256,1152]{1,0:T(8,128)S(1)}, f32[256,1152]{1,0:T(8,128)S(1)}, u32[]{:S(2)}, u32[]{:S(2)}) collective-permute-start(f32[256,1152]{1,0:T(8,128)S(1)} %fusion.93), channel_id=1, source_target_pairs={{31,0},{0,1},{1,2},{2,3},{3,4},{4,5},{5,6},{6,7},{7,8},{8,9},{9,10... | collective-permute-start | bytes 3538952 | tf_op jit(solution)/shard_map/ppermute | solution.py:16
  204.4 12.4 %collective-permute-start.11 = (bf16[256,1152]{1,0:T(8,128)(2,1)S(1)}, bf16[256,1152]{1,0:T(8,128)(2,1)S(1)}, u32[]{:S(2)}, u32[]{:S(2)}) collective-permute-start(bf16[256,1152]{1,0:T(8,128)(2,1)S(1)} %collective-permute-done.9), channel_id=1, source_target_pairs={{31,0},{0,1},{1,2},{2,3},{3,4},{4,5},{5,6},{6,7},{7,8},{8,9},{9,10... | collective-permute-start | bytes 1769480 | tf_op jit(solution)/shard_map/ppermute | solution.py:16
  214.9 4.9 %collective-permute-start.10 = (s32[256]{0:T(256)S(1)}, s32[256]{0:T(256)S(1)}, u32[]{:S(2)}, u32[]{:S(2)}) collective-permute-start(s32[256]{0:T(256)S(1)} %collective-permute-done.8), channel_id=1, source_target_pairs={{31,0},{0,1},{1,2},{2,3},{3,4},{4,5},{5,6},{6,7},{7,8},{8,9},{9,10... | collective-permute-start | bytes 3080 | tf_op jit(solution)/shard_map/ppermute | solution.py:16
  220.3 61.5 %collective-permute-start.20 = (f32[256,1152]{1,0:T(8,128)S(1)}, f32[256,1152]{1,0:T(8,128)S(1)}, u32[]{:S(2)}, u32[]{:S(2)}) collective-permute-start(f32[256,1152]{1,0:T(8,128)S(1)} %fusion.87), channel_id=1, source_target_pairs={{31,0},{0,1},{1,2},{2,3},{3,4},{4,5},{5,6},{6,7},{7,8},{8,9},{9,10... | collective-permute-start | bytes 3538952 | tf_op jit(solution)/shard_map/ppermute | solution.py:16
  266.1 13.2 %collective-permute-start.13 = (bf16[256,1152]{1,0:T(8,128)(2,1)S(1)}, bf16[256,1152]{1,0:T(8,128)(2,1)S(1)}, u32[]{:S(2)}, u32[]{:S(2)}) collective-permute-start(bf16[256,1152]{1,0:T(8,128)(2,1)S(1)} %collective-permute-done.11), channel_id=1, source_target_pairs={{31,0},{0,1},{1,2},{2,3},{3,4},{4,5},{5,6},{6,7},{7,8},{8,9},{9,10... | collective-permute-start | bytes 1769480 | tf_op jit(solution)/shard_map/ppermute | solution.py:16
  276.9 4.9 %collective-permute-start.12 = (s32[256]{0:T(256)S(1)}, s32[256]{0:T(256)S(1)}, u32[]{:S(2)}, u32[]{:S(2)}) collective-permute-start(s32[256]{0:T(256)S(1)} %collective-permute-done.10), channel_id=1, source_target_pairs={{31,0},{0,1},{1,2},{2,3},{3,4},{4,5},{5,6},{6,7},{7,8},{8,9},{9,10... | collective-permute-start | bytes 3080 | tf_op jit(solution)/shard_map/ppermute | solution.py:16
  282.3 62.9 %collective-permute-start.21 = (f32[256,1152]{1,0:T(8,128)S(1)}, f32[256,1152]{1,0:T(8,128)S(1)}, u32[]{:S(2)}, u32[]{:S(2)}) collective-permute-start(f32[256,1152]{1,0:T(8,128)S(1)} %fusion.81), channel_id=1, source_target_pairs={{6,0},{7,1},{8,2},{9,3},{10,4},{11,5},{12,6},{13,7},{14,8},{15,9},... | collective-permute-start | bytes 3538952 | tf_op jit(solution)/shard_map/ppermute | solution.py:16
  345.2 112.1 %collective-permute-start.22 = (f32[256,1152]{1,0:T(8,128)S(1)}, f32[256,1152]{1,0:T(8,128)S(1)}, u32[]{:S(2)}, u32[]{:S(2)}) collective-permute-start(f32[256,1152]{1,0:T(8,128)S(1)} %collective-permute-done.21), channel_id=1, source_target_pairs={{32,0},{64,32},{96,64},{128,96},{160,128},{192,160},{224,192},{256... | collective-permute-start | bytes 3538952 | tf_op jit(solution)/shard_map/ppermute | solution.py:16
where the time goes:
time: 460 us; the launch traced here: 459 us
  starting transfers between devices  229 us (50%)
  waiting for transfers between devices  210 us (46%)
  matrix products  10.6 us (2%)
  other arithmetic  5.65 us (1%)
    ppermute x23, starting transfers between devices, from_behind(): return lax.ppermute(block, axis, route)  229 us
    ppermute x23, waiting for transfers between devices, from_behind(): return lax.ppermute(block, axis, route)  210 us
  transfers between devices with their start and end apart: 23, of which 9 were waited for; matrix products, arithmetic and copies ran while one was open for 2% of the time, Pallas kernels for 0%

commit v1 on v0

v1 whole, which is shorter than its diff:
```python
import functools

import jax
import jax.numpy as jnp
from jax import lax
from jax.experimental import pallas as pl
from jax.experimental.pallas import tpu as pltpu
from jax.sharding import PartitionSpec as P

MESH = pl.DeviceIdType.MESH
EPSILON = 1e-06

SPAN = 4
SLOTS = 8
RUN = 16
CHUNKS = 4
LATE = 4


def kernel(
    n_grp,
    n_blk,
    image_hbm,
    text_hbm,
    image_ids,
    text_ids,
    sharpness,
    offset,
    adjoint,
    grad_image,
    grad_text,
    raw,
    buf,
    ids,
    own_ids,
    inverse,
    total,
    load_sem,
    send_sem,
    id_send_sem,
    wrap_sem,
    wrap_id_sem,
    recv_sem,
    id_recv_sem,
):
    rows = buf.shape[2]
    piece = rows // CHUNKS
    g = lax.axis_index("grp")
    k = lax.axis_index("blk")
    j = lax.rem(k, RUN)

    loads = [
        pltpu.make_async_copy(text_hbm, raw.at[0], load_sem.at[0]),
        pltpu.make_async_copy(image_hbm, raw.at[1], load_sem.at[1]),
    ]
    for load in loads:
        load.start()

    def device(dg, dk):
        return (lax.rem(g + dg + n_grp, n_grp), lax.rem(k + dk + n_blk, n_blk))

    barrier = pltpu.get_barrier_semaphore()

    def greet(target):
        pl.semaphore_signal(barrier, inc=1, device_id=target, device_id_type=MESH)

    for target in (device(0, 1), device(0, -1), device(1, 0), device(-1, 0)):
        greet(target)

    @pl.when(j == 0)
    def _():
        for back in range(2, 7):
            greet(device(0 if back < 4 else -1, -back))

    @pl.when(j == RUN - 1)
    def _():
        for ahead in range(2, 7):
            greet(device(0 if ahead < 4 else 1, ahead))

    def wrap_distance(stream):
        to_edge = RUN - j if stream == 0 else j + 1
        return to_edge, (to_edge >= 2) & (to_edge <= 6)

    for stream in range(2):
        loads[stream].wait()
        for c in range(CHUNKS):
            part = pl.ds(c * piece, piece)
            wide = raw[stream, part, :].astype(jnp.float32)
            inv = lax.rsqrt(jnp.sum(wide * wide, axis=-1, keepdims=True) + EPSILON)
            inverse[stream, part, :] = jnp.broadcast_to(inv, (piece, 128))
            buf[stream, 0, part, :] = (wide * inv).astype(jnp.bfloat16)
    ids[0, 0] = text_ids[...].astype(jnp.float32)
    ids[1, 0] = image_ids[...].astype(jnp.float32)

    far_sends = sum(wrap_distance(stream)[1].astype(jnp.int32) for stream in range(2))
    pl.semaphore_wait(barrier, 4 + far_sends)

    def route(stream, s):
        step = 1 - 2 * stream
        hop = s == SPAN - 1
        zero = jnp.int32(0)
        target = device(jnp.where(hop, step, zero), jnp.where(hop, zero, step))
        edge = j == jnp.where(stream == 0, RUN - 1, 0)
        goes = (s < SLOTS - 1) & (jnp.logical_not(edge) | (s == 0) | hop)
        return target, goes

    def block_copy(stream, s, c, target):
        part = pl.ds(c * piece, piece)
        return pltpu.make_async_remote_copy(
            src_ref=buf.at[stream, s, part],
            dst_ref=buf.at[stream, s + 1, part],
            send_sem=send_sem.at[stream, s],
            recv_sem=recv_sem.at[stream, s + 1, c],
            device_id=target,
            device_id_type=MESH,
        )

    def id_copy(stream, s, target):
        return pltpu.make_async_remote_copy(
            src_ref=ids.at[stream, s],
            dst_ref=ids.at[stream, s + 1],
            send_sem=id_send_sem.at[stream, s],
            recv_sem=id_recv_sem.at[stream, s + 1],
            device_id=target,
            device_id_type=MESH,
        )

    def forward(stream, s, c):
        target, goes = route(stream, s)

        @pl.when(goes)
        def _():
            if c is None:
                id_copy(stream, s, target).start()
            else:
                block_copy(stream, s, c, target).start()

    def receive(stream, s, c):
        target, _ = route(stream, s)
        if c is None:
            id_copy(stream, s - 1, target).wait_recv()
        else:
            block_copy(stream, s - 1, c, target).wait_recv()

    def wrap_copies(stream):
        to_edge, far = wrap_distance(stream)
        same = to_edge < SPAN
        slot = jnp.where(same, to_edge, to_edge + 1)
        step = 1 - 2 * stream
        target = device(jnp.where(same, 0, step), step * to_edge)
        copies = [
            pltpu.make_async_remote_copy(
                src_ref=ids.at[stream, 0],
                dst_ref=ids.at[stream, slot],
                send_sem=wrap_id_sem.at[stream],
                recv_sem=id_recv_sem.at[stream, slot],
                device_id=target,
                device_id_type=MESH,
            )
        ]
        for c in range(CHUNKS):
            part = pl.ds(c * piece, piece)
            copies.append(
                pltpu.make_async_remote_copy(
                    src_ref=buf.at[stream, 0, part],
                    dst_ref=buf.at[stream, slot, part],
                    send_sem=wrap_sem.at[stream],
                    recv_sem=recv_sem.at[stream, slot, c],
                    device_id=target,
                    device_id_type=MESH,
                )
            )
        whole = pltpu.make_async_remote_copy(
            src_ref=buf.at[stream, 0],
            dst_ref=buf.at[stream, slot],
            send_sem=wrap_sem.at[stream],
            recv_sem=recv_sem.at[stream, slot, 0],
            device_id=target,
            device_id_type=MESH,
        )
        return far, copies, whole

    for c in (None, *range(CHUNKS)):
        for stream in range(2):
            forward(stream, 0, c)
    for stream in range(2):
        far, copies, _ = wrap_copies(stream)

        @pl.when(far)
        def _():
            for copy in copies:
                copy.start()

    scale = jnp.exp(jnp.full((1, 128), sharpness[0], jnp.float32))[:, :1]
    shift = offset[0]
    weight = -(adjoint[0] * scale / rows)

    row = lax.broadcasted_iota(jnp.int32, (128, 128), 0)
    lane = lax.broadcasted_iota(jnp.int32, (128, 128), 1)
    for stream in range(2):
        for half in range(rows // 128):
            line = jnp.broadcast_to(ids[stream, 0, half : half + 1, :], (128, 128))
            column = jnp.sum(jnp.where(row == lane, line, 0.0), axis=-1, keepdims=True)
            own_ids[stream, pl.ds(half * 128, 128), :] = jnp.broadcast_to(column, (128, 128))

    def compute(stream, s, first=False):
        mine = 1 - stream
        visitor = buf[stream, s]
        grid = lax.dot_general(
            buf[mine, 0], visitor, (((1,), (1,)), ((), ())), preferred_element_type=jnp.float32
        )
        logit = scale * grid + shift
        column = own_ids[mine, :, :]
        parts = []
        for half in range(rows // 128):
            line = ids[stream, s, half : half + 1, :]
            match = column == jnp.broadcast_to(line, (rows, 128))
            here = logit[:, half * 128 : (half + 1) * 128]
            signed = jnp.where(match, here, -here)
            parts.append(jnp.where(match, weight, -weight) * (1.0 / (1.0 + jnp.exp(signed))))
        coef = jnp.concatenate(parts, axis=1).astype(jnp.bfloat16)
        term = jnp.dot(coef, visitor, preferred_element_type=jnp.float32)
        if first:
            total[mine] = term
        else:
            total[mine] += term

    for stream in range(2):
        compute(stream, 0, first=True)

    low = j < RUN // 2
    lead = jnp.where(low, 1, 0)
    lag = 1 - lead
    near = jnp.where(low, j, RUN - 1 - j)

    def late(s):
        return near < jnp.where(s < SPAN, s, s - 1)

    def step(t, carry):
        in_time = t < SLOTS
        lag_now = in_time & jnp.logical_not(late(t))
        old = t - LATE
        lag_old = (old >= 1) & late(old)

        for c in (None, *range(CHUNKS)):

            @pl.when(in_time)
            def _():
                receive(lead, t, c)
                forward(lead, t, c)

            @pl.when(lag_now)
            def _():
                receive(lag, t, c)
                forward(lag, t, c)

        @pl.when(in_time)
        def _():
            compute(lead, t)

        @pl.when(lag_now)
        def _():
            compute(lag, t)

        @pl.when(lag_old)
        def _():
            for c in (None, *range(CHUNKS)):
                receive(lag, old, c)
                forward(lag, old, c)
            compute(lag, old)

        return carry

    lax.fori_loop(1, SLOTS + LATE, step, 0)

    for stream, out in ((1, grad_image), (0, grad_text)):
        for c in range(CHUNKS):
            part = pl.ds(c * piece, piece)
            inv = inverse[stream, part, :][:, :1]
            unit = raw[stream, part, :].astype(jnp.float32) * inv
            grad = total[stream, part, :]
            along = jnp.sum(unit * grad, axis=-1, keepdims=True)
            out[part, :] = inv * (grad - unit * along)

    for stream in range(2):
        for s in range(SLOTS - 1):
            target, goes = route(stream, s)

            @pl.when(goes)
            def _():
                id_copy(stream, s, target).wait_send()
                pltpu.make_async_remote_copy(
                    src_ref=buf.at[stream, s],
                    dst_ref=buf.at[stream, s + 1],
                    send_sem=send_sem.at[stream, s],
                    recv_sem=recv_sem.at[stream, s + 1, 0],
                    device_id=target,
                    device_id_type=MESH,
                ).wait_send()

        far, copies, whole = wrap_copies(stream)

        @pl.when(far)
        def _():
            copies[0].wait_send()
            whole.wait_send()


def body(n_grp, n_blk, image_emb, text_emb, image_pair_index, text_ids, sharpness, offset, adjoint):
    rows, width = image_emb.shape
    vmem = pl.BlockSpec(memory_space=pltpu.VMEM)
    smem = pl.BlockSpec(memory_space=pltpu.SMEM)
    hbm = pl.BlockSpec(memory_space=pl.ANY)
    flops = 4 * SLOTS * 2 * rows * rows * width
    return pl.pallas_call(
        functools.partial(kernel, n_grp, n_blk),
        out_shape=(
            jax.ShapeDtypeStruct((rows, width), jnp.float32),
            jax.ShapeDtypeStruct((rows, width), jnp.float32),
        ),
        in_specs=[hbm, hbm, vmem, vmem, smem, smem, smem],
        out_specs=(vmem, vmem),
        scratch_shapes=[
            pltpu.VMEM((2, rows, width), jnp.bfloat16),
            pltpu.VMEM((2, SLOTS, rows, width), jnp.bfloat16),
            pltpu.VMEM((2, SLOTS, rows // 128, 128), jnp.float32),
            pltpu.VMEM((2, rows, 128), jnp.float32),
            pltpu.VMEM((2, rows, 128), jnp.float32),
            pltpu.VMEM((2, rows, width), jnp.float32),
            pltpu.SemaphoreType.DMA((2,)),
            pltpu.SemaphoreType.DMA((2, SLOTS)),
            pltpu.SemaphoreType.DMA((2, SLOTS)),
            pltpu.SemaphoreType.DMA((2,)),
            pltpu.SemaphoreType.DMA((2,)),
            pltpu.SemaphoreType.DMA((2, SLOTS, CHUNKS)),
            pltpu.SemaphoreType.DMA((2, SLOTS)),
        ],
        compiler_params=pltpu.CompilerParams(
            collective_id=0, has_side_effects=True, vmem_limit_bytes=40 * 1024 * 1024
        ),
        cost_estimate=pl.CostEstimate(
            flops=flops, bytes_accessed=12 * rows * width, transcendentals=2 * SLOTS * rows * rows
        ),
    )(
        image_emb,
        text_emb,
        image_pair_index.reshape(rows // 128, 128),
        text_ids.reshape(rows // 128, 128),
        sharpness,
        offset,
        adjoint,
    )


def solution(mesh):
    both = ("grp", "blk")
    return jax.shard_map(
        functools.partial(body, mesh.shape["grp"], mesh.shape["blk"]),
        mesh=mesh,
        in_specs=(P(both, None), P(both, None), P(both), P(both), P(), P(), P()),
        out_specs=(P(both, None), P(both, None)),
        check_vma=False,
    )
```

time: 460 us -> 129 us (0.28)
  the two profiles are of different devices: /device:TPU:462 before, /device:TPU:64 now
where the time goes in v1:
time: 129 us
  Pallas kernels  121 us (94%)
  local copies, waits for them, and re-layouts  5.51 us (4%)
  between operations  2.59 us (2%)
    pallas_call x1, Pallas kernels, body(): pl.pallas_call(functools.partial(kernel, n_grp, n_blk), out_shape=(jax.Sh...  121 us
    unnamed x10, local copies, waits for them, and re-layouts  5.51 us

profile of v1, /device:TPU:64, one launch (start us, length us, event | category | flops | bytes accessed | tf_op | source)
XLA Modules:
  0.0 129.2 jit_solution(12471212609414759564)
XLA Ops:
  2.6 0.0 copy-start
  2.6 1.1 copy-done
  3.6 0.0 copy-start.1
  3.6 1.1 copy-done.1
  4.7 0.0 copy-start.2
  4.7 0.7 copy-done.2
  5.4 0.0 copy-start.3
  5.4 0.7 copy-done.3
  6.1 121.1 %shard_map.86 = (f32[256,1152]{1,0:T(8,128)S(1)}, f32[256,1152]{1,0:T(8,128)S(1)}) custom-call(bf16[256,1152]{1,0:T(8,128)(2,1)S(1)} %copy-done, bf16[256,1152]{1,0:T(8,128)(2,1)S(1)} %copy-done.1, s32[2,128]{1,0:T(2,128)S(1)} %bitcast.2, s32[2,128]{1,0:T(2,128)S(1)} %bitcast.3, f32[1]{0:T(128)S(6)} %copy.11.sharpness, f32[1]{0:T(128)S(6)} %copy.12.offset, ...), custom_call_target="tpu_custom_call" | custom-call | flops 4831838208 | bytes 3538944 | tf_op jit(solution)/shard_map/pallas_call | solution.py:315
  127.2 1.0 copy.14
  128.2 1.0 copy.15
Async XLA Ops:
  2.6 1.1 copy-start
  3.6 1.1 copy-start.1
  4.7 0.7 copy-start.2
  5.4 0.7 copy-start.3

commit v2 on v1

v2 whole, which is shorter than its diff:
```python
import functools

import jax
import jax.numpy as jnp
from jax import lax
from jax.experimental import pallas as pl
from jax.experimental.pallas import tpu as pltpu
from jax.sharding import PartitionSpec as P

MESH = pl.DeviceIdType.MESH
EPSILON = 1e-06

SPAN = 4
SLOTS = 8
RUN = 16
WAVES = 4
DETOUR = 5


ORDER = (
    (
        10381668, 2261260, 16777260, 150994944, 3491608, 62167621, 184549376, 2793870, 83886126, 218103808,
        4020058, 129938119, 251658240, 33554448, 8219678, 12942865, 72074873, 100663296, 183979163, 201326645,
        134475411, 15728051, 234881079, 268435456,
    ),
    (
        1859908, 19958308, 6408805, 50332489, 87599782, 6679271, 121816011, 150994944, 33554452, 184550509,
        218106778, 251661300, 16080658, 5201819, 167972856, 7841209, 100663345, 67108864, 8335094, 201329911,
        234881024, 268435479, 134217728, 0,
    ),
    (
        10381668, 1475076, 150997769, 196514438, 11059911, 16777262, 218103808, 251775979, 50331661, 83947128,
        13694842, 117440571, 7963952, 183702901, 33555481, 209675709, 234979250, 281915383, 67108881,
        100663314, 134219475, 0, 0, 0,
    ),
    (
        1859908, 19958308, 53779045, 95052682, 117441483, 164809447, 184552813, 218107310, 251886639, 6549372,
        182713436, 201330265, 37832562, 234882746, 268508915, 5105362, 67108885, 100663318, 134219735, 0, 0,
        0, 0, 0,
    ),
    (
        10381668, 162562344, 196383081, 12100010, 218103856, 254573547, 16777228, 50334797, 83887032,
        117440527, 13610169, 172183355, 16588733, 201544860, 241394909, 268519351, 33554432, 73754581,
        100664983, 134217755, 0, 0, 0, 0,
    ),
    (
        1593636, 10902023, 16933640, 60609130, 95478443, 150994944, 129450955, 184549376, 218106805,
        251661743, 14909308, 168008766, 15725882, 201329749, 239543318, 268645527, 33653980, 67229337,
        100665243, 134217759, 0, 0, 0, 0,
    ),
    (
        10381668, 162693636, 196514373, 11207302, 218103854, 3347143, 16780267, 266398861, 50331663, 83889779,
        117440512, 15418448, 167772220, 201579858, 15723923, 234884568, 268435519, 7161497, 40990101,
        67108893, 100663326, 134217759, 0, 0,
    ),
    (
        1859908, 3181092, 16779877, 61498185, 10281616, 83886123, 11596497, 117440564, 150994962, 184552813,
        218103854, 251659503, 14386480, 13196409, 14658774, 7720663, 33654750, 167773820, 67110589, 201326654,
        100667355, 234881024, 134217728, 268435456,
    ),
    (
        10115336, 1347879, 151038760, 187619910, 3318256, 16777262, 218103857, 55769805, 251658240, 83952974,
        117440527, 4672662, 13471063, 5057945, 15842778, 182714301, 33558108, 201330333, 67112670, 234881024,
        100663327, 268435456, 134217728, 0,
    ),
    (
        1859908, 19040524, 10900493, 50331657, 4630926, 83886090, 4897231, 117440523, 150994988, 184549421,
        218203374, 251658287, 7013657, 13219185, 33554460, 67200883, 100665239, 134219768, 15683257,
        183729589, 201326653, 234881086, 268435519, 0,
    ),
    (
        10381668, 1475076, 150997769, 196387241, 230207978, 29180715, 251658240, 50333005, 83887502,
        117441999, 7964508, 33554448, 13739993, 67181915, 113585206, 134298807, 168021555, 201580217,
        234885051, 268435519, 0, 0, 0, 0,
    ),
    (
        1859908, 19958308, 53779045, 3713702, 83886096, 3980007, 117440556, 150994989, 184738904, 218103855,
        251658265, 5093010, 33555740, 8252445, 72822577, 100757363, 134221719, 167775796, 216494069,
        234884791, 268435515, 0, 0, 0,
    ),
    (
        10381668, 162693636, 196514373, 230335110, 254573547, 16778508, 50333005, 83887502, 117440527,
        7698192, 15960030, 33555985, 67110521, 7013565, 100663354, 147277019, 167772160, 16465650, 201326645,
        234881078, 268439543, 0, 0, 0,
    ),
    (
        1859908, 3181092, 16779877, 53913993, 3713767, 83886124, 150994944, 117505803, 184549421, 218106776,
        264230553, 13743124, 4677560, 33555804, 81524601, 167970194, 100663326, 5076983, 134217786, 201326641,
        234881074, 268439283, 0, 0,
    ),
    (
        10381668, 162693636, 10977861, 184553261, 230335110, 11506375, 251662255, 16777228, 167775536,
        50331661, 83947185, 117441492, 15686812, 6379421, 49612787, 4679065, 201326618, 234881024, 6289106,
        67108883, 100663351, 134217728, 268435456, 0,
    ),
    (
        1859908, 151177764, 16777992, 14851365, 184552316, 50332489, 218294950, 83886986, 15383911, 251661309,
        117441483, 167772208, 16584126, 4683313, 201328249, 234884252, 33558228, 72689309, 268438750,
        105756063, 134217751, 0, 0, 0,
    ),
)


def kernel(
    n_grp,
    n_blk,
    image_hbm,
    text_hbm,
    image_ids,
    text_ids,
    sharpness,
    offset,
    adjoint,
    grad_image,
    grad_text,
    raw,
    hat,
    buf,
    ids,
    own_ids,
    inverse,
    total,
    load_sem,
    send_sem,
    id_send_sem,
    wrap_sem,
    wrap_id_sem,
    detour_sem,
    recv_sem,
    id_recv_sem,
):
    rows = hat.shape[1]
    piece = rows // WAVES
    g = lax.axis_index("grp")
    k = lax.axis_index("blk")
    j = lax.rem(k, RUN)

    loads = [
        pltpu.make_async_copy(text_hbm, raw.at[0], load_sem.at[0]),
        pltpu.make_async_copy(image_hbm, raw.at[1], load_sem.at[1]),
    ]
    for load in loads:
        load.start()

    def device(dg, dk):
        return (lax.rem(g + dg + n_grp, n_grp), lax.rem(k + dk + n_blk, n_blk))

    next_grp = [device(step, 0)[0] for step in (1, -1)]
    next_blk = [device(0, step)[1] for step in (1, -1)]

    barrier = pltpu.get_barrier_semaphore()

    def greet(target):
        pl.semaphore_signal(barrier, inc=1, device_id=target, device_id_type=MESH)

    for target in (device(0, 1), device(0, -1), device(1, 0), device(-1, 0)):
        greet(target)

    even = lax.rem(j, 2) == 0

    @pl.when(even & (j >= 2))
    def _():
        greet(device(0, -2))

    @pl.when(jnp.logical_not(even) & (j <= RUN - 3))
    def _():
        greet(device(0, 2))

    @pl.when(j == 0)
    def _():
        for back in range(2, 7):
            greet(device(0 if back < 4 else -1, -back))
        greet(device(-1, -2))

    @pl.when(j == RUN - 1)
    def _():
        for ahead in range(2, 7):
            greet(device(0 if ahead < 4 else 1, ahead))
        greet(device(1, 2))

    def wrap_distance(stream):
        to_edge = RUN - j if stream == 0 else j + 1
        return to_edge, (to_edge >= 2) & (to_edge <= 6)

    words = []
    for i in range(len(ORDER[0])):
        word = jnp.int32(ORDER[0][i])
        for place in range(1, RUN):
            if ORDER[place][i] != ORDER[place - 1][i]:
                word = jnp.where(j >= place, ORDER[place][i], word)
        words.append(word)

    for stream, own in ((0, text_ids), (1, image_ids)):
        loads[stream].wait()
        for c in range(WAVES):
            part = pl.ds(c * piece, piece)
            wide = raw[stream, part, :].astype(jnp.float32)
            inv = lax.rsqrt(jnp.sum(wide * wide, axis=-1, keepdims=True) + EPSILON)
            inverse[stream, part, :] = jnp.broadcast_to(inv, (piece, 128))
            unit = (wide * inv).astype(jnp.bfloat16)
            hat[stream, part, :] = unit
            buf[stream, c, pl.ds(0, piece), :] = unit
            at = c * piece
            line = own[at // 128 : at // 128 + 1, :].astype(jnp.float32)
            line = line[:, at % 128 : at % 128 + piece]
            ids[stream, 0, c] = jnp.concatenate([line] * (128 // piece), axis=1)

    far_sends = sum(wrap_distance(stream)[1].astype(jnp.int32) for stream in range(2))
    for stream in range(2):
        far_sends += (wrap_distance(stream)[0] == 2).astype(jnp.int32)
    skips = jnp.where(even, j != RUN - 2, j != 1).astype(jnp.int32)
    pl.semaphore_wait(barrier, 4 + skips + far_sends)

    def pick(stream, pair):
        return pair[stream] if isinstance(stream, int) else jnp.where(stream == 0, pair[0], pair[1])

    def route(stream, s, reach):
        place = pick(stream, (j, RUN - 1 - j))
        entry = lax.rem(place, 2) == 0
        fresh = (s == 0) | (s == SPAN)
        if reach == 2:
            goes = entry & (place != RUN - 2) & (fresh | (s == 1) | (s == SPAN + 1))
            return (g, pick(stream, [device(0, step)[1] for step in (2, -2)])), goes
        hop = s == SPAN - 1
        target = (
            jnp.where(hop, pick(stream, next_grp), g),
            jnp.where(hop, k, pick(stream, next_blk)),
        )
        goes = jnp.where(place == RUN - 1, s == 0, entry | fresh)
        return target, (s < SLOTS - 1) & (hop | goes)

    def chunk(stream, s, c):
        at = s * piece
        if not isinstance(at, int):
            at = pl.multiple_of(at, piece)
        return buf.at[stream, c, pl.ds(at, piece)]

    def remote(src, dst, send, recv, target):
        return pltpu.make_async_remote_copy(
            src_ref=src,
            dst_ref=dst,
            send_sem=send,
            recv_sem=recv,
            device_id=target,
            device_id_type=MESH,
        )

    def block_copy(stream, s, c, reach, target):
        return remote(
            chunk(stream, s, c),
            chunk(stream, s + reach, c),
            send_sem.at[reach - 1, stream, s],
            recv_sem.at[stream, s + reach, c],
            target,
        )

    def id_copy(stream, s, reach, target):
        return remote(
            ids.at[stream, s],
            ids.at[stream, s + reach],
            id_send_sem.at[reach - 1, stream, s],
            id_recv_sem.at[stream, s + reach],
            target,
        )

    def forward(stream, s, c):
        for reach in (2, 1):
            target, goes = route(stream, s, reach)

            @pl.when(goes)
            def _():
                @pl.when(c == 0)
                def _():
                    id_copy(stream, s, reach, target).start()

                block_copy(stream, s, c, reach, target).start()

    def receive(stream, s, c):
        target = (g, pick(stream, next_blk))

        @pl.when(c == 0)
        def _():
            id_copy(stream, s - 1, 1, target).wait_recv()

        block_copy(stream, s - 1, c, 1, target).wait_recv()

    def wrap_route(stream):
        to_edge, far = wrap_distance(stream)
        same = to_edge < SPAN
        slot = jnp.where(same, to_edge, to_edge + 1)
        step = 1 - 2 * stream
        return far, slot, device(jnp.where(same, 0, step), step * to_edge)

    def wrap_id_copy(stream):
        _, slot, target = wrap_route(stream)
        return remote(
            ids.at[stream, 0],
            ids.at[stream, slot],
            wrap_id_sem.at[stream],
            id_recv_sem.at[stream, slot],
            target,
        )

    def wrap(stream, c):
        far, slot, target = wrap_route(stream)

        if c == 0:

            @pl.when(far)
            def _():
                wrap_id_copy(stream).start()

        if c % 2:
            far = far & (wrap_distance(stream)[0] != DETOUR)

        @pl.when(far)
        def _():
            remote(
                chunk(stream, 0, c),
                chunk(stream, slot, c),
                wrap_sem.at[stream],
                recv_sem.at[stream, slot, c],
                target,
            ).start()

    def detour_copy(stream, c):
        step = pick(stream, (1, -1))
        return remote(
            chunk(stream, SPAN - 1, c),
            chunk(stream, DETOUR + 1, c),
            detour_sem.at[stream],
            recv_sem.at[stream, DETOUR + 1, c],
            device(step, 2 * step),
        )

    def detour(stream, s, c):
        @pl.when((s == SPAN - 1) & (j == pick(stream, (RUN - 2, 1))) & (lax.rem(c, 2) == 1))
        def _():
            detour_copy(stream, c).start()

    for c in range(WAVES):
        for stream in range(2):
            forward(stream, 0, c)
        for stream in range(2):
            wrap(stream, c)

    row = lax.broadcasted_iota(jnp.int32, (128, 128), 0)
    lane = lax.broadcasted_iota(jnp.int32, (128, 128), 1)
    for stream, own in ((0, text_ids), (1, image_ids)):
        for half in range(rows // 128):
            line = jnp.broadcast_to(own[half : half + 1, :].astype(jnp.float32), (128, 128))
            column = jnp.sum(jnp.where(row == lane, line, 0.0), axis=-1, keepdims=True)
            own_ids[stream, pl.ds(half * 128, 128), :] = jnp.broadcast_to(column, (128, 128))
        total[stream] = jnp.zeros(total.shape[1:], jnp.float32)

    scale = jnp.exp(jnp.full((1, 128), sharpness[0], jnp.float32))[:, :1]
    shift = offset[0]
    weight = -(adjoint[0] * scale / rows)
    group = SPAN * piece
    turn = lax.broadcasted_iota(jnp.int32, (1, 128), 1) // piece

    def compute(stream, c, half):
        mine = 1 - stream
        visitors = buf[stream, c, pl.ds(pl.multiple_of(half * group, group), group), :]
        grid = lax.dot_general(
            hat[mine], visitors, (((1,), (1,)), ((), ())), preferred_element_type=jnp.float32
        )
        logit = scale * grid + shift
        column = own_ids[mine, :, :]
        parts = []
        for at in range(0, group, 128):
            s = half * SPAN + at // piece
            line = ids[stream, s, c]
            for other in range(1, 128 // piece):
                line = jnp.where(turn == other, ids[stream, s + other, c], line)
            match = column == jnp.broadcast_to(line, (rows, 128))
            here = logit[:, at : at + 128]
            signed = jnp.where(match, here, -here)
            parts.append(jnp.where(match, weight, -weight) * (1.0 / (1.0 + jnp.exp(signed))))
        coef = jnp.concatenate(parts, axis=1).astype(jnp.bfloat16)
        total[mine] += jnp.dot(coef, visitors, preferred_element_type=jnp.float32)

    def step(i, carry):
        word = words[0]
        for other in range(1, len(words)):
            word = jnp.where(i == other, words[other], word)

        for _ in range(4):
            entry = lax.rem(word, 64)
            word = lax.div(word, 64)
            stream = lax.div(entry, 32)
            s = lax.rem(lax.div(entry, 4), 8)
            c = lax.rem(entry, 4)

            @pl.when(entry > 0)
            def _():
                receive(stream, s, c)
                forward(stream, s, c)
                detour(stream, s, c)

        @pl.when(word > 0)
        def _():
            product = word - 1
            compute(lax.div(product, 8), lax.div(lax.rem(product, 8), 2), lax.rem(product, 2))

        return carry

    lax.fori_loop(0, len(words), step, 0)

    for stream, out in ((1, grad_image), (0, grad_text)):
        for c in range(WAVES):
            part = pl.ds(c * piece, piece)
            inv = inverse[stream, part, :][:, :1]
            unit = raw[stream, part, :].astype(jnp.float32) * inv
            grad = total[stream, part, :]
            along = jnp.sum(unit * grad, axis=-1, keepdims=True)
            out[part, :] = inv * (grad - unit * along)

    for stream in range(2):
        for s in range(SLOTS - 1):
            for reach in (2, 1):
                target, goes = route(stream, s, reach)

                @pl.when(goes)
                def _():
                    id_copy(stream, s, reach, target).wait_send()
                    remote(
                        hat.at[stream],
                        hat.at[stream],
                        send_sem.at[reach - 1, stream, s],
                        recv_sem.at[stream, s + 1, 0],
                        target,
                    ).wait_send()

        far, slot, target = wrap_route(stream)
        detoured = wrap_distance(stream)[0] == DETOUR

        @pl.when(far)
        def _():
            wrap_id_copy(stream).wait_send()

        for cond, amount in ((jnp.logical_not(detoured), rows), (detoured, rows // 2)):

            @pl.when(far & cond)
            def _():
                part = hat.at[stream, pl.ds(0, amount)]
                remote(
                    part, part, wrap_sem.at[stream], recv_sem.at[stream, slot, 0], target
                ).wait_send()

        @pl.when(j == (RUN - 2, 1)[stream])
        def _():
            part = hat.at[stream, pl.ds(0, rows // 2)]
            remote(
                part, part, detour_sem.at[stream], recv_sem.at[stream, slot, 0], target
            ).wait_send()


def body(n_grp, n_blk, image_emb, text_emb, image_pair_index, text_ids, sharpness, offset, adjoint):
    rows, width = image_emb.shape
    vmem = pl.BlockSpec(memory_space=pltpu.VMEM)
    smem = pl.BlockSpec(memory_space=pltpu.SMEM)
    hbm = pl.BlockSpec(memory_space=pltpu.HBM)
    flops = 4 * SLOTS * 2 * rows * rows * width
    return pl.pallas_call(
        functools.partial(kernel, n_grp, n_blk),
        out_shape=(
            jax.ShapeDtypeStruct((rows, width), jnp.float32),
            jax.ShapeDtypeStruct((rows, width), jnp.float32),
        ),
        in_specs=[hbm, hbm, vmem, vmem, smem, smem, smem],
        out_specs=(vmem, vmem),
        scratch_shapes=[
            pltpu.VMEM((2, rows, width), jnp.bfloat16),
            pltpu.VMEM((2, rows, width), jnp.bfloat16),
            pltpu.VMEM((2, WAVES, SLOTS * rows // WAVES, width), jnp.bfloat16),
            pltpu.VMEM((2, SLOTS, WAVES, 1, 128), jnp.float32),
            pltpu.VMEM((2, rows, 128), jnp.float32),
            pltpu.VMEM((2, rows, 128), jnp.float32),
            pltpu.VMEM((2, rows, width), jnp.float32),
            pltpu.SemaphoreType.DMA((2,)),
            pltpu.SemaphoreType.DMA((2, 2, SLOTS)),
            pltpu.SemaphoreType.DMA((2, 2, SLOTS)),
            pltpu.SemaphoreType.DMA((2,)),
            pltpu.SemaphoreType.DMA((2,)),
            pltpu.SemaphoreType.DMA((2,)),
            pltpu.SemaphoreType.DMA((2, SLOTS, WAVES)),
            pltpu.SemaphoreType.DMA((2, SLOTS)),
        ],
        compiler_params=pltpu.CompilerParams(
            collective_id=0, has_side_effects=True, vmem_limit_bytes=60 * 1024 * 1024
        ),
        cost_estimate=pl.CostEstimate(
            flops=flops, bytes_accessed=12 * rows * width, transcendentals=2 * SLOTS * rows * rows
        ),
    )(
        image_emb,
        text_emb,
        image_pair_index.reshape(rows // 128, 128),
        text_ids.reshape(rows // 128, 128),
        sharpness,
        offset,
        adjoint,
    )


def solution(mesh):
    both = ("grp", "blk")
    return jax.shard_map(
        functools.partial(body, mesh.shape["grp"], mesh.shape["blk"]),
        mesh=mesh,
        in_specs=(P(both, None), P(both, None), P(both), P(both), P(), P(), P()),
        out_specs=(P(both, None), P(both, None)),
        check_vma=False,
    )
```

time: 129 us -> 112 us (0.87)
  the two profiles are of different devices: /device:TPU:64 before, /device:TPU:155 now
where the time goes in v2:
time: 112 us
  Pallas kernels  106 us (95%)
  local copies, waits for them, and re-layouts  3.47 us (3%)
  between operations  2.58 us (2%)
    pallas_call x1, Pallas kernels, body(): pl.pallas_call(functools.partial(kernel, n_grp, n_blk), out_shape=(jax.Sh...  106 us
    unnamed x4, local copies, waits for them, and re-layouts  3.47 us

profile of v2, /device:TPU:155, one launch (start us, length us, event | category | flops | bytes accessed | tf_op | source)
XLA Modules:
  0.0 111.9 jit_solution(6499952091760917606)
XLA Ops:
  2.6 105.8 %shard_map.86 = (f32[256,1152]{1,0:T(8,128)}, f32[256,1152]{1,0:T(8,128)}) custom-call(bf16[256,1152]{1,0:T(8,128)(2,1)} %image_hbm.1, bf16[256,1152]{1,0:T(8,128)(2,1)} %text_hbm.1, s32[2,128]{1,0:T(2,128)} %bitcast.2, s32[2,128]{1,0:T(2,128)} %bitcast.3, f32[1]{0:T(128)S(6)} %copy.11.sharpness, f32[1]{0:T(128)S(6)} %copy.12.offset, f32[1]{0:T(128)S(6)} %copy.13.adjoint), custom_call_target="tpu_custom_call" | custom-call | flops 4831838208 | bytes 3538944 | tf_op jit(solution)/shard_map/pallas_call | solution.py:465
  108.4 0.0 copy-start
  108.4 2.5 %copy.14 = f32[256,1152]{1,0:T(8,128)} copy(f32[256,1152]{1,0:T(8,128)} %get-tuple-element.4) | data formatting | bytes 2359296
  110.9 0.0 copy-done
  110.9 1.0 copy.15
Async XLA Ops:
  108.4 2.5 %copy-start = (f32[256,1152]{1,0:T(8,128)S(1)}, f32[256,1152]{1,0:T(8,128)}, u32[]{:S(2)}) copy-start(f32[256,1152]{1,0:T(8,128)} %get-tuple-element.5) | copy-start | bytes 3538948

commit v3 on v2

--- a/solution.py
+++ b/solution.py
@@ -12,91 +12,654 @@
 
 SPAN = 4
 SLOTS = 8
+LINE = 4
+PATIENT = (7, 2)
 RUN = 16
 WAVES = 4
-DETOUR = 5
+DETOURS = (
+)
 
 
 ORDER = (
     (
-        10381668, 2261260, 16777260, 150994944, 3491608, 62167621, 184549376, 2793870, 83886126, 218103808,
-        4020058, 129938119, 251658240, 33554448, 8219678, 12942865, 72074873, 100663296, 183979163, 201326645,
-        134475411, 15728051, 234881079, 268435456,
-    ),
-    (
-        1859908, 19958308, 6408805, 50332489, 87599782, 6679271, 121816011, 150994944, 33554452, 184550509,
-        218106778, 251661300, 16080658, 5201819, 167972856, 7841209, 100663345, 67108864, 8335094, 201329911,
-        234881024, 268435479, 134217728, 0,
-    ),
-    (
-        10381668, 1475076, 150997769, 196514438, 11059911, 16777262, 218103808, 251775979, 50331661, 83947128,
-        13694842, 117440571, 7963952, 183702901, 33555481, 209675709, 234979250, 281915383, 67108881,
-        100663314, 134219475, 0, 0, 0,
-    ),
-    (
-        1859908, 19958308, 53779045, 95052682, 117441483, 164809447, 184552813, 218107310, 251886639, 6549372,
-        182713436, 201330265, 37832562, 234882746, 268508915, 5105362, 67108885, 100663318, 134219735, 0, 0,
+        10639617, 150997798, 184736233, 230598190, 251658283, 2115340, 16777241, 1543181, 3791945, 50331700,
+        4259418, 83927474, 167776058, 33555729, 15592819, 124605127, 67112381, 201328598, 234881086,
+        268697047, 100663314, 134217747, 0, 0,
+    ),
+    (
+        10115329, 10910504, 150994989, 184549376, 218277422, 251837404, 7684889, 7017840, 6153656, 8240313,
+        13583245, 15684602, 16777732, 167772540, 50331657, 204017478, 33554432, 83886087, 117440523, 67363958,
+        234881024, 100663314, 134444287, 268435456,
+    ),
+    (
+        1859908, 9865473, 11430569, 151177692, 184549421, 221368878, 16777216, 251661300, 50385520, 14282549,
+        167775764, 83946570, 16090487, 201326649, 6619890, 33685391, 117440570, 234881024, 7339226, 67108881,
+        268435515, 100664722, 134218967, 0,
+    ),
+    (
+        1859908, 9865473, 11430569, 151177692, 196560413, 14002073, 218103854, 12710939, 251661302, 2346481,
+        167776120, 16777228, 204969033, 50331648, 33613066, 83886130, 132710283, 234881024, 67110226,
+        114126591, 268435456, 134219219, 0, 0,
+    ),
+    (
+        2380292, 6, 162695425, 10005349, 184719815, 218276590, 251837487, 20131377, 14106228, 50332538,
+        183729910, 83944472, 201326653, 235136793, 268436479, 117441821, 33554432, 72742801, 106509970,
+        134219227, 0, 0, 0, 0,
+    ),
+    (
+        2380292, 162695425, 11952549, 186552999, 11207406, 218103857, 251865839, 7720184, 14020212, 8351376,
+        183729876, 201330513, 16854924, 234881024, 50331661, 268514687, 83886094, 33554456, 117440527,
+        67110486, 100663322, 134219227, 0, 0,
+    ),
+    (
+        1859908, 9476616, 41, 26518273, 50334349, 84042635, 117503019, 151176295, 184737042, 232197011,
+        251661423, 14626614, 182709501, 201326649, 235119900, 268558079, 33554456, 67110485, 107575190,
+        134219487, 0, 0, 0, 0,
+    ),
+    (
+        1859908, 2568, 16925441, 50387529, 11076261, 83886094, 128776587, 151177681, 196427026, 218103854,
+        264183152, 5491894, 6504311, 167772216, 201330617, 234884757, 268678591, 33670617, 67110746,
+        100663326, 134219487, 0, 0, 0,
+    ),
+    (
+        1206628, 11555367, 150997513, 6, 1878849, 184552489, 27839371, 218103808, 63353711, 251658260,
+        84094478, 117441493, 4292182, 4697395, 183745973, 201577655, 234885011, 268435519, 33556248, 67110745,
+        100787930, 134217759, 0, 0,
+    ),
+    (
+        10381668, 516, 11571521, 151038470, 12751341, 184549387, 218106794, 16978708, 50525035, 251658240,
+        83886997, 5831864, 117440528, 13844055, 14228858, 183602898, 201579987, 33558428, 234881024,
+        268435519, 74823321, 100663326, 134217759, 0,
+    ),
+    (
+        1859908, 9476616, 41, 16777985, 50483853, 83887018, 11336075, 117440528, 151176295, 196445364,
+        230268243, 264437146, 13092564, 14888789, 167772215, 201584243, 235122646, 268439255, 33554460,
+        67108893, 100663326, 134217759, 0, 0,
+    ),
+    (
+        1859908, 8, 16941825, 50387209, 4346537, 83888782, 121443046, 4819687, 150998316, 184653037,
+        218107246, 12430356, 251860726, 5758140, 167775799, 16487859, 201326620, 33558167, 234881024,
+        268439295, 67108893, 100663326, 134217759, 0,
+    ),
+    (
+        1206628, 11555367, 162955657, 10779658, 184552331, 16777228, 62825329, 218103808, 84093646, 251658260,
+        117444111, 13485077, 7816633, 13964794, 6516446, 33558303, 167772178, 201432951, 67108883, 234881086,
+        100663322, 268435519, 134217755, 0,
+    ),
+    (
+        9980260, 11555367, 150997513, 12767878, 184552007, 218276590, 29816076, 251658283, 50334861, 89883541,
+        117440527, 13868240, 14013916, 14257978, 167774097, 33554432, 14495455, 67112793, 201328275,
+        100663358, 234881024, 134217755, 268435519, 0,
+    ),
+    (
+        1859908, 16828936, 61135113, 11077962, 83886094, 127472587, 151177707, 196447506, 224849235, 12543280,
+        251661402, 7310834, 7576789, 33554454, 67110778, 100789975, 134217759, 167772220, 201326653,
+        234881086, 268435519, 0, 0, 0,
+    ),
+    (
+        1859908, 16828936, 53908068, 2794533, 83886094, 4518630, 117440555, 151176743, 184737042, 225109209,
+        251853877, 7282068, 7568568, 33789299, 67229114, 100906903, 134217759, 167772220, 201326653,
+        234881086, 268435519, 0, 0, 0,
+    ),
+    (
+        10381668, 1491460, 150997513, 2649133, 184549417, 3084782, 218106858, 28101780, 251658240, 50332501,
+        83944883, 117441524, 6247452, 33555997, 4842614, 67237495, 100664979, 134217755, 167775804, 201330301,
+        234884798, 268439295, 0, 0,
+    ),
+    (
+        10381668, 161516292, 12767813, 184549417, 229157766, 12522183, 251658283, 16778004, 50386290,
+        97469334, 117503440, 7675228, 39921590, 73742327, 100663322, 134217755, 167775804, 201330553,
+        234885050, 268439547, 0, 0, 0, 0,
+    ),
+    (
+        1859908, 26264104, 60084841, 4252330, 83886118, 10285803, 117440556, 150994944, 184650577, 218105006,
+        251661273, 12954643, 7453844, 33555827, 67110742, 100665239, 134217759, 183737656, 16215733,
+        201326651, 234885047, 268435519, 0, 0,
+    ),
+    (
+        1859908, 3180840, 16777257, 53779109, 11314214, 83888590, 151176267, 117440527, 184550573, 218106776,
+        251658287, 6895216, 13219121, 40987861, 67110743, 100663326, 134219772, 167775544, 201563517,
+        235122110, 268680703, 0, 0, 0,
+    ),
+    (
+        10381668, 1346308, 150994984, 195322477, 3072647, 218103850, 16954159, 251658240, 50332500, 83886094,
+        117441871, 7698198, 6682142, 33621722, 71814196, 100865205, 167772216, 148582227, 201326649,
+        250342899, 268439547, 0, 0, 0,
+    ),
+    (
+        10381668, 1491460, 150994984, 10773101, 184549386, 229159406, 16778031, 251658283, 50332500, 83887438,
+        117441935, 7960412, 15833048, 16221914, 167775536, 14150777, 201326650, 235105471, 268664059,
+        33554448, 67108881, 100663314, 134217747, 0,
+    ),
+    (
+        1859908, 3293736, 16777257, 50387273, 11428522, 83886987, 117440527, 151176231, 184549421, 218103854,
+        251661272, 7186001, 8251228, 15926482, 33554452, 67198072, 167772212, 100667222, 201546937, 134217751,
+        251358899, 268697335, 0, 0,
+    ),
+    (
+        1859908, 20070952, 11162217, 50331661, 87734666, 129135563, 150994944, 184549421, 218103854,
+        251661272, 7452313, 15157112, 14023710, 15690874, 4682802, 168019123, 33555731, 67108885, 201326653,
+        100663318, 134217751, 234881086, 268435519, 0,
+    ),
+    (
+        10381668, 151161604, 184717869, 218278789, 253426377, 5288394, 16777228, 50332501, 83886094,
+        117440527, 8251228, 4689680, 16065972, 167772208, 33653975, 201546873, 6778046, 67108922, 234881024,
+        100773363, 134221787, 268435515, 0, 0,
+    ),
+    (
+        10381668, 150997548, 195330349, 218106542, 251661039, 2646597, 16827079, 50331661, 83886094,
+        117505328, 7822428, 8334750, 5492211, 167772216, 5837845, 5055997, 201328185, 33554432, 67110526,
+        234881082, 100667354, 268435515, 134217755, 0,
+    ),
+    (
+        1859908, 10783016, 16829093, 11432550, 50331661, 150995628, 83952572, 184552267, 218103854, 117440527,
+        251852349, 4973657, 180440376, 7050453, 201530710, 7579099, 33778879, 234881024, 67110771, 100667102,
+        134221279, 268435456, 0, 0,
+    ),
+    (
+        1859908, 9869608, 16826922, 15891174, 50332489, 83886986, 154975037, 117440512, 184552493, 218106990,
+        251915439, 4686899, 167772212, 6812824, 6905428, 215312083, 33670650, 234881078, 67112669, 268435511,
+        100663326, 134217759, 0, 0,
+    ),
+    (
+        10381668, 10506756, 11049592, 2801222, 3124999, 167988244, 16777228, 50388821, 201528373, 83887502,
+        117623951, 158408438, 6366685, 33557374, 234881049, 184549395, 67108894, 112932535, 218216447,
+        268435456, 134217728, 251658287, 0, 0,
+    ),
+    (
+        10381668, 10915448, 11043132, 15381061, 151175814, 19968509, 50331661, 83887028, 167772208, 117440527,
+        184617854, 5578452, 214290421, 6411666, 33557934, 218103827, 234881074, 67110809, 251886579,
+        268435479, 100664991, 134217755, 0, 0,
+    ),
+    (
+        1859908, 16828680, 9945716, 50388326, 87808458, 14222072, 117638097, 167772222, 5215762, 201326641,
+        13272345, 5764791, 150994988, 234883706, 184642395, 33557724, 79341021, 218103867, 268435456,
+        100663326, 251661039, 134217759, 0, 0,
+    ),
+    (
+        1859908, 9658164, 10214949, 16777992, 53779879, 98886312, 117502718, 167775248, 150994988, 11009681,
+        214257106, 5584443, 184551021, 218106542, 234881074, 41088662, 251869911, 268435456, 67108893,
+        100665243, 134217759, 0, 0, 0,
+    ),
+    (
+        10115329, 151177767, 184552297, 218106794, 2146607, 16777259, 251658245, 50385289, 2035210, 6493451,
+        83945268, 13462677, 117503609, 6911861, 7302814, 168021727, 33555511, 201326653, 67112849, 234881024,
+        100663314, 268435519, 134217747, 0,
+    ),
+    (
+        10115329, 151177767, 184552045, 218106542, 5435908, 251658283, 1412208, 14718741, 7704982, 20017842,
+        48712912, 50455386, 67108881, 83887246, 100663296, 121418951, 15580853, 134217759, 167775676,
+        201326653, 234881086, 268439543, 0, 0,
+    ),
+    (
+        1859908, 9865473, 11446697, 151177672, 16777228, 184605513, 50334986, 83886094, 117502704, 218221464,
+        13063760, 251852634, 13233563, 182681361, 216520691, 33555604, 234884798, 67112917, 268435515,
+        100664534, 134217751, 0, 0, 0,
+    ),
+    (
+        1859908, 10914049, 11430565, 16826919, 150997784, 2463540, 50331661, 184551085, 7276362, 83887029,
+        5855124, 218103854, 117503435, 33623473, 251658287, 13180727, 67108920, 167772191, 201404029,
+        100663358, 234881082, 149766131, 268435456, 0,
+    ),
+    (
+        2380292, 6, 11700481, 10934602, 150997383, 184549415, 218278795, 254983152, 16777265, 50388530,
+        87792947, 131661493, 5471964, 167776029, 201577502, 234885023, 268436863, 33653905, 67212502,
+        100663322, 134219479, 0, 0, 0,
+    ),
+    (
+        20996, 11682369, 150997541, 11823590, 184552010, 12255943, 218103850, 251837425, 16778034, 13843996,
+        50332509, 15423417, 83886094, 6516447, 167772220, 201578137, 117695479, 234881051, 268521424,
+        33554432, 67110225, 100742546, 134217751, 0,
+    ),
+    (
+        1859908, 2509320, 152233, 16777985, 50331661, 86829482, 117440527, 151177707, 184552749, 218323888,
+        266007601, 14664818, 5233874, 168005528, 201326649, 234884756, 268439547, 40985945, 67229146,
+        100663326, 134219739, 0, 0, 0,
+    ),
+    (
+        1859908, 150024, 27562753, 50334029, 84059018, 3979664, 117440555, 150997799, 184621940, 218323888,
+        251861970, 14664950, 168005490, 201564060, 242984819, 268439295, 33654047, 67110485, 100771286,
+        134217755, 0, 0, 0, 0,
+    ),
+    (
+        10381668, 2380292, 151022124, 2019969, 184550121, 27986828, 218103821, 50332591, 83886123, 251661391,
+        117440512, 13606072, 13978938, 183729910, 201330517, 234881086, 268439510, 39912924, 67213137,
+        7185618, 100663326, 134217759, 0, 0,
+    ),
+    (
+        10381668, 2380292, 161508097, 10779466, 184550128, 218106794, 16777228, 50525012, 251718763, 83886080,
+        117440527, 5741752, 14134516, 183745942, 201577975, 234881086, 268435519, 40993872, 74814674,
+        100787930, 134217759, 0, 0, 0,
+    ),
+    (
+        1859908, 9476616, 16945921, 50483853, 83888782, 117502694, 151177707, 184552308, 218106805, 251658287,
+        13093942, 14519485, 167775795, 201561150, 234882682, 268439295, 4830298, 33556244, 67229011,
+        100787670, 134217759, 0, 0, 0,
+    ),
+    (
+        1859908, 2568, 16777985, 50385508, 87708329, 3979690, 117440528, 162630123, 184552308, 218295633,
+        258407856, 14626609, 167776120, 217816282, 234884754, 268681179, 40981779, 67229142, 100663326,
+        134217759, 0, 0, 0, 0,
+    ),
+    (
+        9980260, 11555367, 150997513, 2019974, 197323339, 16779916, 218103857, 50334669, 251659179, 83886080,
+        117440527, 15011378, 15420625, 183723189, 5232443, 201326647, 234881086, 268695380, 5895518, 33554456,
+        67110487, 100663322, 134217755, 0,
+    ),
+    (
+        9980260, 11555367, 150997513, 12767878, 184552007, 27839371, 218104689, 50331695, 251658283, 83944754,
+        117440527, 13436728, 15418745, 15848565, 167772214, 14668987, 201326611, 234885022, 268563903,
+        33555991, 67108889, 100663322, 134217755, 0,
+    ),
+    (
+        1859908, 16828936, 61133412, 2689701, 83886094, 3978342, 117440555, 150997799, 184737042, 218295635,
+        264203284, 14888021, 13463159, 6534650, 167772220, 49661593, 201326592, 67110747, 234881086,
+        100663326, 268435519, 134217759, 0, 0,
+    ),
+    (
+        1859908, 16828936, 61133412, 2794533, 83886094, 3978342, 117440555, 151176359, 189631348, 218103854,
+        257100789, 13212790, 13458936, 15300025, 167776059, 201330522, 234999707, 33554432, 268435519,
+        67108893, 100663326, 134217759, 0, 0,
+    ),
+    (
+        10381668, 161516292, 12767813, 184740422, 218106506, 12368967, 251658283, 16862348, 50332501,
+        84096398, 117505296, 13993047, 5057945, 15840951, 33554460, 167772216, 201330301, 67108893, 100665278,
+        234881082, 134221791, 268435515, 0, 0,
+    ),
+    (
+        10381668, 161516292, 12767813, 184549417, 229157766, 12368967, 251658283, 16829588, 50332501,
+        83946710, 121467956, 39917365, 15848630, 67108889, 168002807, 216383322, 100665278, 234881082,
+        134461439, 268435456, 0, 0, 0, 0,
+    ),
+    (
+        1859908, 3180840, 16777257, 53779109, 3712038, 83886123, 11580519, 150994959, 117440557, 184549394,
+        218103854, 251661272, 7013971, 5618772, 33556274, 67108893, 108623283, 134219768, 15425140, 183729910,
+        201326653, 234881086, 268435519, 0,
+    ),
+    (
+        1859908, 3180840, 16777257, 53779109, 11314214, 83944167, 150996076, 184549421, 117440527, 218179118,
+        251658287, 6895216, 13219121, 33672725, 7695667, 67108921, 167776023, 100666718, 134217759, 201330554,
+        251363062, 268435519, 0, 0,
+    ),
+    (
+        10381668, 1491460, 150994984, 2648905, 184549417, 229159406, 16956364, 251658240, 50332500, 83886997,
+        117441494, 7698192, 39921553, 73744159, 100861620, 134217755, 16457085, 14630070, 167776248,
+        201326649, 234881082, 268435515, 0, 0,
+    ),
+    (
+        10381668, 1491460, 150994984, 2648905, 184549417, 229159406, 16956364, 251658240, 50332500, 83887438,
+        117531600, 13829980, 7959676, 33555986, 168004977, 73742333, 114007450, 201326654, 134217755,
+        235122163, 268439295, 0, 0, 0,
+    ),
+    (
+        1859908, 20070952, 11162217, 50331661, 87624074, 3979755, 117443345, 150994944, 184549421, 218103854,
+        251733551, 5350617, 41125211, 74808342, 100663326, 134221407, 13577905, 183721716, 201580022,
+        234881086, 268435519, 0, 0, 0,
+    ),
+    (
+        1859908, 20070952, 11162217, 50331661, 87624074, 121420267, 150994988, 184552273, 218105006,
+        251661272, 12666451, 12934682, 6002420, 33554460, 15424663, 67108893, 100663326, 134348211, 168021499,
+        201326653, 234881086, 268435519, 0, 0,
+    ),
+    (
+        10381668, 1491460, 150994984, 196514185, 218294922, 263123655, 16777228, 50332500, 83886997,
+        117441494, 7698228, 4582736, 38374844, 67212511, 100663322, 134220827, 13311485, 167772216, 201564083,
+        234885114, 268435515, 0, 0, 0,
+    ),
+    (
+        10381668, 10666500, 150994949, 184717933, 218276270, 251837386, 20005575, 3497012, 50331701, 87778737,
+        4553872, 117440527, 4836599, 33554456, 73742237, 100664991, 134219516, 167775805, 201330302,
+        234884799, 268435515, 0, 0, 0,
+    ),
+    (
+        1859908, 20072968, 53909833, 3713450, 83886123, 117502695, 150994988, 184552316, 218106776, 251852413,
+        4304816, 16587867, 5713428, 33646354, 67228887, 100666974, 134219763, 167772212, 201330042, 234884854,
+        268435511, 0, 0, 0,
+    ),
+    (
+        1859908, 3293736, 16777257, 53913929, 2783974, 150994988, 83886094, 184552316, 121824203, 218103808,
+        12572208, 251658257, 6808753, 5322418, 7167987, 33556246, 67340119, 100663326, 134217759, 167775545,
+        201330042, 234884539, 268435511, 0,
+    ),
+    (
+        10381668, 2380292, 14723590, 11055593, 16778041, 50332523, 150997818, 83887036, 184737083, 218106813,
+        117503294, 5622837, 167772176, 4715933, 214247319, 251788278, 33555987, 67112089, 234881024,
+        100873911, 268435483, 134217728, 0, 0,
+    ),
+    (
+        10381668, 1475076, 11178616, 2798009, 151243578, 16233159, 184549421, 16778004, 218105198, 50331661,
+        251874302, 88401296, 121632210, 180475667, 33773086, 67110873, 201326641, 100665014, 134220955,
+        234881024, 268439027, 0, 0, 0,
+    ),
+    (
+        1859908, 16777992, 50479945, 9744180, 83886094, 16210315, 117440527, 16476711, 150994988, 12025848,
+        167772208, 184549417, 233499321, 201329744, 6796376, 5612692, 256846575, 234881024, 13464987,
+        268435484, 33554432, 67108893, 100663326, 134217759,
+    ),
+    (
+        1859908, 16777992, 9739556, 50332540, 16153958, 83946890, 151177784, 14603006, 117441551, 184720313,
+        4979665, 218106520, 251661050, 167853081, 5748372, 214267606, 33554460, 234881074, 67108893,
+        100666590, 268435456, 134217759, 0, 0,
+    ),
+    (
+        10115329, 151177767, 184552297, 218106542, 2289932, 16777229, 251658283, 52749573, 1674352, 46777359,
+        86724117, 13488601, 6250070, 117487514, 14284538, 67110011, 167775740, 201326653, 100663314,
+        234881086, 268436735, 134217728, 0, 0,
+    ),
+    (
+        10115329, 150997800, 184720231, 229163310, 16970253, 251658283, 52752718, 83930630, 117486855,
+        13720688, 5885080, 48715344, 67109981, 7959706, 100663354, 8337147, 167772220, 134217747, 201330550,
+        234881086, 268439039, 0, 0, 0,
+    ),
+    (
+        1859908, 9865473, 11430569, 28363208, 150994944, 50386441, 5456540, 184549421, 83946521, 12107101,
+        218105521, 33554448, 13301659, 251659254, 117440512, 182679548, 71800179, 201326653, 4812730,
+        234881083, 100663296, 268436735, 134217751, 0,
+    ),
+    (
+        1859908, 10914049, 11430565, 16828872, 150997769, 50334989, 83886986, 117503499, 7443504, 184549421,
+        7033969, 33554452, 218180509, 67110262, 251658287, 107968406, 167902780, 15195283, 201326615,
+        134217728, 234884798, 268648191, 0, 0,
+    ),
+    (
+        2380292, 10633601, 150994988, 10005349, 184552039, 229302983, 13024240, 251658252, 16777216, 53972210,
+        15060240, 6349941, 83886134, 15693690, 117687250, 167772190, 33556436, 201326653, 234881086,
+        268439507, 67110233, 100664730, 134219479, 0,
+    ),
+    (
+        2380292, 162695425, 10250661, 184720202, 12772039, 218103850, 16970545, 251661042, 50388531, 97840756,
+        117441488, 5465914, 4701661, 167772220, 201450877, 33554456, 234885010, 67368534, 268435456,
+        100663322, 141391071, 0, 0, 0,
+    ),
+    (
+        1859908, 2509320, 41, 16777985, 50334029, 84059018, 121696998, 151177707, 184552273, 218295348,
+        13063316, 251661298, 13485430, 5848572, 167776120, 201330302, 33558168, 234881024, 268439295,
+        67213143, 100664990, 134219739, 0, 0,
+    ),
+    (
+        1859908, 150024, 16777985, 50500425, 94954149, 121418790, 162601451, 184736820, 230366546, 264187284,
+        6540787, 167772216, 201561469, 250189054, 33554460, 268694971, 67110746, 100663326, 134346455, 0, 0,
         0, 0, 0,
     ),
     (
-        10381668, 162562344, 196383081, 12100010, 218103856, 254573547, 16777228, 50334797, 83887032,
-        117440527, 13610169, 172183355, 16588733, 201544860, 241394909, 268519351, 33554432, 73754581,
-        100664983, 134217755, 0, 0, 0, 0,
-    ),
-    (
-        1593636, 10902023, 16933640, 60609130, 95478443, 150994944, 129450955, 184549376, 218106805,
-        251661743, 14909308, 168008766, 15725882, 201329749, 239543318, 268645527, 33653980, 67229337,
-        100665243, 134217759, 0, 0, 0, 0,
-    ),
-    (
-        10381668, 162693636, 196514373, 11207302, 218103854, 3347143, 16780267, 266398861, 50331663, 83889779,
-        117440512, 15418448, 167772220, 201579858, 15723923, 234884568, 268435519, 7161497, 40990101,
-        67108893, 100663326, 134217759, 0, 0,
-    ),
-    (
-        1859908, 3181092, 16779877, 61498185, 10281616, 83886123, 11596497, 117440564, 150994962, 184552813,
-        218103854, 251659503, 14386480, 13196409, 14658774, 7720663, 33654750, 167773820, 67110589, 201326654,
-        100667355, 234881024, 134217728, 268435456,
-    ),
-    (
-        10115336, 1347879, 151038760, 187619910, 3318256, 16777262, 218103857, 55769805, 251658240, 83952974,
-        117440527, 4672662, 13471063, 5057945, 15842778, 182714301, 33558108, 201330333, 67112670, 234881024,
-        100663327, 268435456, 134217728, 0,
-    ),
-    (
-        1859908, 19040524, 10900493, 50331657, 4630926, 83886090, 4897231, 117440523, 150994988, 184549421,
-        218203374, 251658287, 7013657, 13219185, 33554460, 67200883, 100665239, 134219768, 15683257,
-        183729589, 201326653, 234881086, 268435519, 0,
-    ),
-    (
-        10381668, 1475076, 150997769, 196387241, 230207978, 29180715, 251658240, 50333005, 83887502,
-        117441999, 7964508, 33554448, 13739993, 67181915, 113585206, 134298807, 168021555, 201580217,
-        234885051, 268435519, 0, 0, 0, 0,
-    ),
-    (
-        1859908, 19958308, 53779045, 3713702, 83886096, 3980007, 117440556, 150994989, 184738904, 218103855,
-        251658265, 5093010, 33555740, 8252445, 72822577, 100757363, 134221719, 167775796, 216494069,
-        234884791, 268435515, 0, 0, 0,
-    ),
-    (
-        10381668, 162693636, 196514373, 230335110, 254573547, 16778508, 50333005, 83887502, 117440527,
-        7698192, 15960030, 33555985, 67110521, 7013565, 100663354, 147277019, 167772160, 16465650, 201326645,
-        234881078, 268439543, 0, 0, 0,
-    ),
-    (
-        1859908, 3181092, 16779877, 53913993, 3713767, 83886124, 150994944, 117505803, 184549421, 218106776,
-        264230553, 13743124, 4677560, 33555804, 81524601, 167970194, 100663326, 5076983, 134217786, 201326641,
-        234881074, 268439283, 0, 0,
-    ),
-    (
-        10381668, 162693636, 10977861, 184553261, 230335110, 11506375, 251662255, 16777228, 167775536,
-        50331661, 83947185, 117441492, 15686812, 6379421, 49612787, 4679065, 201326618, 234881024, 6289106,
-        67108883, 100663351, 134217728, 268435456, 0,
-    ),
-    (
-        1859908, 151177764, 16777992, 14851365, 184552316, 50332489, 218294950, 83886986, 15383911, 251661309,
-        117441483, 167772208, 16584126, 4683313, 201328249, 234884252, 33558228, 72689309, 268438750,
-        105756063, 134217751, 0, 0, 0,
+        10381668, 2380292, 44, 151159169, 2915146, 184549417, 29551244, 218103821, 50331648, 251661291,
+        83944753, 117673103, 13866320, 6503802, 15801750, 167772219, 201578103, 234881086, 268435519, 5076626,
+        33554460, 67110747, 100663326, 134217759,
+    ),
+    (
+        10381668, 516, 11571521, 151159430, 11965127, 184549424, 16779916, 218103854, 50334797, 255523540,
+        83886080, 117441522, 13700629, 15424761, 168021398, 217560631, 234885009, 268435519, 33554460,
+        73258578, 100665242, 134346451, 0, 0,
+    ),
+    (
+        1859908, 9476616, 16777985, 50331661, 3035817, 84060558, 117441551, 151177959, 184735284, 12774737,
+        218105428, 251661302, 16199473, 174706168, 33554432, 5582771, 201326649, 67348351, 234881024,
+        268435515, 100787603, 134346203, 0, 0,
+    ),
+    (
+        1859908, 8, 16777985, 59822696, 87726410, 11166416, 117440527, 151177707, 198366296, 224877614,
+        251861972, 16199478, 167849498, 15199731, 201326620, 33554432, 234884799, 268435515, 74802389,
+        100665243, 134219735, 0, 0, 0,
+    ),
+    (
+        9980260, 11555367, 150997513, 195482246, 12104176, 218103850, 16777228, 50535373, 89336526, 251658240,
+        117444111, 15013648, 40086835, 14013589, 167997243, 217544595, 234972798, 67108864, 268435519,
+        100664983, 134219487, 0, 0, 0,
+    ),
+    (
+        9980260, 11555367, 150997513, 2019974, 197180329, 218103850, 16777228, 257080431, 50331661, 83889294,
+        117441528, 4429148, 15415156, 33556021, 15953617, 167772178, 206560734, 234885014, 268435519,
+        67108889, 100664983, 134219487, 0, 0,
+    ),
+    (
+        1859908, 16828936, 61133412, 3713360, 83886122, 3978342, 117440555, 164809170, 184628781, 218189166,
+        265903088, 14536497, 39530009, 167772160, 201563389, 251379351, 67110557, 100665243, 134217759,
+        268435519, 0, 0, 0, 0,
+    ),
+    (
+        1859908, 16828936, 61133412, 2795856, 83886094, 4518630, 117440555, 150997799, 196560402, 218106805,
+        14351379, 251860249, 7572663, 33554453, 15297785, 74954391, 100665243, 167772220, 201326653,
+        134221727, 234881024, 268435519, 0, 0,
+    ),
+    (
+        10381668, 161516292, 10932805, 184549424, 229157766, 12893127, 251658283, 16778004, 63755634,
+        83944888, 15037492, 117440527, 40064785, 6919350, 67348307, 100787959, 134217759, 167776059,
+        201326653, 234881086, 268435519, 0, 0, 0,
+    ),
+    (
+        10381668, 161516292, 10932805, 184549808, 218276526, 3079239, 251661012, 16778034, 50541397, 83886998,
+        117441524, 13989648, 33654609, 67212470, 7185655, 100663326, 134219768, 183746233, 201326653,
+        234881086, 268435519, 0, 0, 0,
+    ),
+    (
+        1859908, 3180840, 16777257, 53779109, 3712038, 83886123, 162575463, 117440527, 184549421, 218293778,
+        251763700, 14001392, 7163004, 33672341, 13462973, 67108893, 100665239, 134217759, 182681598,
+        201326649, 234881082, 268435515, 0, 0,
+    ),
+    (
+        1859908, 3180840, 16777257, 53779109, 11338406, 83886094, 151175911, 117625935, 184549376, 218106776,
+        251661266, 5090329, 13219121, 33765141, 67110742, 100665239, 134217759, 14146876, 14679486, 167772216,
+        201326649, 234881082, 268435515, 0,
+    ),
+    (
+        10381668, 1491460, 150994984, 2648905, 184549417, 229159406, 5295088, 16777259, 251658240, 50331661,
+        83944817, 121466384, 7808785, 7962194, 33555987, 67110495, 100663322, 134217755, 13614906, 167775549,
+        201326645, 234884542, 268439039, 0,
+    ),
+    (
+        10381668, 1491460, 150994984, 2648905, 184549417, 229159406, 16780236, 50334413, 251658260, 83886094,
+        117507029, 4576668, 39921118, 67213267, 100663322, 134217755, 15146544, 15679154, 167775548,
+        201330549, 234885046, 268439543, 0, 0,
+    ),
+    (
+        1859908, 20070952, 11162217, 50331661, 87624074, 2955755, 117440527, 150994988, 184552274, 218106776,
+        258426095, 5723796, 40990422, 67108893, 100663326, 134221215, 15191544, 167772208, 15675057,
+        201330547, 234881086, 268435519, 0, 0,
+    ),
+    (
+        1859908, 20070952, 11162217, 50331661, 4254090, 83886123, 129135563, 150994944, 184552273, 218103854,
+        251852306, 6894873, 40986325, 67110743, 100663326, 134217759, 14642548, 168021048, 15412849,
+        201572211, 234881086, 268435519, 0, 0,
+    ),
+    (
+        10381668, 1491460, 150994984, 195324745, 218276526, 11471815, 251658251, 16778004, 50386289, 83886998,
+        117503440, 4925201, 7818451, 33554456, 81108510, 167772220, 100663322, 134219487, 16482166, 201330303,
+        234881082, 268435515, 0, 0,
+    ),
+    (
+        10381668, 161516292, 195482181, 229157766, 264155847, 16777228, 50332941, 83887438, 117440527,
+        39913238, 4838487, 67213232, 7023699, 100663327, 134219507, 168005428, 216493941, 235122615,
+        268439295, 0, 0, 0, 0, 0,
+    ),
+    (
+        1859908, 20070952, 11162217, 50331661, 3712038, 84048593, 151243531, 117441679, 184552280, 218106813,
+        251851993, 5502654, 12674395, 46517527, 167772216, 67108893, 100663326, 134348402, 215465651,
+        234881078, 268435511, 0, 0, 0,
+    ),
+    (
+        1859908, 10783016, 16777228, 53779109, 10281638, 83886123, 117621707, 150995004, 184549421, 218172312,
+        264050301, 5091218, 33670463, 74802523, 100665239, 134220831, 167775544, 215428721, 235105971,
+        268439035, 0, 0, 0, 0,
+    ),
+    (
+        10381668, 2380292, 1743416, 11315897, 15532538, 16237265, 12660628, 16781260, 150994988, 167772212,
+        50332501, 184552278, 83886094, 121468149, 218105646, 12445558, 251658264, 33781745, 201326592,
+        67108889, 100663322, 134220955, 234881024, 268435507,
+    ),
+    (
+        10381668, 14844420, 1741381, 2069162, 32033483, 50578299, 16772948, 150994988, 83887438, 117441488,
+        7538065, 184549421, 167987031, 218294162, 33555987, 12539487, 67108913, 251658240, 201326592,
+        100663322, 134219510, 234881074, 268439027, 0,
+    ),
+    (
+        1859908, 16777992, 9503348, 50331661, 13967141, 4969126, 83888590, 14499766, 14939403, 117504789,
+        12035641, 150997563, 167775254, 184552025, 201329774, 218106522, 234881074, 263042543, 268435507,
+        33554460, 67108893, 100663326, 134217759, 0,
+    ),
+    (
+        1859908, 20138248, 10002213, 50335053, 94167741, 133755638, 16584247, 6526060, 12041874, 150997523,
+        10831470, 184551061, 167775279, 218103850, 264680859, 201326592, 33556247, 67108893, 234881074,
+        100663326, 134221023, 268435456, 0, 0,
+    ),
+    (
+        10115329, 10910504, 150994989, 184549376, 218277422, 3475212, 38868591, 251661021, 67108885, 1142042,
+        7175518, 16777759, 1543222, 50334793, 100666962, 2847154, 83887034, 134217747, 121420999, 167776059,
+        201326653, 234881086, 268435519, 0,
+    ),
+    (
+        10115329, 150997800, 196778855, 224414348, 16811823, 258388877, 7816197, 33752335, 50331657, 6843509,
+        84009650, 1908147, 67108885, 117551864, 5895351, 100663353, 134456535, 167775996, 201326653,
+        234881086, 268435519, 0, 0, 0,
+    ),
+    (
+        1859908, 9865473, 7498409, 10343723, 163759637, 33555481, 2299802, 184552283, 16778015, 218295602,
+        62709065, 251658240, 15953110, 83956618, 67108919, 182702807, 117441679, 100663296, 201326649,
+        134221715, 234881082, 268439547, 0, 0,
+    ),
+    (
+        1859908, 10914049, 11430565, 27051784, 150994988, 5282845, 184552557, 50332504, 33620638, 218107054,
+        83889422, 2989269, 251661301, 117442511, 67110289, 14927542, 167869915, 100663314, 134456569,
+        201326653, 234885051, 268435519, 0, 0,
+    ),
+    (
+        2380292, 6, 11700481, 150994954, 2021989, 184549414, 229303015, 251661039, 12698648, 8095577,
+        33555761, 16778316, 13446303, 50331661, 5090932, 83887029, 67110266, 117503734, 100666838, 134217751,
+        167772220, 201330555, 234881086, 268435519,
+    ),
+    (
+        2380292, 10668289, 150994981, 11958662, 184717959, 218278795, 16778031, 251658283, 53941296, 4663064,
+        84118734, 33554452, 6630772, 117440527, 14540217, 67196122, 8220318, 100665084, 167772160, 134221655,
+        201326592, 234885051, 268435519, 0,
+    ),
+    (
+        1859908, 2509320, 16828993, 50334029, 88140426, 117504395, 11696849, 150994962, 184549421, 218106780,
+        13751508, 251658287, 39935868, 12677118, 6155381, 67214518, 115453151, 167772160, 134452983,
+        201326592, 234881082, 268435515, 0, 0,
+    ),
+    (
+        1859908, 2568, 26252033, 50332521, 11076261, 93918091, 117440527, 162605547, 184549421, 218103854,
+        251658287, 7587028, 12797309, 40050686, 13462898, 6679965, 67108887, 167772216, 100793946, 201326592,
+        134217755, 234884791, 268435515, 0,
+    ),
+    (
+        10381668, 2380292, 161508097, 10793418, 184549421, 218106794, 16777228, 50525453, 251658283, 83886094,
+        130085909, 15439288, 6276184, 7446269, 33554481, 5242770, 13483162, 167774068, 67108864, 201326645,
+        100666782, 234881024, 134221279, 268435456,
+    ),
+    (
+        10381668, 20996, 10525441, 150994950, 186553005, 218278795, 16971020, 50509133, 251658240, 83886094,
+        121463864, 15306352, 15539991, 6758226, 13189118, 33554460, 167775514, 201447157, 67108915, 234881078,
+        100663326, 268435511, 134217759, 0,
+    ),
+    (
+        1859908, 2568, 26264129, 50331661, 3840330, 83888784, 117502694, 6363627, 150994988, 184552749,
+        218293529, 264086709, 14933814, 33556245, 15197403, 7843831, 67108923, 100787670, 134217759,
+        167772208, 201326641, 234881074, 268435507, 0,
+    ),
+    (
+        1859908, 8, 16828929, 10801764, 50331664, 11069770, 83886097, 128776587, 151176359, 198286168,
+        218103854, 258559343, 7565075, 33554488, 14507867, 15298489, 67352447, 167775255, 100663326,
+        201326641, 234883058, 134217728, 268435507, 0,
+    ),
+    (
+        9980260, 11555367, 150997513, 195482246, 12772039, 218104618, 16777216, 11326767, 50331697, 251658240,
+        83889294, 117670927, 15058005, 33768989, 6005918, 14400883, 67356243, 167772160, 217413623, 234881086,
+        268435519, 100663322, 134217755, 0,
+    ),
+    (
+        9980260, 11555367, 151159177, 10777261, 184738544, 218106516, 22485964, 251658283, 50331661, 14771122,
+        83887056, 117440512, 7838940, 33653876, 7961978, 8371602, 167773436, 67110519, 201326653, 100663322,
+        234881086, 268435519, 134217755, 0,
+    ),
+    (
+        1859908, 16828936, 61133412, 3713360, 83886122, 3978342, 117440555, 151176359, 184737048, 218106771,
+        12424501, 251659632, 46518070, 6909815, 167775794, 7812606, 67108921, 201326655, 234881082, 268439259,
+        100663326, 134217759, 0, 0,
+    ),
+    (
+        1859908, 16828936, 10803465, 50331664, 87730506, 4088907, 117440555, 162690578, 184737049, 218106771,
+        5442906, 251658287, 5753974, 33782940, 173790968, 216366334, 67108893, 234885114, 100667102,
+        268435456, 134217759, 0, 0, 0,
+    ),
+    (
+        10381668, 161516292, 195482181, 2820998, 218103850, 13038279, 251661012, 22514828, 56311373, 83886094,
+        15418832, 117440527, 6510353, 33674427, 67358105, 167772160, 108754579, 201326653, 234885019,
+        134217759, 268435519, 0, 0, 0,
+    ),
+    (
+        10381668, 1346308, 151179880, 184552006, 2026506, 218106507, 263015535, 16777228, 50388117, 87766456,
+        121586745, 4572666, 6368605, 33554462, 167772220, 72334745, 100793818, 201326653, 134217755,
+        234881086, 268435519, 0, 0, 0,
+    ),
+    (
+        1859908, 3180840, 16777257, 53779109, 3713424, 83886123, 11580519, 150994959, 117440512, 12011026,
+        184549429, 218106777, 251765999, 7163312, 13196785, 33646392, 67110771, 168019449, 100663326,
+        201457530, 134217728, 234885051, 268435519, 0,
+    ),
+    (
+        1859908, 20070952, 53891689, 3712042, 83886118, 3044459, 117443343, 150994944, 184734872, 218293876,
+        12518645, 251658266, 7324982, 168002929, 5996402, 33558428, 82171379, 201328575, 100663354, 234881024,
+        268437499, 134217728, 0, 0,
+    ),
+    (
+        10381668, 1491460, 150994984, 2648905, 184740905, 218149354, 11324401, 16777236, 251658240, 50331661,
+        83944818, 121582992, 7677713, 5106967, 33656373, 73885689, 100892314, 134217755, 167776059, 201326653,
+        234881086, 268435519, 0, 0,
+    ),
+    (
+        10381668, 1346308, 150994984, 195322477, 12771975, 218299019, 28132145, 251658240, 50332530, 83952533,
+        130874902, 4673116, 4838906, 39972597, 73790710, 100665015, 134217755, 167772220, 201326653,
+        234881086, 268435519, 0, 0, 0,
+    ),
+    (
+        1859908, 20070952, 11162217, 50331661, 87624074, 3044459, 117440527, 150994988, 184552274, 218106776,
+        251659503, 12690713, 12938517, 13204827, 33554460, 67231155, 100663326, 134219767, 15707768,
+        167772220, 201326653, 234881086, 268435519, 0,
+    ),
+    (
+        1859908, 3293736, 16777257, 50387273, 10003498, 83944171, 117601359, 150994988, 184552274, 218106776,
+        258426095, 12692820, 14507126, 40987803, 67230935, 100665272, 134217759, 183746233, 201326653,
+        234881086, 268435519, 0, 0, 0,
+    ),
+    (
+        10381668, 151161604, 184720200, 229153669, 251834799, 12628426, 16829524, 54580594, 87627187,
+        117515223, 7683356, 33554456, 67110494, 100665013, 134331807, 168005431, 201330301, 234884798,
+        268439295, 0, 0, 0, 0, 0,
+    ),
+    (
+        10381668, 161513772, 184552045, 229302853, 2821062, 251658283, 13152753, 20005939, 55104849, 87770515,
+        117441495, 39966517, 73889718, 100894682, 134217755, 167772220, 201330553, 235122686, 268435515, 0, 0,
+        0, 0, 0,
+    ),
+    (
+        1859908, 10783016, 16829093, 11311504, 50332497, 4902695, 150994954, 83887037, 184549421, 134021003,
+        218293779, 251659887, 12670612, 40990107, 67110769, 100665266, 134219763, 167775544, 201330041,
+        234884538, 268439035, 0, 0, 0,
+    ),
+    (
+        1859908, 2267432, 16778021, 4233642, 50334413, 162574119, 83886094, 11842685, 184549391, 117440512,
+        218106814, 12420370, 251745535, 6227353, 13220954, 33556275, 67110772, 100663326, 134217759,
+        167772216, 201330293, 235106042, 268435511, 0,
+    ),
+    (
+        10381668, 10715652, 15706745, 2607749, 2649963, 150994988, 3142142, 16778004, 50332501, 83944470,
+        129299921, 184549376, 5101330, 33554456, 67110809, 218103854, 100791984, 167772212, 134220891,
+        251661679, 201326592, 234884530, 268438775, 0,
+    ),
+    (
+        10381668, 10522116, 1550969, 11516553, 16035590, 16544830, 3228369, 16780332, 150994944, 50332501,
+        83944598, 184612333, 117440512, 167890200, 33554451, 67230809, 218105518, 213773659, 100663296,
+        251658271, 134217782, 234881074, 268438775, 0,
+    ),
+    (
+        1859908, 20073736, 16146229, 4423606, 2619793, 15105554, 50331661, 3714728, 83886139, 150995692,
+        117440527, 5086040, 195380910, 5879151, 218221207, 33554432, 67108893, 167772208, 100842590,
+        201326592, 251658271, 134217778, 234881024, 268435507,
+    ),
+    (
+        1859908, 20070964, 16145788, 14457270, 50495373, 14987256, 83886094, 4699194, 5579476, 117441516,
+        150994984, 10851859, 184735130, 167775259, 33554460, 225880983, 67108864, 213773041, 100663296,
+        251658240, 134220959, 234881024, 268435507, 0,
     ),
 )
 
@@ -126,6 +689,7 @@
     wrap_sem,
     wrap_id_sem,
     detour_sem,
+    ready_sem,
     recv_sem,
     id_recv_sem,
 ):
@@ -153,8 +717,12 @@
     def greet(target):
         pl.semaphore_signal(barrier, inc=1, device_id=target, device_id_type=MESH)
 
-    for target in (device(0, 1), device(0, -1), device(1, 0), device(-1, 0)):
+    for target in (device(0, -1), device(1, 0), device(-1, 0)):
         greet(target)
+
+    @pl.when(j != RUN - 1)
+    def _():
+        greet(device(0, 1))
 
     even = lax.rem(j, 2) == 0
 
@@ -166,29 +734,46 @@
     def _():
         greet(device(0, 2))
 
+    def wrap_target(stream, owner, sender):
+        step = 1 - 2 * stream
+        return (0 if owner < SPAN else step, step * sender)
+
+    def wrap_links(stream):
+        links = [(distance, distance) for distance in range(1, SLOTS - 1)]
+        links += [(owner, sender) for which, owner, sender, _, _ in DETOURS if which == stream]
+        return sorted({(wrap_target(stream, *link), link[1]) for link in links})
+
+    def others(stream):
+        return [link for link in wrap_links(stream) if link[0] != (0, 1 - 2 * stream)]
+
     @pl.when(j == 0)
     def _():
-        for back in range(2, 7):
-            greet(device(0 if back < 4 else -1, -back))
-        greet(device(-1, -2))
-
-    @pl.when(j == RUN - 1)
-    def _():
-        for ahead in range(2, 7):
-            greet(device(0 if ahead < 4 else 1, ahead))
-        greet(device(1, 2))
+        for (dg, dk), _ in others(0):
+            greet(device(-dg, -dk))
+
+    far_sends = sum([(RUN - j == sender).astype(jnp.int32) for _, sender in others(0)])
+    far_sends += jnp.where(j == RUN - 1, len(others(1)), 0) - jnp.where(j == 0, 1, 0)
+    ready_count = sum([(j + 1 == sender).astype(jnp.int32) for _, sender in wrap_links(1)])
+    for (dg, dk), sender in others(1):
+
+        @pl.when(j + 1 == sender)
+        def _():
+            greet(device(dg, dk))
 
     def wrap_distance(stream):
         to_edge = RUN - j if stream == 0 else j + 1
         return to_edge, (to_edge >= 2) & (to_edge <= 6)
 
-    words = []
-    for i in range(len(ORDER[0])):
-        word = jnp.int32(ORDER[0][i])
-        for place in range(1, RUN):
-            if ORDER[place][i] != ORDER[place - 1][i]:
-                word = jnp.where(j >= place, ORDER[place][i], word)
-        words.append(word)
+    skips = jnp.where(even, j != RUN - 2, j != 1).astype(jnp.int32)
+    barrier_count = 4 + skips + far_sends
+
+    @pl.when(j == RUN - 1)
+    def _():
+        pl.semaphore_wait(barrier, barrier_count)
+        for (dg, dk), _ in wrap_links(1):
+            pl.semaphore_signal(
+                ready_sem, inc=1, device_id=device(-dg, -dk), device_id_type=MESH
+            )
 
     for stream, own in ((0, text_ids), (1, image_ids)):
         loads[stream].wait()
@@ -205,11 +790,9 @@
             line = line[:, at % 128 : at % 128 + piece]
             ids[stream, 0, c] = jnp.concatenate([line] * (128 // piece), axis=1)
 
-    far_sends = sum(wrap_distance(stream)[1].astype(jnp.int32) for stream in range(2))
-    for stream in range(2):
-        far_sends += (wrap_distance(stream)[0] == 2).astype(jnp.int32)
-    skips = jnp.where(even, j != RUN - 2, j != 1).astype(jnp.int32)
-    pl.semaphore_wait(barrier, 4 + skips + far_sends)
+    @pl.when(j != RUN - 1)
+    def _():
+        pl.semaphore_wait(barrier, barrier_count)
 
     def pick(stream, pair):
         return pair[stream] if isinstance(stream, int) else jnp.where(stream == 0, pair[0], pair[1])
@@ -301,17 +884,8 @@
             target,
         )
 
-    def wrap(stream, c):
-        far, slot, target = wrap_route(stream)
-
-        if c == 0:
-
-            @pl.when(far)
-            def _():
-                wrap_id_copy(stream).start()
-
-        if c % 2:
-            far = far & (wrap_distance(stream)[0] != DETOUR)
+    def wrap(stream, c, far):
+        _, slot, target = wrap_route(stream)
 
         @pl.when(far)
         def _():
@@ -323,26 +897,68 @@
                 target,
             ).start()
 
-    def detour_copy(stream, c):
-        step = pick(stream, (1, -1))
+    def wrap_early(stream):
+        to_edge, far = wrap_distance(stream)
+
+        @pl.when(far)
+        def _():
+            wrap_id_copy(stream).start()
+
+        for c in range(WAVES):
+            now = far & (to_edge < PATIENT[stream])
+            for which, owner, _, _, waves in DETOURS:
+                if which == stream and c in waves:
+                    now = now & (to_edge != owner)
+            wrap(stream, c, now)
+
+    def wrap_late(other, s, c):
+        for stream in range(2):
+            to_edge, far = wrap_distance(stream)
+            now = far & (to_edge >= PATIENT[stream]) & (other == 1 - stream) & (s == SPAN - 1)
+            for which, owner, _, _, waves in DETOURS:
+                if which == stream:
+                    kept = functools.reduce(jnp.logical_and, [c != wave for wave in waves])
+                    now = now & ((to_edge != owner) | kept)
+            wrap(stream, c, now)
+
+    def detour_copy(n, c):
+        stream, owner, sender, s, _ = DETOURS[n]
+        slot = owner if owner < SPAN else owner + 1
         return remote(
-            chunk(stream, SPAN - 1, c),
-            chunk(stream, DETOUR + 1, c),
-            detour_sem.at[stream],
-            recv_sem.at[stream, DETOUR + 1, c],
-            device(step, 2 * step),
+            chunk(stream, s, c),
+            chunk(stream, slot, c),
+            detour_sem.at[n],
+            recv_sem.at[stream, slot, c],
+            device(*wrap_target(stream, owner, sender)),
         )
 
     def detour(stream, s, c):
-        @pl.when((s == SPAN - 1) & (j == pick(stream, (RUN - 2, 1))) & (lax.rem(c, 2) == 1))
+        for n, (which, _, sender, slot, waves) in enumerate(DETOURS):
+            place = RUN - sender if which == 0 else sender - 1
+            now = functools.reduce(jnp.logical_or, [c == wave for wave in waves])
+
+            @pl.when((stream == which) & (s == slot) & (j == place) & now)
+            def _():
+                detour_copy(n, c).start()
+
+    for c in range(WAVES):
+        forward(0, 0, c)
+
+        @pl.when(j != 0)
         def _():
-            detour_copy(stream, c).start()
-
-    for c in range(WAVES):
-        for stream in range(2):
-            forward(stream, 0, c)
-        for stream in range(2):
-            wrap(stream, c)
+            forward(1, 0, c)
+
+    wrap_early(0)
+
+    def cross():
+        pl.semaphore_wait(ready_sem, ready_count)
+        for c in range(WAVES):
+
+            @pl.when(j == 0)
+            def _():
+                forward(1, 0, c)
+
+        wrap_early(1)
 
     row = lax.broadcasted_iota(jnp.int32, (128, 128), 0)
     lane = lax.broadcasted_iota(jnp.int32, (128, 128), 1)
@@ -380,10 +996,28 @@
         coef = jnp.concatenate(parts, axis=1).astype(jnp.bfloat16)
         total[mine] += jnp.dot(coef, visitors, preferred_element_type=jnp.float32)
 
+    words = []
+    line = lax.rem(g, LINE)
+    turn_at = 2 * j + lax.div(k, RUN)
+    for i in range(len(ORDER[0])):
+        word = jnp.int32(0)
+        for row in reversed(range(LINE)):
+            entries = [ORDER[row * 2 * RUN + place][i] for place in range(2 * RUN)]
+            entry = jnp.int32(entries[0])
+            for place in range(1, 2 * RUN):
+                if entries[place] != entries[place - 1]:
+                    entry = jnp.where(turn_at >= place, entries[place], entry)
+            word = entry if row == LINE - 1 else jnp.where(line == row, entry, word)
+        words.append(word)
+
     def step(i, carry):
         word = words[0]
         for other in range(1, len(words)):
             word = jnp.where(i == other, words[other], word)
+
+        @pl.when(lax.rem(word, 64) == 1)
+        def _():
+            cross()
 
         for _ in range(4):
             entry = lax.rem(word, 64)
@@ -392,10 +1026,11 @@
             s = lax.rem(lax.div(entry, 4), 8)
             c = lax.rem(entry, 4)
 
-            @pl.when(entry > 0)
+            @pl.when(entry > 1)
             def _():
                 receive(stream, s, c)
                 forward(stream, s, c)
+                wrap_late(stream, s, c)
                 detour(stream, s, c)
 
         @pl.when(word > 0)
@@ -433,26 +1068,31 @@
                     ).wait_send()
 
         far, slot, target = wrap_route(stream)
-        detoured = wrap_distance(stream)[0] == DETOUR
 
         @pl.when(far)
         def _():
             wrap_id_copy(stream).wait_send()
 
-        for cond, amount in ((jnp.logical_not(detoured), rows), (detoured, rows // 2)):
-
-            @pl.when(far & cond)
-            def _():
-                part = hat.at[stream, pl.ds(0, amount)]
-                remote(
-                    part, part, wrap_sem.at[stream], recv_sem.at[stream, slot, 0], target
-                ).wait_send()
-
-        @pl.when(j == (RUN - 2, 1)[stream])
+        for distance in range(2, SLOTS - 1):
+            away = [len(d[4]) for d in DETOURS if d[0] == stream and d[1] == distance]
+            amount = rows - piece * sum(away)
+            if amount:
+
+                @pl.when(wrap_distance(stream)[0] == distance)
+                def _():
+                    part = hat.at[stream, pl.ds(0, amount)]
+                    remote(
+                        part, part, wrap_sem.at[stream], recv_sem.at[stream, slot, 0], target
+                    ).wait_send()
+
+    for n, (stream, _, sender, _, waves) in enumerate(DETOURS):
+
+        @pl.when(j == (RUN - sender if stream == 0 else sender - 1))
         def _():
-            part = hat.at[stream, pl.ds(0, rows // 2)]
+            part = hat.at[stream, pl.ds(0, piece * len(waves))]
+            target = device(0, 1 - 2 * stream)
             remote(
-                part, part, detour_sem.at[stream], recv_sem.at[stream, slot, 0], target
+                part, part, detour_sem.at[n], recv_sem.at[stream, 1, 0], target
             ).wait_send()
 
 
@@ -483,7 +1123,8 @@
             pltpu.SemaphoreType.DMA((2, 2, SLOTS)),
             pltpu.SemaphoreType.DMA((2,)),
             pltpu.SemaphoreType.DMA((2,)),
-            pltpu.SemaphoreType.DMA((2,)),
+            pltpu.SemaphoreType.DMA((max(1, len(DETOURS)),)),
+            pltpu.SemaphoreType.REGULAR,
             pltpu.SemaphoreType.DMA((2, SLOTS, WAVES)),
             pltpu.SemaphoreType.DMA((2, SLOTS)),
         ],

time: 112 us -> 102 us (0.911)
  the two profiles are of different devices: /device:TPU:155 before, /device:TPU:377 now
where the time goes in v3:
time: 102 us; the launch traced here: 101 us
  Pallas kernels  95.3 us (93%)
  local copies, waits for them, and re-layouts  3.47 us (3%)
  between operations  2.58 us (3%)
    pallas_call x1, Pallas kernels, body(): pl.pallas_call(functools.partial(kernel, n_grp, n_blk), out_shape=(jax.Sh...  95.3 us
    unnamed x4, local copies, waits for them, and re-layouts  3.47 us

profile of v3, /device:TPU:377, one launch (start us, length us, event | category | flops | bytes accessed | tf_op | source)
XLA Modules:
  0.0 101.3 jit_solution(1698442985060107266)
XLA Ops:
  2.6 95.3 %shard_map.86 = (f32[256,1152]{1,0:T(8,128)}, f32[256,1152]{1,0:T(8,128)}) custom-call(bf16[256,1152]{1,0:T(8,128)(2,1)} %image_hbm.1, bf16[256,1152]{1,0:T(8,128)(2,1)} %text_hbm.1, s32[2,128]{1,0:T(2,128)} %bitcast.2, s32[2,128]{1,0:T(2,128)} %bitcast.3, f32[1]{0:T(128)S(6)} %copy.11.sharpness, f32[1]{0:T(128)S(6)} %copy.12.offset, f32[1]{0:T(128)S(6)} %copy.13.adjoint), custom_call_target="tpu_custom_call" | custom-call | flops 4831838208 | bytes 3538944 | tf_op jit(solution)/shard_map/pallas_call | solution.py:1105
  97.9 0.0 copy-start
  97.9 2.5 %copy.14 = f32[256,1152]{1,0:T(8,128)} copy(f32[256,1152]{1,0:T(8,128)} %get-tuple-element.4) | data formatting | bytes 2359296
  100.3 0.0 copy-done
  100.3 1.0 copy.15
Async XLA Ops:
  97.9 2.5 %copy-start = (f32[256,1152]{1,0:T(8,128)S(1)}, f32[256,1152]{1,0:T(8,128)}, u32[]{:S(2)}) copy-start(f32[256,1152]{1,0:T(8,128)} %get-tuple-element.5) | copy-start | bytes 3538948

commit v4 on v3

v4 whole, which is shorter than its diff:
```python
import functools

import jax
import jax.numpy as jnp
from jax import lax
from jax.experimental import pallas as pl
from jax.experimental.pallas import tpu as pltpu
from jax.sharding import PartitionSpec as P

MESH = pl.DeviceIdType.MESH
EPSILON = 1e-06

SPAN = 4
SLOTS = 8
LINE = 4
PATIENT = (7, 2)
RUN = 16
WAVES = 4
DETOURS = (
)


ORDER = (
    (
        10639617, 10394406, 11111341, 150994991, 184549376, 218219307, 251761156, 16777216, 1543181, 3791945,
        50331700, 4259418, 15245746, 13452412, 2078645, 16102731, 16381366, 83889623, 167772223, 33554432,
        117440512, 67108864, 201326610, 234881024, 268435456, 100663315, 134217728,
    ),
    (
        10115329, 10910504, 150994989, 184722990, 218106844, 5293675, 251661341, 14789717, 15038358, 3536626,
        15416590, 1293647, 16777224, 167809404, 53022534, 201548487, 33554432, 83890065, 117440512, 67108882,
        235107583, 100663296, 134217728, 268435456, 0, 0, 0,
    ),
    (
        1859908, 9865473, 11430569, 151177692, 184549421, 221368878, 16777216, 2558964, 251907405, 50331678,
        168002870, 14478410, 84137493, 4242617, 8381401, 16725690, 201569371, 33554432, 117440512, 234881024,
        67108864, 268435456, 100664722, 134218967, 0, 0, 0,
    ),
    (
        1859908, 9865473, 11430569, 151177692, 12011037, 184551321, 7269722, 14354384, 218103855, 251658240,
        2346481, 167825272, 16777216, 204969033, 13165834, 65601419, 15725906, 33557718, 83887571, 117440512,
        234881024, 67108864, 100663296, 268435456, 134217728, 0, 0,
    ),
    (
        2380292, 6, 11700481, 10005349, 12229063, 151190155, 184552176, 218103857, 251658240, 13683896,
        16780537, 64544437, 6540795, 168022928, 84141849, 201326592, 240243711, 268435456, 117442449,
        33554432, 67110239, 106509970, 134219227, 0, 0, 0, 0,
    ),
    (
        2380292, 11700481, 11952549, 150995623, 3072489, 184549424, 218299498, 251661483, 7720184, 14020212,
        8351376, 15957716, 167772177, 201326653, 16854924, 234881024, 5070797, 50331662, 268436440, 83886080,
        33554432, 117440512, 67110486, 100663322, 134219227, 0, 0,
    ),
    (
        1859908, 9476616, 41, 9741057, 16779917, 11428747, 50332624, 84067431, 122608914, 151215150,
        184552559, 218312502, 251662199, 168005555, 216614713, 234881024, 268558079, 33554456, 67110485,
        107575190, 134219487, 0, 0, 0, 0, 0, 0,
    ),
    (
        1859908, 2568, 2507521, 2773865, 2943632, 4633574, 16780071, 50331666, 83886080, 117626100, 150994944,
        184549422, 218107248, 251661297, 5491894, 6504311, 167772216, 201330617, 234884757, 268678591,
        33670617, 67110746, 100663326, 134219487, 0, 0, 0,
    ),
    (
        1206628, 11555367, 27145, 1878849, 150998057, 195611531, 13022063, 16777236, 5713422, 6264207,
        218107088, 50405044, 251658293, 83886134, 4947771, 117441789, 167772160, 201326654, 234881087,
        268435456, 33556248, 67110745, 100787930, 134217759, 0, 0, 0,
    ),
    (
        10381668, 516, 11571521, 162834950, 187632199, 3230634, 230480625, 13337493, 16844175, 64175703,
        251731322, 83886080, 6534326, 117440572, 168025555, 201330588, 33554432, 234881087, 268435456,
        74823321, 100663326, 134217759, 0, 0, 0, 0, 0,
    ),
    (
        1859908, 9476616, 41, 2675457, 16777253, 60339114, 10291919, 4934417, 83888984, 129604947, 12778906,
        13092564, 14888789, 150998263, 184553401, 6270934, 218103867, 251658240, 167772160, 201326592,
        234881024, 268435456, 33554460, 67108893, 100663326, 134217759, 0,
    ),
    (
        1859908, 8, 16941825, 10803465, 3737930, 4503978, 50331663, 4819687, 83889452, 117544173, 12668270,
        7302106, 150998833, 14507890, 184549432, 16487859, 218342876, 251662079, 167772160, 201326592,
        33554432, 234881024, 268435456, 67108893, 100663326, 134217759, 0,
    ),
    (
        1206628, 11555367, 11960713, 10779658, 150997899, 11066444, 184549423, 22227662, 4283919, 6003932,
        6268788, 50457937, 8228283, 16217276, 218359001, 84000730, 251658240, 117440512, 33554432, 167772160,
        201326592, 67108864, 234881024, 100663296, 268435456, 134217728, 0,
    ),
    (
        9980260, 11555367, 2648585, 150994989, 12227056, 184549387, 12403498, 13163249, 218103829, 16870926,
        15152143, 251754292, 50572637, 4679228, 83886110, 14495455, 6897497, 117440574, 167776219, 33554432,
        67108864, 201326592, 100663296, 234881024, 134217728, 268435456, 0,
    ),
    (
        1859908, 2411016, 16946020, 61409610, 4518606, 83888870, 117517095, 151180852, 6745427, 12543280,
        184552538, 218103808, 7310834, 251658261, 5885555, 49117050, 67108864, 100663326, 134217759,
        167772220, 201326653, 234881086, 268435519, 0, 0, 0, 0,
    ),
    (
        1859908, 9488904, 16833097, 2794533, 3979662, 50494161, 13708056, 83965549, 12801710, 13067567,
        117648923, 150994944, 5715767, 184549433, 218103808, 6149562, 251662046, 33554432, 67108895,
        100663296, 134217728, 167772220, 201326653, 234881086, 268435519, 0, 0,
    ),
    (
        10381668, 1491460, 163764745, 12227206, 11058247, 184549423, 229428372, 16778069, 251717043, 50332660,
        90133532, 122119709, 6780062, 33554463, 67110547, 100663323, 134217728, 167775804, 201584253,
        234881082, 268439295, 0, 0, 0, 0, 0, 0,
    ),
    (
        10381668, 10521348, 163762757, 2810281, 12890602, 3230447, 184604018, 218103808, 265241494, 16840144,
        7675228, 6367158, 56965111, 83886106, 117440539, 33554432, 67108864, 100663296, 134217728, 167775804,
        201330553, 234885050, 268439547, 0, 0, 0, 0,
    ),
    (
        1859908, 9486888, 26530409, 4252330, 3980006, 50334503, 83987281, 129864878, 163949587, 184549376,
        218217620, 251658240, 33643740, 67110742, 100665239, 134217759, 15965496, 167772213, 217046458,
        234885047, 268435519, 0, 0, 0, 0, 0, 0,
    ),
    (
        1859908, 3180840, 16777257, 3447461, 11314214, 4504014, 4903916, 50334616, 88972335, 7162970,
        150996338, 117440512, 184549427, 218105622, 251658240, 33556311, 67239710, 100663296, 134470968,
        182185589, 201326650, 234881087, 268439287, 0, 0, 0, 0,
    ),
    (
        10381668, 1346308, 151034728, 184552006, 3072647, 218106858, 16779980, 251659092, 50331662, 83887439,
        117442326, 6416215, 7186015, 33554448, 71814196, 115545269, 167772160, 148582227, 16481529, 201326650,
        234881024, 268439547, 0, 0, 0, 0, 0,
    ),
    (
        10381668, 1491460, 150994984, 10773101, 2915210, 184549418, 5419823, 218103821, 16777216, 251659598,
        50331648, 83887503, 117440540, 6415837, 7063135, 12836379, 167772212, 14150777, 201326650, 235105471,
        268664059, 33554448, 67108881, 100663314, 134217747, 0, 0,
    ),
    (
        1859908, 3293736, 16777257, 61397321, 3062154, 4355022, 83886124, 12422061, 117440529, 150994944,
        184549401, 218103834, 251658240, 7984923, 12661919, 33785148, 67323249, 181116758, 15414773,
        100667318, 201330423, 134217728, 234881024, 268435519, 0, 0, 0,
    ),
    (
        1859908, 3293736, 16777257, 3582281, 50334090, 3978155, 83888935, 129862573, 150994969, 184549376,
        218103834, 251658240, 7833371, 12709492, 13086047, 4402934, 4928631, 167772220, 33555731, 67108885,
        201328061, 100663296, 134221719, 234881087, 268435456, 0, 0,
    ),
    (
        10381668, 151161604, 1479213, 184549422, 12497514, 218103814, 251658240, 5288394, 16777228, 50332501,
        83886094, 117440527, 8251228, 4689680, 16065972, 6370800, 16473209, 183082418, 33664499, 201326592,
        67108864, 234885083, 100663296, 134217787, 268435456, 0, 0,
    ),
    (
        10381668, 150997548, 195330349, 11467438, 218104389, 251658240, 2912902, 16777228, 13829005, 50331663,
        91708508, 125775262, 5492211, 167772216, 5837845, 5055997, 201328185, 33556094, 15726266, 67108891,
        234881024, 100663296, 268435456, 134217728, 0, 0, 0,
    ),
    (
        1859908, 10783016, 10013349, 16777225, 11590375, 50335498, 162837518, 83886080, 191091694, 218103855,
        117440537, 251658240, 14757777, 5702964, 167882323, 7282006, 16633495, 201330098, 33554432, 234882931,
        67108864, 100667102, 134221279, 268435456, 0, 0, 0,
    ),
    (
        1859908, 9869608, 10011178, 16779755, 50385532, 84136842, 151057132, 117440512, 184552493, 218106990,
        251915439, 4686899, 167772212, 6812824, 6905428, 215312083, 33670650, 14661494, 234881054, 67108864,
        268435487, 100663296, 134217728, 0, 0, 0, 0,
    ),
    (
        10381668, 10506756, 11049592, 2801222, 3124999, 167988244, 16777228, 13950805, 50334800, 201328014,
        14339215, 84001915, 117440512, 6366685, 5086078, 13479390, 158203886, 33554432, 234881071, 184549376,
        67108864, 100663296, 218103808, 268435456, 134217728, 251658240, 0,
    ),
    (
        10381668, 10915448, 11043132, 15381061, 151175814, 3191293, 12643597, 16777231, 50331648, 89197438,
        13980795, 167772223, 117440540, 7693489, 5204888, 184549426, 12531609, 208270839, 33554459, 218103808,
        234881024, 67108864, 251658240, 268435456, 100663296, 134217728, 0,
    ),
    (
        1859908, 30460168, 10116873, 50332533, 87808458, 14222072, 16450513, 117442066, 167772160, 208082169,
        14625300, 11624410, 11909754, 7812886, 15657623, 150994974, 235010799, 184549376, 33554432, 67108864,
        218103808, 268435456, 100663296, 251658240, 134217728, 0, 0,
    ),
    (
        1859908, 9658164, 10214949, 16777992, 3448231, 15000232, 50331710, 83887051, 117440512, 167775248,
        16753772, 150994985, 12930514, 5584443, 201328237, 184549376, 5974702, 6147034, 218107115, 234881053,
        33554432, 251660187, 268435487, 67108864, 100663296, 134217728, 0,
    ),
    (
        10115329, 10930727, 151186093, 184549679, 218103808, 18264588, 251658240, 2675081, 50363448, 6493451,
        83945268, 13462677, 13956729, 117440541, 15328919, 15595254, 167775740, 33558352, 201326592, 67112849,
        234881024, 100667346, 268435475, 134217728, 0, 0, 0,
    ),
    (
        10115329, 11979303, 150994985, 184549422, 230457642, 251661012, 1412208, 14718741, 7704982, 3240626,
        31935696, 33554432, 4580186, 50332814, 71087303, 83886080, 100667061, 117440512, 134348507, 167775676,
        201326653, 235142654, 268435456, 0, 0, 0, 0,
    ),
    (
        1859908, 9865473, 11446697, 3328456, 150994953, 16777216, 198222701, 50331648, 83934222, 7529999,
        117440528, 218103808, 7019865, 14269405, 267459742, 8338999, 167772221, 201326649, 49013908,
        234881024, 67354581, 268436694, 100663296, 134217751, 0, 0, 0,
    ),
    (
        1859908, 10914049, 11430565, 16826919, 150997784, 2463540, 50331661, 184551085, 7276362, 83887029,
        5855124, 4027118, 230493617, 13180727, 15194104, 117444498, 5242106, 33554491, 251658240, 67108864,
        167772160, 201326592, 100663296, 234881024, 134217728, 268435456, 0,
    ),
    (
        2380292, 6, 11700481, 10934602, 154040711, 184552110, 218103808, 3324912, 251658289, 13426226,
        16780916, 50335054, 83886080, 117662714, 5471964, 4321053, 168028157, 201327999, 234881041, 268435456,
        33555986, 67212502, 100663322, 134219479, 0, 0, 0,
    ),
    (
        20996, 11682369, 10381861, 10791750, 12255943, 150994986, 184552433, 218156203, 251658240, 16989724,
        50386804, 15423417, 83886094, 6516447, 167772220, 215996057, 121749391, 234882367, 268435456,
        33555793, 67108882, 100664534, 134217751, 0, 0, 0, 0,
    ),
    (
        1859908, 2509320, 152233, 11064065, 20755366, 50334187, 83886124, 117440512, 150994944, 184552749,
        218323888, 266007601, 14664818, 5233874, 168005528, 201326649, 234884756, 268439547, 40985945,
        67229146, 100663326, 134219739, 0, 0, 0, 0, 0,
    ),
    (
        1859908, 150024, 10785537, 16779597, 50331648, 4367242, 95220454, 117440551, 155639084, 184549376,
        223042480, 251882607, 13336339, 167775805, 13606812, 217968285, 234964987, 268435480, 33554432,
        67110485, 100771286, 134217755, 0, 0, 0, 0, 0,
    ),
    (
        10381668, 2380292, 27180, 2019969, 150995689, 11209612, 11332557, 184552527, 16780472, 218103865,
        50331648, 84102835, 251658240, 117665108, 173526523, 217935805, 234882524, 268435456, 33555984,
        67213137, 7185618, 100663326, 134217759, 0, 0, 0, 0,
    ),
    (
        10381668, 2380292, 10513153, 10779466, 150995696, 184601514, 11465556, 218104753, 16777231, 50334904,
        251658240, 13583737, 83889530, 117440534, 168021750, 201577975, 234881086, 268435519, 7439440,
        33658066, 67108893, 100787930, 134217759, 0, 0, 0, 0,
    ),
    (
        1859908, 9476616, 3576577, 16779594, 3041934, 50331663, 83888619, 117443884, 150998381, 184549422,
        234032559, 251866993, 14892504, 15438910, 168017881, 201327706, 234881024, 268435456, 7423131,
        33554451, 67110741, 100787670, 134217759, 0, 0, 0, 0,
    ),
    (
        1859908, 2568, 2507521, 9742925, 3041934, 27177999, 62343960, 96660817, 12950518, 117440572,
        150994944, 16223730, 184549402, 4976243, 218363642, 251659515, 167772160, 201326592, 234881024,
        268435456, 33670484, 67229142, 100663326, 134217759, 0, 0, 0,
    ),
    (
        9980260, 11555367, 150997513, 2019974, 197323339, 3611276, 3992303, 16780850, 218107472, 65752273,
        251658293, 83886080, 15715730, 131940188, 184407358, 201326592, 234881024, 268435456, 5895518,
        33554456, 67110487, 100663322, 134217755, 0, 0, 0, 0,
    ),
    (
        9980260, 11555367, 150997513, 12767878, 196655687, 3611276, 5450479, 16777230, 218107407, 50541596,
        15418745, 15848565, 16068342, 251782391, 83886142, 117440512, 167900607, 201326592, 234881024,
        268435479, 33554456, 67108889, 100663322, 134217755, 0, 0, 0,
    ),
    (
        1859908, 26266120, 50500425, 2689701, 83888526, 11334353, 131148583, 12276973, 12545044, 150998101,
        184549376, 218103808, 251887154, 15414713, 183602903, 49661593, 201326592, 67110747, 234881086,
        100663326, 268437503, 134217728, 0, 0, 0, 0, 0,
    ),
    (
        1859908, 26266120, 50500425, 2794533, 2955662, 4881103, 83886124, 122522484, 12778862, 151199124,
        14650521, 184549397, 218107507, 251658240, 15705558, 167772220, 201330522, 234999707, 33554495,
        268435456, 67108893, 100663326, 134217759, 0, 0, 0, 0,
    ),
    (
        10381668, 161516292, 12767813, 2812486, 184549418, 12368967, 223552299, 251659093, 16777216, 4404622,
        50426868, 6772241, 83887286, 117440512, 7187923, 33785660, 167772221, 201328505, 67108864, 100902846,
        234881024, 134221791, 268435515, 0, 0, 0, 0,
    ),
    (
        10381668, 161516292, 12767813, 184738217, 218135178, 11465457, 251710612, 16778069, 13692118,
        13956560, 50332764, 7679384, 5207676, 91215544, 117440512, 33554489, 67108926, 167775902, 201326592,
        100907007, 234881024, 134217728, 268435456, 0, 0, 0, 0,
    ),
    (
        1859908, 3180840, 16777257, 3447461, 3712038, 2955755, 4903916, 50525742, 83886080, 7013971,
        151108692, 7720085, 117441971, 184549399, 218107422, 251661599, 33554432, 67108921, 100663296,
        134217728, 15691445, 167776055, 201326653, 234881086, 268435519, 0, 0,
    ),
    (
        1859908, 3180840, 16777257, 3447461, 50332710, 3046090, 11868942, 88705935, 150994991, 6895216,
        13219121, 13487637, 184550836, 15826525, 15334750, 117444029, 218361339, 251658303, 33554432,
        67108864, 167772160, 100663296, 134217728, 201326592, 234881024, 268435456, 0,
    ),
    (
        10381668, 1491460, 150994984, 2648905, 184552361, 218276551, 16956364, 3756884, 259064790, 50403159,
        83886110, 117442066, 33558303, 7030355, 67110640, 100663296, 134221181, 13332401, 184520179,
        201326649, 234884858, 268435456, 0, 0, 0, 0, 0,
    ),
    (
        10381668, 1491460, 150994984, 2648905, 184552361, 218276551, 5422028, 16777229, 251658240, 3999054,
        50331670, 13829980, 83887228, 117442455, 14095890, 5111672, 33554457, 13344154, 14628606, 167776250,
        67108923, 100663296, 201326592, 134217728, 234881024, 268435456, 0,
    ),
    (
        1859908, 3293736, 16777257, 3582281, 50334090, 10400656, 95491019, 117443501, 151070255, 184550617,
        218105114, 251658240, 7570779, 33557526, 67110743, 100663326, 134422111, 13843642, 168021371,
        201580022, 234881086, 268435519, 0, 0, 0, 0, 0,
    ),
    (
        1859908, 3293736, 16777257, 3582281, 3737994, 3979755, 50517100, 96306350, 12666451, 117444122,
        150994944, 184549376, 7294037, 218219961, 251658240, 15424663, 33554461, 8350942, 67108923, 100663351,
        134217728, 167772220, 201326653, 234881086, 268435519, 0, 0,
    ),
    (
        10381668, 1491460, 150994984, 196514185, 2026122, 218103819, 251710191, 16777236, 50333005, 83886094,
        117654486, 4314588, 15800245, 33629750, 67212511, 100663322, 134220827, 13311485, 167772216,
        201564083, 234885114, 268435515, 0, 0, 0, 0, 0,
    ),
    (
        10381668, 10666500, 150994949, 196776557, 218106502, 251837386, 3228359, 16866356, 56302925, 97059766,
        14480471, 6367027, 117520285, 33554432, 15837145, 67108891, 100663296, 134217728, 167775805,
        201330302, 234884799, 268435515, 0, 0, 0, 0, 0,
    ),
    (
        1859908, 20072968, 3578185, 50375082, 3046094, 83888911, 117541756, 163422062, 184659888, 218103808,
        251658240, 4658896, 13337919, 39437461, 67228887, 8339038, 100663348, 134217728, 167772160, 201330042,
        234884854, 268435511, 0, 0, 0, 0, 0,
    ),
    (
        1859908, 3293736, 16777257, 3582281, 50331686, 11577835, 3071758, 12651407, 155647832, 83886080,
        191358129, 117440512, 218103858, 251659482, 5766356, 33670555, 67340119, 100663326, 134217759,
        167775545, 201330042, 234884539, 268435511, 0, 0, 0, 0,
    ),
    (
        10381668, 2380292, 14723590, 11055593, 16778041, 50332523, 150997818, 97760188, 184553325, 218107822,
        117441492, 5622837, 167772176, 4715933, 12920727, 5110774, 201533016, 258946743, 33554432, 67108864,
        234881024, 100663296, 268435456, 134217728, 0, 0, 0,
    ),
    (
        10381668, 1475076, 11178616, 2798009, 153078586, 196599499, 16778004, 16307566, 5836079, 218104910,
        4191698, 63035155, 251876894, 83886080, 14358489, 117440538, 167775387, 33558003, 67108864, 201326592,
        100663296, 134217728, 234881024, 268435456, 0, 0, 0,
    ),
    (
        1859908, 16777992, 13779785, 50332348, 83887013, 16210315, 117440527, 16476711, 150998572, 180542975,
        184553065, 218344362, 201428048, 5349073, 12408466, 251739307, 234882459, 268553431, 33554461,
        67110878, 100663296, 134217728, 0, 0, 0, 0, 0,
    ),
    (
        1859908, 16777992, 9739556, 64381820, 14200679, 83886094, 151177784, 14603006, 117441551, 4627385,
        184549423, 229213375, 12688122, 251658259, 167772160, 5748372, 214267606, 33676444, 234884318,
        67108895, 100663296, 268435456, 134217728, 0, 0, 0, 0,
    ),
    (
        10115329, 10930727, 151169965, 184549376, 218296588, 16954184, 251658245, 62952340, 3958321, 33761040,
        2838037, 13488601, 83886102, 6913401, 117441246, 14284538, 67110011, 167775740, 201327805, 100663358,
        234882303, 268435456, 134217728, 0, 0, 0, 0,
    ),
    (
        10115329, 11959080, 150994985, 184549422, 218276612, 16970253, 251679659, 50332239, 83930630,
        117486855, 13720688, 5885080, 15160912, 33555549, 7959706, 67108922, 100663296, 8337147, 167773436,
        134221686, 201326592, 234881086, 268439039, 0, 0, 0, 0,
    ),
    (
        1859908, 9865473, 11430569, 28363208, 150994944, 50386441, 5456540, 184549421, 7662617, 13034229,
        83887130, 13301659, 218104822, 33554432, 251885564, 117440512, 15031544, 167776081, 67108922,
        216868286, 234882303, 100663319, 268435456, 134217728, 0, 0, 0,
    ),
    (
        1859908, 10914049, 11430565, 16828872, 150997769, 50334989, 83886986, 117503499, 7443504, 184549421,
        7033969, 38463316, 218105206, 14542255, 67112731, 13187064, 251756157, 100663296, 167772160, 15728318,
        201326643, 134217728, 234881024, 268435456, 0, 0, 0,
    ),
    (
        2380292, 10633601, 2808172, 151165414, 195748551, 218103808, 13024240, 251658252, 16777266, 4251187,
        50331700, 4677212, 99313166, 4963805, 117567247, 168024020, 33555710, 201326655, 234881024, 268435456,
        67110233, 100664730, 134219479, 0, 0, 0, 0,
    ),
    (
        2380292, 11700481, 10250661, 151165770, 12772039, 184549418, 218103808, 13300529, 16777259, 251658240,
        64020019, 84104121, 117441488, 5465914, 4701661, 167772220, 207742333, 6647698, 38663871, 234882775,
        67108864, 268435456, 100663296, 134217728, 0, 0, 0,
    ),
    (
        1859908, 2509320, 41, 26530561, 60466058, 83952587, 117440555, 150997799, 184765265, 4803504,
        218106997, 5729266, 266325212, 183993747, 201330302, 33558168, 234979071, 268435456, 67110493,
        100664990, 134219739, 0, 0, 0, 0, 0, 0,
    ),
    (
        1859908, 150024, 16777985, 60199753, 10134410, 83948240, 117440555, 151176295, 184736820, 230366546,
        12529044, 6540787, 251658296, 168007037, 15308030, 16608988, 201451354, 234881047, 33554459,
        268435487, 67108864, 100663296, 134217728, 0, 0, 0, 0,
    ),
    (
        10381668, 2380292, 44, 151159169, 2915146, 184549417, 12774028, 16777229, 5446635, 218103822,
        50564239, 251659600, 83889465, 117440512, 6503802, 15801750, 167772219, 201578103, 234881086,
        268435519, 5076626, 33554460, 67110747, 100663326, 134217759, 0, 0,
    ),
    (
        10381668, 516, 11571521, 151159430, 11965127, 184549424, 3598988, 16777265, 3865300, 232870898,
        63937808, 265907893, 99454460, 117440573, 167772160, 201330577, 234882879, 268435456, 33554432,
        73258578, 100743066, 134219739, 0, 0, 0, 0, 0,
    ),
    (
        1859908, 9476616, 27579137, 50334026, 11166603, 83887119, 117443303, 162893100, 12774737, 184550996,
        234036214, 251658240, 14651250, 167773852, 5582771, 33554489, 201566079, 67108923, 234881024,
        268435456, 100787603, 134346203, 0, 0, 0, 0, 0,
    ),
    (
        1859908, 8, 16941825, 50479945, 3840330, 11166416, 83886095, 117443051, 151066156, 184552749,
        224877614, 14359508, 251911356, 13446682, 175349687, 201326592, 33558207, 234882427, 268435475,
        67110742, 100665243, 134219735, 0, 0, 0, 0, 0,
    ),
    (
        9980260, 11555367, 150997513, 10932870, 12104176, 184550186, 218307533, 5450446, 24186383, 13844049,
        4806202, 15973725, 14542070, 50331709, 83886080, 251750014, 117440575, 33554432, 167772160, 201326592,
        234881024, 67108864, 268435456, 100664983, 134219487, 0, 0,
    ),
    (
        9980260, 11555367, 150997513, 2019974, 12630953, 13038378, 184603947, 222268558, 4429148, 15415156,
        32314933, 7941942, 5848951, 251658302, 50331711, 83886080, 117440537, 33554432, 167772160, 201326592,
        234881047, 268435456, 67108864, 100663322, 134219487, 0, 0,
    ),
    (
        1859908, 26266120, 4363081, 50331685, 10134410, 95220433, 117443026, 6479148, 150994963, 12668270,
        184771951, 218103857, 6780732, 251751608, 33791229, 167775895, 201326592, 241819579, 67108864,
        100665243, 134217759, 268435519, 0, 0, 0, 0, 0,
    ),
    (
        1859908, 26266120, 50500425, 2795856, 83888526, 11342795, 117440551, 13730988, 150994989, 12663733,
        5348783, 184549425, 218103863, 257281586, 33647865, 15574522, 67108893, 100665243, 167772220,
        201326653, 134221727, 234881024, 268435519, 0, 0, 0, 0,
    ),
    (
        10381668, 161516292, 10932805, 2810288, 184549418, 12893127, 231261483, 14889813, 4408214, 251723351,
        23287569, 50435254, 15324378, 83886135, 117440512, 33554459, 67108864, 100663326, 134467295,
        167772160, 201326653, 234881086, 268435519, 0, 0, 0, 0,
    ),
    (
        10381668, 161516292, 10932805, 2810288, 184549418, 221183047, 251661012, 3494706, 16777267, 50332566,
        7406580, 7675223, 6630808, 83993847, 117440512, 33556379, 67108864, 100663296, 134219768, 183746233,
        201326653, 234881086, 268435519, 0, 0, 0, 0,
    ),
    (
        1859908, 3180840, 16777257, 3447461, 50332710, 10400650, 4113105, 83886125, 151184914, 130128884,
        15947411, 184661297, 16108693, 225916342, 251660183, 33554432, 67108895, 100663296, 134217728,
        182681598, 201326649, 234881082, 268435515, 0, 0, 0, 0,
    ),
    (
        1859908, 3180840, 16777257, 3447461, 50331686, 3847178, 4113127, 83888977, 163392408, 5090329,
        130659633, 5977877, 184549405, 218103831, 251658270, 33554432, 67108895, 100663296, 134217728,
        14146876, 14679486, 167772216, 201326649, 234881082, 268435515, 0, 0,
    ),
    (
        10381668, 1491460, 150994984, 2648905, 184552361, 230859463, 28132143, 3759181, 255684112, 7808785,
        58293842, 84014611, 117440537, 33554458, 67108891, 100663296, 134217786, 16203516, 167772212,
        201326645, 234884542, 268439039, 0, 0, 0, 0, 0,
    ),
    (
        10381668, 1491460, 150994984, 2648905, 184552361, 218276551, 16780236, 50416333, 251658254, 83952597,
        117441948, 6153309, 33555986, 67213267, 100663322, 134217755, 15146544, 15679154, 167775548,
        201330549, 251625398, 268435456, 0, 0, 0, 0, 0,
    ),
    (
        1859908, 3293736, 16777257, 3582281, 50399626, 4618958, 4899787, 84076077, 117440512, 157762799,
        190273172, 218103830, 251658267, 33556247, 67108893, 100663326, 134221215, 15191544, 167772208,
        15675057, 201330547, 234881086, 268435519, 0, 0, 0, 0,
    ),
    (
        1859908, 3293736, 16777257, 3582281, 50334090, 84063246, 11695051, 4909905, 117443544, 150994944,
        191444249, 218103808, 251658240, 40986325, 67110743, 100663326, 134217759, 14642548, 13093944,
        167772217, 16203442, 201326651, 234881086, 268435519, 0, 0, 0,
    ),
    (
        10381668, 1491460, 150994984, 10775369, 184722094, 11471815, 218103819, 251658260, 16866380, 50331661,
        83886998, 4519376, 117517468, 7818451, 33554456, 13999646, 74315452, 167772214, 100666877, 134217728,
        201564158, 234881082, 268435515, 0, 0, 0, 0,
    ),
    (
        10381668, 161516292, 10932805, 184593286, 11317738, 218103855, 251658252, 16778509, 50331648,
        83887438, 117556623, 33555984, 4838487, 5085104, 67108913, 100791986, 134219507, 168005428, 15167349,
        201326647, 234884798, 268439295, 0, 0, 0, 0, 0,
    ),
    (
        1859908, 3293736, 16777257, 3582281, 50373670, 94286926, 4180747, 150994962, 12311384, 117440537,
        191622099, 218103808, 251658303, 5854932, 7554544, 33558065, 167772189, 8363166, 67108915, 100663296,
        134217786, 201330043, 234881078, 268435511, 0, 0, 0,
    ),
    (
        1859908, 10783016, 16777228, 3447461, 50331686, 95318922, 133350347, 150994989, 16059288, 4912217,
        16594622, 184551188, 218103808, 251659611, 33554432, 67204950, 100663326, 134220831, 167775544,
        14102129, 201326643, 234884538, 268439035, 0, 0, 0, 0,
    ),
    (
        10381668, 2380292, 1743416, 11315897, 15532538, 16237265, 12660628, 13815756, 11887445, 6110542,
        16777231, 158820142, 12946398, 167775711, 50333337, 184552603, 83886080, 117440512, 218103808,
        251658291, 33554432, 201326592, 67108864, 100663296, 134217728, 234881024, 268435456,
    ),
    (
        10381668, 14844420, 1741381, 2069162, 32033483, 55821179, 11796413, 150996302, 83886080, 123278288,
        6215472, 7941405, 184549422, 167773715, 12539487, 218103857, 33554432, 80330138, 251658240, 201330163,
        100663296, 134217728, 234881024, 268435456, 0, 0, 0,
    ),
    (
        1859908, 16777992, 9503348, 4704589, 50375093, 10282173, 83967926, 16597751, 4113784, 117440569,
        15654552, 151193000, 167772160, 13036121, 184549402, 6225066, 201326619, 218103808, 234884331,
        251658268, 268435456, 33556381, 67108895, 100663296, 134217728, 0, 0,
    ),
    (
        1859908, 20138248, 10002213, 2874701, 50334158, 100201206, 117440512, 16584247, 6526060, 12041874,
        150997523, 10831470, 197326485, 11364074, 167772209, 231331607, 251658270, 201329887, 33554432,
        67108864, 234881024, 100663296, 134217728, 268435456, 0, 0, 0,
    ),
    (
        10115329, 10910504, 162106285, 184549376, 218105612, 6746960, 33555729, 251747037, 1142042, 67108894,
        8238581, 16777224, 1543222, 50334793, 100666962, 2847154, 1913786, 99414771, 134217788, 117440573,
        167772160, 201326654, 234881024, 268435519, 0, 0, 0,
    ),
    (
        10115329, 11959080, 150997929, 184549376, 224414348, 20219695, 251763406, 7816197, 2557199, 33557621,
        50538118, 14366602, 14766545, 4945611, 84120991, 67347671, 117444348, 100663357, 134217728, 167772222,
        201326592, 234881024, 268435519, 0, 0, 0, 0,
    ),
    (
        1859908, 9865473, 7498409, 10343723, 12764693, 150995993, 35854234, 3275611, 184552754, 16777216,
        218103854, 62709065, 267611350, 14488458, 14930647, 83887247, 82568441, 167772160, 117440571,
        100663296, 201326655, 134217728, 234881024, 268435456, 0, 0, 0,
    ),
    (
        1859908, 10914049, 11430565, 27051784, 150994988, 5282845, 188058733, 50331648, 12124830, 33554482,
        218107150, 2989269, 8190965, 90924433, 14532156, 251892887, 117440512, 67362451, 167772160, 100667323,
        134217728, 201326592, 234881024, 268435519, 0, 0, 0,
    ),
    (
        2380292, 6, 11700481, 11966794, 3045767, 150994990, 184549376, 218103850, 251661039, 12698648,
        8095577, 38061361, 16780447, 13688018, 50331705, 87774426, 7300474, 67108879, 117444054, 100663296,
        150454039, 167772222, 201326655, 234881024, 268435456, 0, 0,
    ),
    (
        2380292, 10668289, 10379685, 150994989, 3052167, 184549422, 218106858, 16779980, 251658240, 3609648,
        50331672, 3742876, 97603123, 4035765, 33676729, 123025079, 67112606, 107988950, 167772160, 134221655,
        201326592, 234885051, 268435519, 0, 0, 0, 0,
    ),
    (
        1859908, 2509320, 3459649, 3842725, 4088528, 16779985, 50331687, 83887276, 117440512, 150994944,
        184549421, 223169436, 251854109, 39935868, 12677118, 6155381, 8232118, 67108915, 7306778, 100663353,
        167772218, 134217787, 201326592, 234881024, 268435456, 0, 0,
    ),
    (
        1859908, 2568, 9474817, 2773865, 16779920, 50331648, 10032011, 83888847, 117440512, 151176359,
        184549421, 218103854, 267466031, 13721436, 13107120, 33554456, 13462898, 6679965, 67108887, 167772216,
        100793946, 201326592, 134458843, 234881083, 268435456, 0, 0,
    ),
    (
        10381668, 2380292, 161508097, 10793418, 184549421, 218155946, 28243213, 3999054, 65367600, 251658240,
        83957306, 117442044, 7446269, 33809585, 13214975, 175590619, 67108917, 201330078, 100663296,
        234884575, 134217728, 268435456, 0, 0, 0, 0, 0,
    ),
    (
        10381668, 20996, 10525441, 150994950, 186553005, 218278795, 16971020, 50509133, 5836302, 251661327,
        83886137, 117538456, 4961404, 16358525, 41100543, 167775514, 214816501, 67108864, 234882998,
        100663351, 268435487, 134217728, 0, 0, 0, 0, 0,
    ),
    (
        1859908, 2568, 9486913, 16777229, 50501962, 10134542, 83887051, 6363627, 117440556, 150998317,
        198632729, 218298002, 251662134, 40984125, 15197403, 7843831, 67110331, 100665239, 134220831,
        167772209, 201326592, 234881074, 268435507, 0, 0, 0, 0,
    ),
    (
        1859908, 8, 9488897, 16777225, 2689613, 50331685, 2955918, 84063206, 123913383, 151209581, 184549422,
        6901103, 218328851, 251658240, 49659420, 16489941, 7863958, 67108923, 167898135, 100663345, 201326592,
        234883058, 134217728, 268435507, 0, 0, 0,
    ),
    (
        9980260, 11555367, 150997513, 195482246, 12772039, 218104618, 11326767, 16777265, 50331648, 4258958,
        7411064, 265389945, 6005918, 83889523, 6634939, 117440572, 49641463, 67108864, 167772222, 201328319,
        234881024, 268435456, 100663323, 134217728, 0, 0, 0,
    ),
    (
        9980260, 11555367, 11960713, 12751306, 150997899, 12372628, 3585393, 14771122, 184550352, 7838940,
        218103860, 14132753, 14231447, 22005755, 251659895, 50587325, 83886080, 117440575, 33554459,
        167772160, 67108864, 201326592, 100663296, 234881024, 268435456, 134217728, 0,
    ),
    (
        1859908, 26266120, 4363081, 50331685, 10134410, 83886097, 10400715, 13732626, 14083309, 12777044,
        117440533, 163958582, 6909815, 184553010, 7812606, 7319545, 218103867, 251658240, 33554432, 167772160,
        67108894, 201326592, 234881024, 268435487, 100663296, 134217728, 0,
    ),
    (
        1859908, 2411016, 21140324, 3844426, 4088907, 10323115, 50331692, 5168409, 12801710, 13069268,
        13223292, 16105015, 84098966, 15326807, 117440575, 150998750, 184549376, 218103808, 251658240,
        33554432, 167772191, 201326592, 67108864, 234881024, 100663296, 268435456, 134217728,
    ),
    (
        10381668, 161516292, 10932805, 2820998, 184549418, 13038279, 218106580, 257395852, 5979725, 13726734,
        7410682, 4961845, 15951453, 8091283, 16779005, 50331710, 83890143, 117440512, 33554432, 67108864,
        167772160, 100663296, 201326592, 234881024, 134217728, 268435456, 0,
    ),
    (
        10381668, 1346308, 151179880, 12626502, 11055598, 184549423, 221426993, 266394773, 16837846, 4146233,
        4572666, 6368605, 14262046, 50332923, 16121306, 83890075, 117440575, 33554432, 167772160, 67108864,
        100663296, 201326592, 134217728, 234881024, 268435456, 0, 0,
    ),
    (
        1859908, 3180840, 16777257, 3447461, 50334096, 10400650, 87999185, 12011026, 151185013, 12690671,
        12956982, 14886263, 117441948, 6264691, 184549436, 226483870, 251662267, 33554495, 67108864,
        167772160, 100663296, 201326592, 134217728, 234881024, 268435456, 0, 0,
    ),
    (
        1859908, 3293736, 16777257, 11065673, 10019472, 50331691, 3979729, 83886124, 117440512, 164811928,
        184552345, 12518645, 218107290, 264617748, 16199189, 16369079, 15062515, 168011711, 33556475,
        67108864, 201326592, 100663296, 234881024, 268435456, 134217728, 0, 0,
    ),
    (
        10381668, 1491460, 150994984, 2648905, 184740905, 12890602, 223523631, 3759245, 20919696, 251660049,
        64059218, 14898398, 83886104, 124217337, 7306906, 33554491, 67108864, 100663296, 134217728, 167772220,
        201326653, 234881086, 268435519, 0, 0, 0, 0,
    ),
    (
        10381668, 1346308, 151034728, 184552006, 12771975, 13040267, 218281228, 3756914, 16777232, 13434390,
        4673116, 4838906, 6418165, 6681846, 251659959, 50335515, 83886080, 117440512, 33554493, 67108864,
        100663358, 134217791, 167772160, 201326592, 234881024, 268435456, 0,
    ),
    (
        1859908, 3293736, 16777257, 3582281, 50399626, 10296014, 4899787, 83886125, 117443480, 151098607,
        184551060, 218105200, 258938292, 41100789, 67231155, 100666846, 134217759, 15707768, 167772220,
        201326653, 234881086, 268435519, 0, 0, 0, 0, 0,
    ),
    (
        1859908, 3293736, 16777257, 11065673, 61760144, 4518795, 83888935, 129600338, 150994944, 6767855,
        12692820, 184549430, 218330481, 251751579, 33764828, 67108893, 100665272, 134217759, 183746233,
        201326653, 234881086, 268435519, 0, 0, 0, 0, 0,
    ),
    (
        10381668, 151161604, 1481544, 184722030, 218280367, 251658250, 5440199, 5710641, 5977101, 16778129,
        7414743, 50451700, 83886080, 117440536, 7034462, 33668511, 67108919, 100663296, 134217728, 167775804,
        201330301, 235142846, 268435515, 0, 0, 0, 0,
    ),
    (
        10381668, 161513772, 2382445, 184552110, 2821062, 218103851, 251658240, 13152753, 20005939, 55104849,
        87770515, 117441495, 6412085, 33554486, 67214814, 100894682, 134217755, 167772220, 201330553,
        235122686, 268435515, 0, 0, 0, 0, 0, 0,
    ),
    (
        1859908, 10783016, 4246181, 4633190, 11782605, 3920530, 16777261, 50335627, 150998991, 84076051,
        184549376, 117440512, 218103808, 251659887, 12670612, 7435675, 33554481, 13495453, 67108895,
        100663296, 134217728, 167775544, 201330041, 235126202, 268435511, 0, 0,
    ),
    (
        1859908, 2267432, 16778021, 4233642, 50334413, 11579175, 150994958, 11842685, 83886095, 5319614,
        184549400, 117440512, 5586927, 224331161, 251658266, 13575921, 33554460, 67110772, 100663326,
        134217759, 167772216, 201330293, 235106042, 268435511, 0, 0, 0,
    ),
    (
        10381668, 10715652, 15706745, 2607749, 2649963, 16547756, 150994955, 16778004, 50332501, 83944470,
        129299921, 184551186, 33653981, 67299225, 13760176, 232193115, 100663296, 167772160, 134221234,
        251658240, 201329911, 234881024, 268435456, 0, 0, 0, 0,
    ),
    (
        10381668, 10522116, 1550969, 11516553, 16035590, 16544830, 3228369, 16780332, 150995797, 50331648,
        83944598, 184612333, 5098776, 12180569, 117440538, 180219227, 33557919, 67108914, 218107127,
        201326592, 100663296, 251658240, 134217728, 234881024, 268435456, 0, 0,
    ),
    (
        1859908, 20073736, 16146229, 4423606, 2619793, 15105554, 2861581, 50335438, 83948268, 150994968,
        117440512, 12138093, 197039386, 6121173, 218105642, 33557533, 67288158, 167775391, 100663347,
        201326592, 251658240, 134217728, 234881024, 268435456, 0, 0, 0,
    ),
    (
        1859908, 3293748, 16780668, 10186597, 16309705, 50331687, 14987256, 99421838, 4764945, 10550037,
        117442067, 150994944, 5876313, 184549421, 167775259, 11199964, 33554461, 230550257, 67108864,
        201329823, 100663296, 251658240, 134217779, 234881024, 268435456, 0, 0,
    ),
)


def kernel(
    n_grp,
    n_blk,
    image_hbm,
    text_hbm,
    image_ids,
    text_ids,
    sharpness,
    offset,
    adjoint,
    grad_image,
    grad_text,
    raw,
    hat,
    buf,
    ids,
    own_ids,
    inverse,
    total,
    load_sem,
    send_sem,
    id_send_sem,
    wrap_sem,
    wrap_id_sem,
    detour_sem,
    ready_sem,
    recv_sem,
    id_recv_sem,
):
    rows = hat.shape[1]
    piece = rows // WAVES
    g = lax.axis_index("grp")
    k = lax.axis_index("blk")
    j = lax.rem(k, RUN)

    loads = [
        pltpu.make_async_copy(text_hbm, raw.at[0], load_sem.at[0]),
        pltpu.make_async_copy(image_hbm, raw.at[1], load_sem.at[1]),
    ]
    for load in loads:
        load.start()

    def device(dg, dk):
        return (lax.rem(g + dg + n_grp, n_grp), lax.rem(k + dk + n_blk, n_blk))

    next_grp = [device(step, 0)[0] for step in (1, -1)]
    next_blk = [device(0, step)[1] for step in (1, -1)]

    barrier = pltpu.get_barrier_semaphore()

    def greet(target):
        pl.semaphore_signal(barrier, inc=1, device_id=target, device_id_type=MESH)

    for target in (device(0, -1), device(1, 0), device(-1, 0)):
        greet(target)

    @pl.when(j != RUN - 1)
    def _():
        greet(device(0, 1))

    even = lax.rem(j, 2) == 0

    @pl.when(even & (j >= 2))
    def _():
        greet(device(0, -2))

    @pl.when(jnp.logical_not(even) & (j <= RUN - 3))
    def _():
        greet(device(0, 2))

    def wrap_target(stream, owner, sender):
        step = 1 - 2 * stream
        return (0 if owner < SPAN else step, step * sender)

    def wrap_links(stream):
        links = [(distance, distance) for distance in range(1, SLOTS - 1)]
        links += [(owner, sender) for which, owner, sender, _, _ in DETOURS if which == stream]
        return sorted({(wrap_target(stream, *link), link[1]) for link in links})

    def others(stream):
        return [link for link in wrap_links(stream) if link[0] != (0, 1 - 2 * stream)]

    @pl.when(j == 0)
    def _():
        for (dg, dk), _ in others(0):
            greet(device(-dg, -dk))

    far_sends = sum([(RUN - j == sender).astype(jnp.int32) for _, sender in others(0)])
    far_sends += jnp.where(j == RUN - 1, len(others(1)), 0) - jnp.where(j == 0, 1, 0)
    ready_count = sum([(j + 1 == sender).astype(jnp.int32) for _, sender in wrap_links(1)])
    for (dg, dk), sender in others(1):

        @pl.when(j + 1 == sender)
        def _():
            greet(device(dg, dk))

    def wrap_distance(stream):
        to_edge = RUN - j if stream == 0 else j + 1
        return to_edge, (to_edge >= 2) & (to_edge <= 6)

    skips = jnp.where(even, j != RUN - 2, j != 1).astype(jnp.int32)
    barrier_count = 4 + skips + far_sends

    @pl.when(j == RUN - 1)
    def _():
        pl.semaphore_wait(barrier, barrier_count)
        for (dg, dk), _ in wrap_links(1):
            pl.semaphore_signal(
                ready_sem, inc=1, device_id=device(-dg, -dk), device_id_type=MESH
            )

    for stream, own in ((0, text_ids), (1, image_ids)):
        loads[stream].wait()
        for c in range(WAVES):
            part = pl.ds(c * piece, piece)
            wide = raw[stream, part, :].astype(jnp.float32)
            inv = lax.rsqrt(jnp.sum(wide * wide, axis=-1, keepdims=True) + EPSILON)
            inverse[stream, part, :] = jnp.broadcast_to(inv, (piece, 128))
            unit = (wide * inv).astype(jnp.bfloat16)
            hat[stream, part, :] = unit
            buf[stream, c, pl.ds(0, piece), :] = unit
            at = c * piece
            line = own[at // 128 : at // 128 + 1, :].astype(jnp.float32)
            line = line[:, at % 128 : at % 128 + piece]
            ids[stream, 0, c] = jnp.concatenate([line] * (128 // piece), axis=1)

    @pl.when(j != RUN - 1)
    def _():
        pl.semaphore_wait(barrier, barrier_count)

    def pick(stream, pair):
        return pair[stream] if isinstance(stream, int) else jnp.where(stream == 0, pair[0], pair[1])

    def route(stream, s, reach):
        place = pick(stream, (j, RUN - 1 - j))
        entry = lax.rem(place, 2) == 0
        fresh = (s == 0) | (s == SPAN)
        if reach == 2:
            goes = entry & (place != RUN - 2) & (fresh | (s == 1) | (s == SPAN + 1))
            return (g, pick(stream, [device(0, step)[1] for step in (2, -2)])), goes
        hop = s == SPAN - 1
        target = (
            jnp.where(hop, pick(stream, next_grp), g),
            jnp.where(hop, k, pick(stream, next_blk)),
        )
        goes = jnp.where(place == RUN - 1, s == 0, entry | fresh)
        return target, (s < SLOTS - 1) & (hop | goes)

    def chunk(stream, s, c):
        at = s * piece
        if not isinstance(at, int):
            at = pl.multiple_of(at, piece)
        return buf.at[stream, c, pl.ds(at, piece)]

    def remote(src, dst, send, recv, target):
        return pltpu.make_async_remote_copy(
            src_ref=src,
            dst_ref=dst,
            send_sem=send,
            recv_sem=recv,
            device_id=target,
            device_id_type=MESH,
        )

    def block_copy(stream, s, c, reach, target):
        return remote(
            chunk(stream, s, c),
            chunk(stream, s + reach, c),
            send_sem.at[reach - 1, stream, s],
            recv_sem.at[stream, s + reach, c],
            target,
        )

    def id_copy(stream, s, reach, target):
        return remote(
            ids.at[stream, s],
            ids.at[stream, s + reach],
            id_send_sem.at[reach - 1, stream, s],
            id_recv_sem.at[stream, s + reach],
            target,
        )

    def forward(stream, s, c):
        for reach in (2, 1):
            target, goes = route(stream, s, reach)

            @pl.when(goes)
            def _():
                @pl.when(c == 0)
                def _():
                    id_copy(stream, s, reach, target).start()

                block_copy(stream, s, c, reach, target).start()

    def receive(stream, s, c):
        target = (g, pick(stream, next_blk))

        @pl.when(c == 0)
        def _():
            id_copy(stream, s - 1, 1, target).wait_recv()

        block_copy(stream, s - 1, c, 1, target).wait_recv()

    def wrap_route(stream):
        to_edge, far = wrap_distance(stream)
        same = to_edge < SPAN
        slot = jnp.where(same, to_edge, to_edge + 1)
        step = 1 - 2 * stream
        return far, slot, device(jnp.where(same, 0, step), step * to_edge)

    def wrap_id_copy(stream):
        _, slot, target = wrap_route(stream)
        return remote(
            ids.at[stream, 0],
            ids.at[stream, slot],
            wrap_id_sem.at[stream],
            id_recv_sem.at[stream, slot],
            target,
        )

    def wrap(stream, c, far):
        _, slot, target = wrap_route(stream)

        @pl.when(far)
        def _():
            remote(
                chunk(stream, 0, c),
                chunk(stream, slot, c),
                wrap_sem.at[stream],
                recv_sem.at[stream, slot, c],
                target,
            ).start()

    def wrap_early(stream):
        to_edge, far = wrap_distance(stream)

        @pl.when(far)
        def _():
            wrap_id_copy(stream).start()

        for c in range(WAVES):
            now = far & (to_edge < PATIENT[stream])
            for which, owner, _, _, waves in DETOURS:
                if which == stream and c in waves:
                    now = now & (to_edge != owner)
            wrap(stream, c, now)

    def wrap_late(other, s, c):
        for stream in range(2):
            to_edge, far = wrap_distance(stream)
            now = far & (to_edge >= PATIENT[stream]) & (other == 1 - stream) & (s == SPAN - 1)
            for which, owner, _, _, waves in DETOURS:
                if which == stream:
                    kept = functools.reduce(jnp.logical_and, [c != wave for wave in waves])
                    now = now & ((to_edge != owner) | kept)
            wrap(stream, c, now)

    def detour_copy(n, c):
        stream, owner, sender, s, _ = DETOURS[n]
        slot = owner if owner < SPAN else owner + 1
        return remote(
            chunk(stream, s, c),
            chunk(stream, slot, c),
            detour_sem.at[n],
            recv_sem.at[stream, slot, c],
            device(*wrap_target(stream, owner, sender)),
        )

    def detour(stream, s, c):
        for n, (which, _, sender, slot, waves) in enumerate(DETOURS):
            place = RUN - sender if which == 0 else sender - 1
            now = functools.reduce(jnp.logical_or, [c == wave for wave in waves])

            @pl.when((stream == which) & (s == slot) & (j == place) & now)
            def _():
                detour_copy(n, c).start()

    for c in range(WAVES):
        forward(0, 0, c)

        @pl.when(j != 0)
        def _():
            forward(1, 0, c)

    wrap_early(0)

    def cross():
        pl.semaphore_wait(ready_sem, ready_count)
        for c in range(WAVES):

            @pl.when(j == 0)
            def _():
                forward(1, 0, c)

        wrap_early(1)

    row = lax.broadcasted_iota(jnp.int32, (128, 128), 0)
    lane = lax.broadcasted_iota(jnp.int32, (128, 128), 1)
    for stream, own in ((0, text_ids), (1, image_ids)):
        for half in range(rows // 128):
            line = jnp.broadcast_to(own[half : half + 1, :].astype(jnp.float32), (128, 128))
            column = jnp.sum(jnp.where(row == lane, line, 0.0), axis=-1, keepdims=True)
            own_ids[stream, pl.ds(half * 128, 128), :] = jnp.broadcast_to(column, (128, 128))
        total[stream] = jnp.zeros(total.shape[1:], jnp.float32)

    scale = jnp.exp(jnp.full((1, 128), sharpness[0], jnp.float32))[:, :1]
    shift = offset[0]
    weight = -(adjoint[0] * scale / rows)
    group = SPAN * piece
    turn = lax.broadcasted_iota(jnp.int32, (1, 128), 1) // piece

    def compute(stream, c, half):
        mine = 1 - stream
        visitors = buf[stream, c, pl.ds(pl.multiple_of(half * group, group), group), :]
        grid = lax.dot_general(
            hat[mine], visitors, (((1,), (1,)), ((), ())), preferred_element_type=jnp.float32
        )
        logit = scale * grid + shift
        column = own_ids[mine, :, :]
        parts = []
        for at in range(0, group, 128):
            s = half * SPAN + at // piece
            line = ids[stream, s, c]
            for other in range(1, 128 // piece):
                line = jnp.where(turn == other, ids[stream, s + other, c], line)
            match = column == jnp.broadcast_to(line, (rows, 128))
            here = logit[:, at : at + 128]
            signed = jnp.where(match, here, -here)
            parts.append(jnp.where(match, weight, -weight) * (1.0 / (1.0 + jnp.exp(signed))))
        coef = jnp.concatenate(parts, axis=1).astype(jnp.bfloat16)
        total[mine] += jnp.dot(coef, visitors, preferred_element_type=jnp.float32)

    words = []
    line = lax.rem(g, LINE)
    turn_at = 2 * j + lax.div(k, RUN)
    for i in range(len(ORDER[0])):
        word = jnp.int32(0)
        for row in reversed(range(LINE)):
            entries = [ORDER[row * 2 * RUN + place][i] for place in range(2 * RUN)]
            entry = jnp.int32(entries[0])
            for place in range(1, 2 * RUN):
                if entries[place] != entries[place - 1]:
                    entry = jnp.where(turn_at >= place, entries[place], entry)
            word = entry if row == LINE - 1 else jnp.where(line == row, entry, word)
        words.append(word)

    def step(i, carry):
        word = words[0]
        for other in range(1, len(words)):
            word = jnp.where(i == other, words[other], word)

        @pl.when(lax.rem(word, 64) == 1)
        def _():
            cross()

        for _ in range(4):
            entry = lax.rem(word, 64)
            word = lax.div(word, 64)
            stream = lax.div(entry, 32)
            s = lax.rem(lax.div(entry, 4), 8)
            c = lax.rem(entry, 4)

            @pl.when(entry > 1)
            def _():
                receive(stream, s, c)
                forward(stream, s, c)
                wrap_late(stream, s, c)
                detour(stream, s, c)

        @pl.when(word > 0)
        def _():
            product = word - 1
            compute(lax.div(product, 8), lax.div(lax.rem(product, 8), 2), lax.rem(product, 2))

        return carry

    lax.fori_loop(0, len(words), step, 0)

    for stream, out in ((1, grad_image), (0, grad_text)):
        for c in range(WAVES):
            part = pl.ds(c * piece, piece)
            inv = inverse[stream, part, :][:, :1]
            unit = raw[stream, part, :].astype(jnp.float32) * inv
            grad = total[stream, part, :]
            along = jnp.sum(unit * grad, axis=-1, keepdims=True)
            out[part, :] = inv * (grad - unit * along)

    for stream in range(2):
        for s in range(SLOTS - 1):
            for reach in (2, 1):
                target, goes = route(stream, s, reach)

                @pl.when(goes)
                def _():
                    id_copy(stream, s, reach, target).wait_send()
                    remote(
                        hat.at[stream],
                        hat.at[stream],
                        send_sem.at[reach - 1, stream, s],
                        recv_sem.at[stream, s + 1, 0],
                        target,
                    ).wait_send()

        far, slot, target = wrap_route(stream)

        @pl.when(far)
        def _():
            wrap_id_copy(stream).wait_send()

        for distance in range(2, SLOTS - 1):
            away = [len(d[4]) for d in DETOURS if d[0] == stream and d[1] == distance]
            amount = rows - piece * sum(away)
            if amount:

                @pl.when(wrap_distance(stream)[0] == distance)
                def _():
                    part = hat.at[stream, pl.ds(0, amount)]
                    remote(
                        part, part, wrap_sem.at[stream], recv_sem.at[stream, slot, 0], target
                    ).wait_send()

    for n, (stream, _, sender, _, waves) in enumerate(DETOURS):

        @pl.when(j == (RUN - sender if stream == 0 else sender - 1))
        def _():
            part = hat.at[stream, pl.ds(0, piece * len(waves))]
            target = device(0, 1 - 2 * stream)
            remote(
                part, part, detour_sem.at[n], recv_sem.at[stream, 1, 0], target
            ).wait_send()


def body(n_grp, n_blk, image_emb, text_emb, image_pair_index, text_ids, sharpness, offset, adjoint):
    rows, width = image_emb.shape
    vmem = pl.BlockSpec(memory_space=pltpu.VMEM)
    smem = pl.BlockSpec(memory_space=pltpu.SMEM)
    hbm = pl.BlockSpec(memory_space=pltpu.HBM)
    flops = 4 * SLOTS * 2 * rows * rows * width
    return pl.pallas_call(
        functools.partial(kernel, n_grp, n_blk),
        out_shape=(
            jax.ShapeDtypeStruct((rows, width), jnp.float32),
            jax.ShapeDtypeStruct((rows, width), jnp.float32),
        ),
        in_specs=[hbm, hbm, vmem, vmem, smem, smem, smem],
        out_specs=(vmem, vmem),
        scratch_shapes=[
            pltpu.VMEM((2, rows, width), jnp.bfloat16),
            pltpu.VMEM((2, rows, width), jnp.bfloat16),
            pltpu.VMEM((2, WAVES, SLOTS * rows // WAVES, width), jnp.bfloat16),
            pltpu.VMEM((2, SLOTS, WAVES, 1, 128), jnp.float32),
            pltpu.VMEM((2, rows, 128), jnp.float32),
            pltpu.VMEM((2, rows, 128), jnp.float32),
            pltpu.VMEM((2, rows, width), jnp.float32),
            pltpu.SemaphoreType.DMA((2,)),
            pltpu.SemaphoreType.DMA((2, 2, SLOTS)),
            pltpu.SemaphoreType.DMA((2, 2, SLOTS)),
            pltpu.SemaphoreType.DMA((2,)),
            pltpu.SemaphoreType.DMA((2,)),
            pltpu.SemaphoreType.DMA((max(1, len(DETOURS)),)),
            pltpu.SemaphoreType.REGULAR,
            pltpu.SemaphoreType.DMA((2, SLOTS, WAVES)),
            pltpu.SemaphoreType.DMA((2, SLOTS)),
        ],
        compiler_params=pltpu.CompilerParams(
            collective_id=0, has_side_effects=True, vmem_limit_bytes=60 * 1024 * 1024
        ),
        cost_estimate=pl.CostEstimate(
            flops=flops, bytes_accessed=12 * rows * width, transcendentals=2 * SLOTS * rows * rows
        ),
    )(
        image_emb,
        text_emb,
        image_pair_index.reshape(rows // 128, 128),
        text_ids.reshape(rows // 128, 128),
        sharpness,
        offset,
        adjoint,
    )


def solution(mesh):
    both = ("grp", "blk")
    return jax.shard_map(
        functools.partial(body, mesh.shape["grp"], mesh.shape["blk"]),
        mesh=mesh,
        in_specs=(P(both, None), P(both, None), P(both), P(both), P(), P(), P()),
        out_specs=(P(both, None), P(both, None)),
        check_vma=False,
    )
```

time: 102 us -> 100 us (0.980)
  the two profiles are of different devices: /device:TPU:377 before, /device:TPU:349 now
where the time goes in v4:
time: 100 us
  Pallas kernels  94.2 us (94%)
  local copies, waits for them, and re-layouts  3.47 us (3%)
  between operations  2.58 us (3%)
    pallas_call x1, Pallas kernels, body(): pl.pallas_call(functools.partial(kernel, n_grp, n_blk), out_shape=(jax.Sh...  94.2 us
    unnamed x4, local copies, waits for them, and re-layouts  3.47 us

profile of v4, /device:TPU:349, one launch (start us, length us, event | category | flops | bytes accessed | tf_op | source)
XLA Modules:
  0.0 100.2 jit_solution(15069572080470012532)
XLA Ops:
  2.6 94.2 %shard_map.86 = (f32[256,1152]{1,0:T(8,128)}, f32[256,1152]{1,0:T(8,128)}) custom-call(bf16[256,1152]{1,0:T(8,128)(2,1)} %image_hbm.1, bf16[256,1152]{1,0:T(8,128)(2,1)} %text_hbm.1, s32[2,128]{1,0:T(2,128)} %bitcast.2, s32[2,128]{1,0:T(2,128)} %bitcast.3, f32[1]{0:T(128)S(6)} %copy.11.sharpness, f32[1]{0:T(128)S(6)} %copy.12.offset, f32[1]{0:T(128)S(6)} %copy.13.adjoint), custom_call_target="tpu_custom_call" | custom-call | flops 4831838208 | bytes 3538944 | tf_op jit(solution)/shard_map/pallas_call | solution.py:1105
  96.8 0.0 copy-start
  96.8 2.5 %copy.14 = f32[256,1152]{1,0:T(8,128)} copy(f32[256,1152]{1,0:T(8,128)} %get-tuple-element.4) | data formatting | bytes 2359296
  99.2 0.0 copy-done
  99.2 1.0 %copy.15 = f32[256,1152]{1,0:T(8,128)} copy(f32[256,1152]{1,0:T(8,128)S(1)} %copy-done) | data formatting | bytes 2359296
Async XLA Ops:
  96.8 2.5 %copy-start = (f32[256,1152]{1,0:T(8,128)S(1)}, f32[256,1152]{1,0:T(8,128)}, u32[]{:S(2)}) copy-start(f32[256,1152]{1,0:T(8,128)} %get-tuple-element.5) | copy-start | bytes 3538948

commit v5 on v3

v5 whole, which is shorter than its diff:
```python
import functools

import jax
import jax.numpy as jnp
from jax import lax
from jax.experimental import pallas as pl
from jax.experimental.pallas import tpu as pltpu
from jax.sharding import PartitionSpec as P

MESH = pl.DeviceIdType.MESH
EPSILON = 1e-06

SPAN = 4
SLOTS = 8
LINE = 4
PATIENT = (7, 2)
RUN = 16
WAVES = 4
DETOURS = (
)


ORDER = (
    (
        10639617, 10394406, 150994989, 184549422, 218299032, 251658283, 2115340, 16777241, 1543181, 3791945,
        50331700, 4259418, 83927474, 173088570, 33554483, 2078645, 117552459, 67112381, 201328598, 234881086,
        268697047, 100663314, 134217747, 0, 0, 0, 0, 0,
    ),
    (
        10115329, 10910504, 150994989, 184549376, 218277422, 251837404, 7684889, 7017840, 6153656, 8240313,
        13583245, 15684602, 16777732, 167772540, 50331657, 204017478, 33554432, 83886087, 117440523, 67363958,
        234881024, 100663314, 134444287, 268435456, 0, 0, 0, 0,
    ),
    (
        1859908, 9865473, 11430569, 151177692, 184549421, 221368878, 16777216, 251661300, 13947504, 50331708,
        182537630, 83946570, 16090487, 201326649, 6619890, 33685391, 117440570, 234881050, 71679987,
        268435515, 100664722, 134218967, 0, 0, 0, 0, 0, 0,
    ),
    (
        1859908, 9865473, 11430569, 151177692, 196560413, 14002073, 218103854, 12710939, 251661302, 2346481,
        167776120, 16777228, 204969033, 50331648, 46720266, 99155851, 117440512, 234881042, 67354581,
        100666582, 268435456, 134219219, 0, 0, 0, 0, 0, 0,
    ),
    (
        2380292, 6, 162695425, 10005349, 184719815, 218276590, 251837487, 3354161, 16989812, 64544437,
        168021499, 83944472, 201326653, 235136793, 268436479, 117441821, 33554432, 72742801, 106509970,
        134219227, 0, 0, 0, 0, 0, 0, 0, 0,
    ),
    (
        2380292, 162695425, 11952549, 2003623, 184746734, 218299498, 251661483, 7720184, 14020212, 8351376,
        183729876, 201330513, 16854924, 234881024, 50331661, 272184703, 83886080, 33554456, 117440527,
        67110486, 100663322, 134219227, 0, 0, 0, 0, 0, 0,
    ),
    (
        1859908, 9476616, 41, 9741057, 16779917, 50331648, 84042635, 117503019, 151176295, 184737042,
        232197011, 251661423, 14626614, 182709501, 201326649, 235119900, 268558079, 33554456, 67110485,
        107575190, 134219487, 0, 0, 0, 0, 0, 0, 0,
    ),
    (
        1859908, 2568, 16925441, 50387529, 11076261, 83886094, 11336075, 117440529, 150997799, 196427026,
        218103854, 264183152, 5491894, 6504311, 167772216, 201330617, 234884757, 268678591, 33670617,
        67110746, 100663326, 134219487, 0, 0, 0, 0, 0, 0,
    ),
    (
        1206628, 11555367, 150997513, 6, 1878849, 184552489, 27839371, 218103808, 63353711, 251658260,
        89599502, 117441935, 13436409, 13967028, 168021750, 201577655, 234885011, 268435519, 33556248,
        67110745, 100787930, 134217759, 0, 0, 0, 0, 0, 0,
    ),
    (
        10381668, 516, 11571521, 162834950, 187632199, 3230634, 218103857, 16970603, 50331648, 251659157,
        83889336, 117507471, 13844055, 14228858, 183602898, 201579987, 33558428, 234881024, 268435519,
        74823321, 100663326, 134217759, 0, 0, 0, 0, 0, 0,
    ),
    (
        1859908, 9476616, 41, 16777985, 50483853, 93893546, 117508815, 151176295, 196445364, 230268243,
        264437146, 13092564, 14888789, 167772215, 201584243, 235122646, 268439255, 33554460, 67108893,
        100663326, 134217759, 0, 0, 0, 0, 0, 0, 0,
    ),
    (
        1859908, 8, 16941825, 61135113, 3737930, 83886122, 121443046, 4819687, 150998316, 184653037,
        218107246, 12430356, 267589366, 14507890, 167772216, 16487859, 201326620, 33558167, 234881024,
        268439295, 67108893, 100663326, 134217759, 0, 0, 0, 0, 0,
    ),
    (
        1206628, 11555367, 162955657, 10779658, 184552331, 11066444, 16777263, 50331648, 218311374, 83886100,
        251658240, 117444111, 13485077, 7816633, 13964794, 6516446, 33632031, 172859255, 201326654, 67108864,
        234885082, 100663323, 268435456, 134217728, 0, 0, 0, 0,
    ),
    (
        9980260, 11555367, 2648585, 150994989, 12227056, 184549387, 218103850, 29816076, 251658283, 50420877,
        83979790, 117440527, 13868240, 14013916, 14257978, 167774097, 33554432, 14495455, 67112793, 201582227,
        100663296, 234881051, 134217791, 268435456, 0, 0, 0, 0,
    ),
    (
        1859908, 16828936, 61135113, 11077962, 83886798, 128869455, 150997799, 196447506, 6745427, 218105136,
        264612854, 7310834, 7576789, 33558166, 67352029, 100663326, 134217759, 167772220, 201326653,
        234881086, 268435519, 0, 0, 0, 0, 0, 0, 0,
    ),
    (
        1859908, 16828936, 53908068, 2794533, 83886094, 4518630, 117440555, 155895335, 189635444, 218322606,
        251661296, 7282068, 7568568, 33789299, 67229114, 100906903, 134217759, 167772220, 201326653,
        234881086, 268435519, 0, 0, 0, 0, 0, 0, 0,
    ),
    (
        10381668, 1491460, 163764745, 12227206, 11058247, 184549423, 229428372, 5976917, 7404814, 16874832,
        256337437, 6780062, 50439391, 83886107, 117440512, 33554432, 67108864, 100663296, 134217728,
        167775804, 201584253, 235126778, 268435456, 0, 0, 0, 0, 0,
    ),
    (
        10381668, 10521348, 163762757, 2810281, 12890602, 3230447, 184604018, 13583254, 218166736, 7675228,
        6367158, 258291703, 16778970, 50331648, 83886080, 117440512, 33554432, 67108924, 100663352, 134217728,
        167776121, 201326650, 234881086, 268439547, 0, 0, 0, 0,
    ),
    (
        1859908, 9486888, 9753193, 4252330, 3980006, 16780071, 12159825, 50525778, 96840723, 117440512,
        151108756, 184549376, 218103808, 251747548, 33556310, 67110807, 100663327, 134217728, 15965496,
        167772213, 217046458, 235143095, 268435456, 0, 0, 0, 0, 0,
    ),
    (
        1859908, 3180840, 16777257, 3447461, 11314214, 4504014, 4903916, 50334616, 88972335, 7162970,
        150996338, 117556659, 184551255, 218234654, 251911480, 47967861, 67108922, 100663359, 134221559,
        167772160, 201326592, 234881024, 268435456, 0, 0, 0, 0, 0,
    ),
    (
        10381668, 1346308, 151034728, 184552006, 3072647, 218106858, 3492556, 16777230, 251659599, 50333462,
        83886080, 117442391, 6682142, 33621722, 4705332, 81990837, 14364499, 16481529, 100663354, 167772160,
        134221819, 201326592, 234881024, 268435456, 0, 0, 0, 0,
    ),
    (
        10381668, 1491460, 1612648, 2024105, 3340939, 151049515, 184549376, 218105166, 16778639, 251658268,
        50456029, 83886080, 117440536, 7063135, 12836379, 16457332, 167775925, 217017535, 234881024,
        268439027, 33554448, 67108881, 100663314, 134217747, 0, 0, 0, 0,
    ),
    (
        1859908, 3293736, 16777257, 61397321, 3062154, 4355022, 83886124, 12422061, 117440529, 150994969,
        184549402, 218103835, 251658240, 8251228, 15926482, 33558036, 5981553, 14102141, 14396631, 67354110,
        167772160, 100663359, 201326592, 134217728, 234881024, 268435456, 0, 0,
    ),
    (
        1859908, 3293736, 16777257, 3582281, 3848586, 62026699, 96308141, 117440537, 150994944, 184549402,
        218103808, 251658240, 7833371, 12709492, 13086047, 4402934, 4928631, 167772220, 33555731, 67202901,
        201330583, 100663359, 134217728, 234881024, 268435456, 0, 0, 0,
    ),
    (
        10381668, 151161604, 1479213, 184549422, 12497514, 218103814, 251658698, 16827659, 50332501, 83886094,
        117561103, 15796190, 5981304, 6229842, 13080083, 14364597, 167775897, 33664499, 201326592, 67112923,
        234881024, 100663355, 134217728, 268435456, 0, 0, 0, 0,
    ),
    (
        10381668, 150997548, 195330349, 11467438, 218104389, 251658240, 2912902, 16777228, 13829005, 14096143,
        13330333, 50331679, 83886080, 117440512, 5492211, 167772216, 5837845, 5055997, 201328185, 33556094,
        15726266, 67108891, 234881024, 100663296, 268435456, 134217728, 0, 0,
    ),
    (
        1859908, 10783016, 10013349, 16955849, 15772429, 62174222, 157537262, 83886127, 184549401, 218103808,
        117440512, 251658240, 14757777, 5702964, 5877331, 6143093, 13367098, 167772214, 201328499, 33554432,
        234884830, 67108864, 100666847, 134217728, 268435456, 0, 0, 0,
    ),
    (
        1859908, 9869608, 10011178, 16779755, 50385532, 84136842, 151057132, 117443629, 184549376, 218106990,
        251915439, 4686899, 167772212, 6812824, 6905428, 215312083, 33670650, 14661494, 234881054, 67108895,
        268435456, 100663296, 134217728, 0, 0, 0, 0, 0,
    ),
    (
        10381668, 10506756, 11049592, 2801222, 3124999, 171133972, 16777216, 13950805, 56159312, 14339215,
        201442427, 6366685, 5086078, 13479390, 91095022, 117440559, 150994944, 33554432, 234881024, 184549376,
        67108864, 100663296, 218103808, 268435456, 134217728, 251658240, 0, 0,
    ),
    (
        10381668, 10915448, 11043132, 15381061, 16171654, 150995655, 3883852, 16778224, 5311358, 13980795,
        50333503, 7693489, 5204888, 13493874, 8224239, 83887834, 167772160, 117440512, 184549376, 201326592,
        33554432, 218103808, 234881024, 67108864, 251658240, 268435456, 100663296, 134217728,
    ),
    (
        1859908, 13682952, 16932617, 50388326, 87808458, 14222072, 16450513, 117442066, 167772160, 208082169,
        14625300, 11624410, 11909754, 7812886, 15657623, 159300574, 234881024, 184549376, 33554432, 67108864,
        218103808, 268435456, 100663296, 251658240, 134217728, 0, 0, 0,
    ),
    (
        1859908, 9658164, 10214949, 31093512, 2786121, 50589262, 83887051, 117440512, 167775248, 16753772,
        5469353, 5082865, 151100245, 201326592, 5974702, 6147034, 184671467, 218232731, 234881024, 33554432,
        251658240, 268435456, 67108864, 100663296, 134217728, 0, 0, 0,
    ),
    (
        10115329, 151177767, 184552297, 218106794, 2146607, 16777259, 251658245, 50385289, 2035210, 6493451,
        83945268, 13462677, 117503609, 6911861, 7302814, 168021727, 33805367, 201326592, 67112849, 234881024,
        100663314, 268435519, 134217747, 0, 0, 0, 0, 0,
    ),
    (
        10115329, 151177767, 184552045, 218106542, 5435908, 251658283, 1412208, 14718741, 7704982, 20017842,
        48712912, 50455386, 67108881, 83887246, 100663296, 121418951, 15580853, 134217759, 167775676,
        201326653, 234881086, 268439543, 0, 0, 0, 0, 0, 0,
    ),
    (
        1859908, 9865473, 11446697, 154323400, 16777225, 184550253, 50334986, 83886094, 6353648, 117442350,
        218103824, 7019865, 251661277, 13233563, 182681361, 216520691, 33555604, 234884798, 67112917,
        268435515, 100664534, 134217751, 0, 0, 0, 0, 0, 0,
    ),
    (
        1859908, 10914049, 11430565, 16826919, 150997784, 2463540, 50331661, 184551085, 7276362, 83887029,
        5855124, 222130926, 117444017, 33554448, 251658287, 13180727, 67108920, 167772191, 201404029,
        100663358, 235142394, 134221523, 268435456, 0, 0, 0, 0, 0,
    ),
    (
        2380292, 6, 11700481, 10934602, 150997383, 184549415, 218278795, 254983152, 16777265, 50388530,
        87792947, 131661493, 5471964, 167898909, 201330512, 234885023, 268436863, 33653905, 67212502,
        100663322, 134219479, 0, 0, 0, 0, 0, 0, 0,
    ),
    (
        20996, 11682369, 150997541, 11823590, 184552010, 12255943, 218103850, 264944625, 16777228, 13843996,
        50332509, 15423417, 83886094, 6516447, 167772220, 215996057, 121749391, 234881024, 268436799,
        33554432, 67110225, 100742546, 134217751, 0, 0, 0, 0, 0,
    ),
    (
        1859908, 2509320, 152233, 16777985, 50331661, 86829482, 117440527, 151177707, 184552749, 218323888,
        266007601, 14664818, 5233874, 168005528, 201326649, 234884756, 268439547, 40985945, 67229146,
        100663326, 134219739, 0, 0, 0, 0, 0, 0, 0,
    ),
    (
        1859908, 150024, 27562753, 50334029, 4367242, 83886118, 117617611, 150997799, 184621940, 218323888,
        251861970, 14664950, 168005490, 13606812, 201326621, 235141050, 268435515, 33654047, 67110485,
        100771286, 134217755, 0, 0, 0, 0, 0, 0, 0,
    ),
    (
        10381668, 2380292, 27180, 150994945, 10779466, 184549387, 27986828, 218103821, 50332591, 84087787,
        251658240, 117443768, 13872377, 15691092, 167776055, 201330517, 234881086, 268439510, 39912924,
        67213137, 7185618, 100663326, 134217759, 0, 0, 0, 0, 0,
    ),
    (
        10381668, 2380292, 161508097, 10779466, 184550128, 218155946, 16777216, 11465556, 50332593, 251658240,
        83886095, 117440512, 5741752, 14134516, 183745942, 201577975, 234881086, 268435519, 40993872,
        74814674, 100787930, 134217759, 0, 0, 0, 0, 0, 0,
    ),
    (
        1859908, 9476616, 3576577, 16779594, 50331648, 83888782, 117502694, 164809195, 184549421, 218106805,
        267586991, 6500209, 168004855, 201561150, 234882682, 268439295, 4830298, 33556244, 67229011,
        100787670, 134217759, 0, 0, 0, 0, 0, 0, 0,
    ),
    (
        1859908, 2568, 19284737, 50331661, 87708329, 3979690, 117440528, 162630123, 184552308, 230878545,
        251763702, 14626609, 167776120, 217816282, 251510418, 268435515, 40981779, 67229142, 100663326,
        134217759, 0, 0, 0, 0, 0, 0, 0, 0,
    ),
    (
        9980260, 11555367, 150997513, 2019974, 197323339, 16779916, 218103857, 50334669, 251659179, 83886095,
        117444146, 13442640, 4939444, 167776054, 5232443, 201326647, 234881086, 268695380, 5895518, 33554456,
        67110487, 100663322, 134217755, 0, 0, 0, 0, 0,
    ),
    (
        9980260, 11555367, 150997513, 12767878, 196655687, 16779916, 218297201, 50331691, 251716914, 83886080,
        117444111, 15152156, 14134549, 182175569, 14668987, 201328531, 234881086, 268563903, 33555991,
        67108889, 100663322, 134217755, 0, 0, 0, 0, 0, 0,
    ),
    (
        1859908, 16828936, 61133412, 2689701, 83886094, 3978342, 117440555, 150997799, 184737042, 218295635,
        264203284, 14888021, 13463159, 6534650, 167772220, 49661593, 201326592, 67110747, 234881086,
        100663326, 268435519, 134217759, 0, 0, 0, 0, 0, 0,
    ),
    (
        1859908, 16828936, 61133412, 2794533, 83886094, 3978342, 117440555, 151176359, 189631348, 218103854,
        5442549, 251661430, 14650521, 6003925, 183746199, 201330522, 234999707, 33554432, 268435519, 67108893,
        100663326, 134217759, 0, 0, 0, 0, 0, 0,
    ),
    (
        10381668, 161516292, 12767813, 2812486, 184549418, 12368967, 223552299, 251659093, 4404622, 16872436,
        6772241, 50332854, 83886080, 117550547, 14798619, 33554493, 167772160, 201328505, 67348414, 100667359,
        234881083, 134217728, 268435456, 0, 0, 0, 0, 0,
    ),
    (
        10381668, 161516292, 12767813, 184738217, 12876426, 5422027, 218104626, 251659093, 13692118, 13956560,
        16778332, 7679384, 5207676, 57661112, 83886137, 117680062, 33798143, 67108864, 167772160, 201326592,
        100663296, 234881024, 134217728, 268435456, 0, 0, 0, 0,
    ),
    (
        1859908, 3180840, 16777257, 3447461, 3712038, 2955755, 4903916, 50525742, 7013971, 83999828, 7720085,
        150996403, 8357783, 117440564, 184549376, 218103865, 251658240, 33554432, 67108864, 100663296,
        134217781, 14663098, 167772220, 201326653, 234885118, 268435456, 0, 0,
    ),
    (
        1859908, 3180840, 16777257, 3447461, 50332710, 3046090, 11868942, 4819855, 83886127, 6895216,
        13219121, 13487637, 150996404, 15826525, 15334750, 184552893, 134213115, 218103808, 251658240,
        33554432, 67108864, 167772160, 100663296, 134217728, 201326592, 234881024, 268435456, 0,
    ),
    (
        10381668, 1491460, 150994984, 2648905, 184552361, 218276551, 5422028, 5825869, 6145039, 16778333,
        251658270, 50333202, 6635295, 91162292, 117440512, 33557885, 67108913, 100663296, 134217790, 14630070,
        167776248, 201326649, 234884858, 268435456, 0, 0, 0, 0,
    ),
    (
        10381668, 1491460, 150994984, 2648905, 184552361, 218276551, 5422028, 16777229, 3999054, 251658262,
        13829980, 50332796, 83888023, 14095890, 5111672, 15165081, 13483954, 117702327, 33554491, 167772160,
        67108864, 100663296, 201326592, 134217728, 234881024, 268435456, 0, 0,
    ),
    (
        1859908, 3293736, 16777257, 3582281, 3737994, 3979755, 50334481, 83889069, 117515823, 156345561,
        184550747, 230778680, 251660119, 46634974, 67108864, 100663296, 134217728, 13843642, 168021371,
        201580022, 234881086, 268435519, 0, 0, 0, 0, 0, 0,
    ),
    (
        1859908, 3293736, 16777257, 3582281, 3737994, 3979755, 12244076, 50525714, 12666451, 83889690,
        117440512, 7294037, 151111097, 15424663, 14366621, 184553183, 218103863, 251658240, 33554432,
        67108864, 100663296, 134217728, 167772220, 201326653, 234881086, 268435519, 0, 0,
    ),
    (
        10381668, 1491460, 150994984, 11964809, 2026122, 184549387, 223398639, 251659597, 16777230, 50331648,
        84100054, 117442012, 8082461, 6516497, 33554450, 67212511, 100861658, 13311485, 134217784, 167772211,
        201330302, 234885114, 268435515, 0, 0, 0, 0, 0,
    ),
    (
        10381668, 10666500, 10787653, 150994990, 12364422, 184549419, 218104519, 251658240, 12796692,
        16777237, 56302925, 97059766, 14480471, 6367027, 117520285, 33554432, 15837145, 67108891, 100663296,
        134217728, 167775805, 201330302, 234884799, 268435515, 0, 0, 0, 0,
    ),
    (
        1859908, 20072968, 3578185, 50375082, 3046094, 83888911, 12159868, 117634685, 151105456, 184549376,
        218103808, 251658256, 16587867, 5713428, 33646354, 67228887, 8339038, 100663348, 134217728, 167772160,
        201330042, 234884854, 268435511, 0, 0, 0, 0, 0,
    ),
    (
        1859908, 3293736, 16777257, 3582281, 50331686, 11577835, 3071758, 12651407, 155647832, 90694833,
        184549426, 117441754, 218103808, 251658260, 7167987, 33556246, 67340119, 100663326, 134217759,
        167775545, 201330042, 234884539, 268435511, 0, 0, 0, 0, 0,
    ),
    (
        10381668, 2380292, 14723590, 11055593, 16778041, 50332523, 150997818, 13874108, 83890029, 184549376,
        218107822, 117441492, 5622837, 167772176, 4715933, 12920727, 5110774, 14624344, 201440474, 251658240,
        33554432, 67108864, 234881024, 100663296, 268435456, 134217728, 0, 0,
    ),
    (
        10381668, 1475076, 11178616, 2798009, 153078586, 196599499, 5694228, 13827981, 4515216, 4191698,
        12703507, 16995870, 14358489, 218310362, 50335219, 251658240, 83886080, 117440512, 167772160,
        33554432, 67108864, 201326592, 100663296, 134217728, 234881024, 268435456, 0, 0,
    ),
    (
        1859908, 16777992, 13779785, 50332348, 83887013, 16210315, 117440527, 16476711, 150998572, 12770815,
        167775849, 184789930, 218103808, 201428048, 5349073, 12408466, 7158955, 251658262, 242601175,
        268437470, 33554432, 67108864, 100663296, 134217728, 0, 0, 0, 0,
    ),
    (
        1859908, 16925448, 15880820, 60774797, 87777981, 151177784, 14603006, 12293135, 117634153, 195658943,
        218103808, 12688122, 251658259, 168015508, 6141333, 201326641, 33676444, 235011294, 67108864,
        100663296, 268435456, 134217728, 0, 0, 0, 0, 0, 0,
    ),
    (
        10115329, 151177767, 184552297, 218106542, 2289932, 16777229, 251658283, 52749573, 1674352, 46777359,
        2838037, 83886105, 5977927, 6913401, 117441246, 14284538, 67110011, 167775740, 201326653, 100663314,
        234881086, 268436735, 134217728, 0, 0, 0, 0, 0,
    ),
    (
        10115329, 150997800, 184720231, 229163310, 16970253, 251658283, 52752718, 83930630, 117486855,
        13720688, 5885080, 48715344, 67109981, 7959706, 100663354, 8337147, 167773436, 134217728, 201330550,
        234881086, 268439039, 0, 0, 0, 0, 0, 0, 0,
    ),
    (
        1859908, 9865473, 11430569, 28363208, 150994944, 50386441, 5456540, 184549421, 91548697, 13034229,
        218103834, 33554448, 13301659, 251659254, 117440512, 14907388, 167772211, 67182165, 201326653,
        4812730, 234881083, 100663296, 268436735, 134217751, 0, 0, 0, 0,
    ),
    (
        1859908, 10914049, 11430565, 16828872, 150997769, 50334989, 83886986, 117503499, 7443504, 184549421,
        7033969, 38463316, 218103808, 67110262, 14542255, 251658267, 100663356, 167774200, 15195283,
        201326615, 134217728, 234884798, 268648191, 0, 0, 0, 0, 0,
    ),
    (
        2380292, 10633601, 150994988, 10005349, 184552039, 229302983, 13024240, 251658252, 16777216, 53972210,
        15060240, 6349941, 83886134, 15693690, 117687250, 167772190, 33556436, 201326653, 234882302,
        268435519, 67110233, 100664730, 134219479, 0, 0, 0, 0, 0,
    ),
    (
        2380292, 162695425, 10250661, 184720202, 12772039, 218103850, 16970545, 251661042, 50388531, 97840756,
        117441488, 5465914, 4701661, 167772220, 207742333, 33554432, 234885010, 67368534, 268435482,
        100663327, 134329811, 0, 0, 0, 0, 0, 0, 0,
    ),
    (
        1859908, 2509320, 41, 16777985, 50334029, 84059018, 121696998, 151177707, 184552273, 218295348,
        13063316, 251661298, 13485430, 5848572, 167776120, 201330302, 33558168, 234881024, 268439295,
        67213143, 100664990, 134219739, 0, 0, 0, 0, 0, 0,
    ),
    (
        1859908, 150024, 16777985, 50500425, 94954149, 121418790, 162601451, 184736820, 230366546, 12529044,
        251661811, 168003132, 201561469, 15308030, 234881052, 33813947, 268437338, 67108894, 100663296,
        134346455, 0, 0, 0, 0, 0, 0, 0, 0,
    ),
    (
        10381668, 2380292, 44, 151159169, 2915146, 184549417, 29551244, 218103821, 50331648, 251661291,
        83944753, 117673103, 13866320, 6503802, 15801750, 167772219, 201578103, 234881086, 268435519, 5076626,
        33554460, 67110747, 100663326, 134217759, 0, 0, 0, 0,
    ),
    (
        10381668, 516, 11571521, 151159430, 11965127, 184549424, 16968332, 218106957, 50331648, 255523540,
        83886130, 117440527, 13700629, 15424761, 168021398, 217560631, 234885009, 268437311, 33554432,
        73258578, 100665242, 134346451, 0, 0, 0, 0, 0, 0,
    ),
    (
        1859908, 9476616, 16777985, 50331661, 3035817, 84060558, 117441551, 151177959, 184735284, 12774737,
        218105428, 251661302, 16199473, 174706168, 33554432, 5582771, 201326649, 67348351, 234881024,
        268435515, 100787603, 134346203, 0, 0, 0, 0, 0, 0,
    ),
    (
        1859908, 8, 16777985, 59822696, 87726410, 11166416, 117440527, 151177707, 198366296, 224877614,
        266017748, 7068860, 167773368, 15199731, 201326620, 33554432, 234884799, 268436859, 67229075,
        100665243, 134219735, 0, 0, 0, 0, 0, 0, 0,
    ),
    (
        9980260, 11555367, 150997513, 195482246, 12104176, 218103850, 16777228, 50535373, 89336526, 259067407,
        117440512, 13844049, 33556026, 14013589, 167997243, 217544595, 234972798, 67108864, 268435519,
        100664983, 134219487, 0, 0, 0, 0, 0, 0, 0,
    ),
    (
        9980260, 11555367, 150997513, 2019974, 197180329, 218103850, 16777228, 5422191, 251658253, 50331648,
        83889294, 117441528, 4429148, 15415156, 49092149, 167849782, 5234142, 201326614, 234881086, 268435519,
        67108889, 100664983, 134219487, 0, 0, 0, 0, 0,
    ),
    (
        1859908, 16828936, 61133412, 3713360, 83886122, 3978342, 117440555, 164809170, 184628781, 218189166,
        265903088, 14536497, 39530009, 167772160, 201563389, 251379351, 67110557, 100665243, 134217759,
        268435519, 0, 0, 0, 0, 0, 0, 0, 0,
    ),
    (
        1859908, 16828936, 61133412, 2795856, 83886094, 4518630, 117440555, 150997799, 196560402, 230767541,
        5348783, 251658289, 7572663, 33554453, 15297785, 74954391, 100665243, 167772220, 201326653, 134221727,
        234881024, 268435519, 0, 0, 0, 0, 0, 0,
    ),
    (
        10381668, 161516292, 10932805, 2810288, 184549418, 12893127, 231261483, 14889813, 4408214, 251723351,
        6510353, 16880822, 15324378, 50331703, 83886107, 117440512, 33554432, 67108864, 100663326, 134467295,
        167772221, 201326654, 234881087, 268435456, 0, 0, 0, 0,
    ),
    (
        10381668, 161516292, 10932805, 2810288, 12521962, 184549387, 3353300, 5976917, 4259086, 4675036,
        4941341, 225000921, 251658240, 16779163, 50331648, 83886080, 117440512, 33554432, 67108864, 100663296,
        134219768, 183746233, 201326653, 234881086, 268435519, 0, 0, 0,
    ),
    (
        1859908, 3180840, 16777257, 3447461, 50332710, 10400650, 4113105, 96044205, 12688372, 15947411,
        151106865, 16108693, 125253046, 184551319, 218103808, 251658271, 33554432, 67108864, 100663296,
        134217728, 182681598, 201326649, 234881082, 268435515, 0, 0, 0, 0,
    ),
    (
        1859908, 3180840, 16777257, 3447461, 50331686, 3847178, 4113127, 83888977, 12397464, 5090329,
        13219121, 5977877, 150994973, 117442455, 184549407, 218103808, 251658240, 33554432, 67108864,
        100663296, 134217728, 14146876, 14679486, 167772216, 201326649, 234881082, 268435515, 0,
    ),
    (
        10381668, 1491460, 150994984, 2648905, 184552361, 12755655, 229458735, 3759181, 4025872, 7808785,
        7962194, 23459347, 251658266, 50331675, 83886080, 117440570, 33554432, 67112700, 100663296, 134217728,
        167989107, 201326645, 249560510, 268435456, 0, 0, 0, 0,
    ),
    (
        10381668, 1491460, 150994984, 2648905, 184552361, 218276551, 16780236, 54086349, 251724757, 4576668,
        90252766, 117544915, 33554458, 67108891, 100663296, 134217728, 15146544, 15679154, 167775548,
        201330549, 251625398, 268435456, 0, 0, 0, 0, 0, 0,
    ),
    (
        1859908, 3293736, 16777257, 3582281, 3737994, 2955755, 11873039, 50334616, 90653935, 123164308,
        150994966, 184549403, 218105623, 251658269, 33554462, 67112351, 100666872, 134217728, 167972476,
        15675057, 201330547, 234881086, 268435519, 0, 0, 0, 0, 0,
    ),
    (
        1859908, 3293736, 16777257, 3582281, 50334090, 84063246, 11695051, 4909905, 117443544, 157889817,
        184549376, 218103808, 251658261, 33670555, 67110743, 100663326, 134217759, 14642548, 13093944,
        167772217, 16203442, 201326651, 234881086, 268435519, 0, 0, 0, 0,
    ),
    (
        10381668, 1491460, 150994984, 10775369, 184722094, 11471815, 218103819, 251658260, 16866380, 50331661,
        83886998, 4519376, 117517468, 7818451, 33554456, 13999646, 7206588, 67338102, 167772160, 100663358,
        134217728, 201330303, 234881082, 268435515, 0, 0, 0, 0,
    ),
    (
        10381668, 161516292, 10932805, 184593286, 11317738, 218103855, 251658252, 16778509, 50333006,
        84002191, 117442064, 33674327, 6679570, 67112019, 100791986, 134219507, 168005428, 15167349,
        201326647, 250609342, 268435456, 0, 0, 0, 0, 0, 0, 0,
    ),
    (
        1859908, 3293736, 16777257, 3582281, 50373670, 94286926, 4180747, 150994962, 12311384, 117440537,
        191622099, 218103871, 251658240, 5854932, 7554544, 33558065, 167772189, 8363166, 67108915, 100663354,
        134217728, 201330043, 234881078, 268435511, 0, 0, 0, 0,
    ),
    (
        1859908, 10783016, 16777228, 3447461, 50331686, 95318922, 133350347, 150994989, 16059288, 4912217,
        16594622, 184551188, 218105179, 251658240, 33554432, 67204950, 100663326, 134220831, 167775544,
        14102129, 201330355, 235110134, 268435456, 0, 0, 0, 0, 0,
    ),
    (
        10381668, 2380292, 1743416, 11315897, 15532538, 16237265, 12660628, 13815756, 11887445, 6110542,
        14273423, 6485917, 17004529, 150996633, 167775387, 50331648, 184549376, 83886131, 117440512,
        218103808, 251658240, 33554432, 201326592, 67108864, 100663296, 134217728, 234881024, 268435456,
    ),
    (
        10381668, 14844420, 1741381, 2069162, 32033483, 55821179, 11796413, 150996302, 83886080, 123278288,
        6215472, 7941405, 184549422, 6682131, 167975925, 218103808, 46775706, 67112435, 251658240, 201326592,
        100663296, 134217728, 234881024, 268435456, 0, 0, 0, 0,
    ),
    (
        1859908, 16777992, 9503348, 4704589, 50375093, 10282173, 83967926, 16597751, 4113784, 117440569,
        15654552, 151193000, 167772160, 13036121, 12528282, 184551127, 201329899, 218103836, 235009949,
        251658240, 268435456, 33554432, 67108864, 100663296, 134217728, 0, 0, 0,
    ),
    (
        1859908, 20138248, 10002213, 2874701, 50334158, 100201206, 134024759, 6526060, 12041874, 150997523,
        10831470, 12777109, 11364074, 7718385, 198047666, 167772160, 218103808, 251658240, 201326592,
        33554432, 67108864, 234881024, 100663296, 134217728, 268435456, 0, 0, 0,
    ),
    (
        10115329, 10910504, 150994989, 184549422, 218106520, 3475212, 38868591, 251661021, 67108885, 1142042,
        7175518, 16777759, 1543222, 50334793, 100666962, 2847154, 83887034, 134217747, 3980487, 117440571,
        167772220, 201326653, 234881086, 268435519, 0, 0, 0, 0,
    ),
    (
        10115329, 162954024, 184552361, 224414348, 16811823, 258388877, 7816197, 33752335, 50331657, 6843509,
        84009650, 1908147, 67108885, 117551864, 5895351, 100663353, 134456535, 167775996, 201326653,
        234881086, 268435519, 0, 0, 0, 0, 0, 0, 0,
    ),
    (
        1859908, 9865473, 7498409, 10343723, 12764693, 150994969, 33554448, 2299802, 184552283, 16982815,
        218106804, 62709065, 251658240, 15953110, 83956618, 67108919, 182702807, 117441679, 100663296,
        201326649, 134221715, 234881082, 268439547, 0, 0, 0, 0, 0,
    ),
    (
        1859908, 10914049, 11430565, 27051784, 150994988, 5282845, 184552557, 50332504, 33620638, 218107054,
        83889422, 2989269, 251661301, 123279311, 67110582, 14532156, 167772183, 100663314, 134456569,
        201326653, 234885051, 268435519, 0, 0, 0, 0, 0, 0,
    ),
    (
        2380292, 6, 11700481, 11966794, 150997383, 184738535, 218103850, 251661039, 12698648, 8095577,
        38061361, 16777216, 13446303, 50568461, 87774426, 74409338, 117440527, 100666838, 134221591,
        167772219, 201326653, 234881086, 268435519, 0, 0, 0, 0, 0,
    ),
    (
        2380292, 10668289, 151151013, 2653031, 184738537, 218103850, 16954159, 251658240, 3609648, 50331672,
        3742876, 83889715, 33557780, 4035765, 117562809, 72693431, 8220318, 100665084, 167772160, 134221655,
        201326592, 234885051, 268435519, 0, 0, 0, 0, 0,
    ),
    (
        1859908, 2509320, 16828993, 50334029, 88140426, 117504395, 11696849, 150994962, 184549421, 218106780,
        13751508, 251658287, 39935868, 12677118, 6155381, 67214518, 115453151, 167772215, 134221403,
        201326592, 234881082, 268435515, 0, 0, 0, 0, 0, 0,
    ),
    (
        1859908, 2568, 26252033, 50332521, 11076261, 93918091, 117440527, 162605547, 184549421, 218103854,
        251658287, 7587028, 12797309, 40050686, 13462898, 6679965, 67108887, 167772216, 100793946, 201326592,
        134217755, 234884791, 268435515, 0, 0, 0, 0, 0,
    ),
    (
        10381668, 2380292, 161508097, 10793418, 184549421, 218106794, 16777228, 50525453, 251658283, 83886094,
        12645397, 117440568, 6532694, 16088849, 46515835, 5242770, 13483162, 167774068, 67108864, 201326645,
        100666782, 234881024, 134221279, 268435456, 0, 0, 0, 0,
    ),
    (
        10381668, 20996, 10525441, 150994950, 186553005, 218278795, 16971020, 50509133, 251658240, 83886094,
        4023352, 117440560, 6268473, 4961404, 16358525, 41100543, 167775514, 201447157, 67108915, 234881078,
        100663326, 268435511, 134217759, 0, 0, 0, 0, 0,
    ),
    (
        1859908, 2568, 26264129, 50331661, 3840330, 83888784, 117502694, 6363627, 150994988, 184552749,
        232187161, 251852434, 14933814, 33556245, 15197403, 7843831, 67108923, 100787670, 134217759,
        167772208, 201326641, 234881074, 268435507, 0, 0, 0, 0, 0,
    ),
    (
        1859908, 8, 16828929, 10801764, 50483856, 2955918, 83886118, 117443279, 157467815, 184764013,
        218103854, 258559343, 7565075, 33554488, 14507867, 15298489, 67352447, 167775255, 100663326,
        201326641, 234883058, 134217728, 268435507, 0, 0, 0, 0, 0,
    ),
    (
        9980260, 11555367, 150997513, 195482246, 12772039, 218104618, 16777216, 11326767, 50331697, 251658240,
        83889294, 123175951, 7837457, 33557784, 6005918, 14400883, 67356243, 167772160, 217413623, 234881086,
        268435519, 100663322, 134217755, 0, 0, 0, 0, 0,
    ),
    (
        9980260, 11555367, 11960713, 150994954, 3082823, 184549422, 218106516, 5708748, 16777259, 251661453,
        4425102, 50331663, 83886080, 117440540, 13753971, 47687185, 14231447, 173000699, 67110519, 201326653,
        100663322, 234881086, 268435519, 134217755, 0, 0, 0, 0,
    ),
    (
        1859908, 16828936, 61133412, 3713360, 83886122, 3978342, 117440555, 151176359, 184737048, 218106771,
        12424501, 251659632, 46518070, 6909815, 167775794, 7812606, 67112953, 201326650, 234881051, 268435515,
        100663326, 134217759, 0, 0, 0, 0, 0, 0,
    ),
    (
        1859908, 16828936, 10803465, 50331664, 3844426, 84042827, 117443279, 162690578, 184737049, 218106771,
        5442906, 251658287, 5753974, 33782940, 173790968, 216366334, 67108893, 234885114, 100667102,
        268435456, 134217759, 0, 0, 0, 0, 0, 0, 0,
    ),
    (
        10381668, 161516292, 10932805, 2820998, 184549418, 13038279, 218106580, 257395852, 5979725, 13726734,
        7410682, 4961845, 15951453, 8091283, 17032957, 50335711, 83886080, 117440512, 33554432, 67108864,
        167772160, 100663296, 201326592, 234881024, 134217728, 268435456, 0, 0,
    ),
    (
        10381668, 1346308, 151179880, 12626502, 11055598, 11357295, 184549388, 14736533, 15002838, 15269136,
        7673623, 7963829, 15689340, 218103827, 16121306, 251662235, 16777279, 50331648, 83886080, 117440512,
        33554432, 167772160, 67108864, 100663296, 201326592, 134217728, 234881024, 268435456,
    ),
    (
        1859908, 3180840, 16777257, 3447461, 50334096, 10400650, 4113105, 12011026, 84076149, 12690671,
        12956982, 14886263, 7812508, 8111609, 15597434, 150995006, 117440575, 184549376, 218103808, 251658240,
        33554432, 67108864, 167772160, 100663296, 201326592, 134217728, 234881024, 268435456,
    ),
    (
        1859908, 3293736, 16777257, 11065673, 10019472, 50331691, 3979729, 83886124, 131257496, 5200793,
        165260272, 12959508, 16199189, 16369079, 15062515, 184788927, 218105851, 251658240, 167772160,
        33554432, 67108864, 201326592, 100663296, 234881024, 268435456, 134217728, 0, 0,
    ),
    (
        10381668, 1491460, 150994984, 2648905, 184740905, 12890602, 5419823, 3759245, 222246288, 16779025,
        265385810, 14898398, 14286424, 50331673, 7306906, 83886139, 117440512, 33554432, 67108864, 100663356,
        134217728, 167772160, 201326653, 234881086, 268435519, 0, 0, 0,
    ),
    (
        10381668, 1346308, 151034728, 184552006, 12771975, 13040267, 218281228, 3756914, 16777232, 13434390,
        4673116, 4838906, 6418165, 6681846, 267499191, 50331648, 83886141, 117440574, 33554495, 67108864,
        100663296, 134217728, 167772160, 201326592, 234881024, 268435456, 0, 0,
    ),
    (
        1859908, 3293736, 16777257, 3582281, 3737994, 3044459, 11873039, 5176216, 50331673, 89589396,
        124720564, 158541301, 184671667, 218234334, 251658296, 33554432, 67108864, 100663296, 134217728,
        183746233, 201326653, 234881086, 268435519, 0, 0, 0, 0, 0,
    ),
    (
        1859908, 3293736, 16777257, 11065673, 61760144, 4518795, 83888935, 129600338, 150994944, 6767855,
        12692820, 184549430, 218330481, 251751579, 33764828, 8252957, 67108921, 100663296, 134217786,
        167776059, 201326653, 234881086, 268435519, 0, 0, 0, 0, 0,
    ),
    (
        10381668, 2263812, 12081773, 150997641, 187347375, 218103808, 251658240, 5440199, 5710641, 5977101,
        16778129, 7414743, 50451700, 83886104, 7034462, 131972511, 33554432, 67108864, 100663296, 134217728,
        167775804, 201330301, 235142846, 268435515, 0, 0, 0, 0,
    ),
    (
        10381668, 161513772, 2382445, 184552110, 2821062, 218103851, 264810993, 20005939, 55104849, 87770515,
        7558103, 8087069, 117442167, 33785818, 67108891, 100663296, 134217728, 167772220, 201330553,
        235122686, 268435515, 0, 0, 0, 0, 0, 0, 0,
    ),
    (
        1859908, 10783016, 4246181, 4633190, 11782605, 3920530, 16777261, 66912139, 151184915, 83886080,
        184549376, 117440512, 218187375, 251856218, 7435675, 33554481, 13495453, 67108895, 100663296,
        134217728, 167775544, 201330041, 235126202, 268435511, 0, 0, 0, 0,
    ),
    (
        1859908, 2267432, 16778021, 4233642, 15891149, 50391818, 11842685, 4910991, 150996500, 5586927,
        90113433, 184549402, 117440512, 218105585, 251658290, 33556275, 67110772, 100663326, 134217759,
        167772216, 201330293, 235106042, 268435511, 0, 0, 0, 0, 0,
    ),
    (
        10381668, 10715652, 15706745, 2607749, 2649963, 16547756, 150994955, 16778004, 50332501, 83944470,
        11859409, 117442322, 184648925, 12773273, 7292890, 33774577, 67108864, 218107314, 100666615,
        167772160, 134217728, 251658240, 201326592, 234881024, 268435456, 0, 0, 0,
    ),
    (
        10381668, 10522116, 1550969, 11516553, 16035590, 16544830, 3228369, 16780332, 150995797, 50390166,
        83949037, 5098776, 12180569, 184549402, 12447067, 14626207, 117440563, 167772160, 33554432, 67108864,
        218103808, 201326592, 100663296, 251658240, 134217728, 234881024, 268435456, 0,
    ),
    (
        1859908, 20073736, 16146229, 4423606, 2619793, 15105554, 2861581, 3067598, 50331663, 83886104,
        150996589, 117440512, 5352339, 191716329, 225617366, 33557533, 8305758, 67108914, 167772211,
        100663296, 201326592, 251658240, 134217728, 234881024, 268435456, 0, 0, 0,
    ),
    (
        1859908, 3293748, 16780668, 10186597, 16309705, 50331687, 14987256, 99421838, 4764945, 10550037,
        117442067, 150994944, 5876313, 184549421, 167775259, 11199964, 33554461, 230550257, 67112095,
        201326592, 100663347, 251658240, 134217728, 234881024, 268435456, 0, 0, 0,
    ),
)


def kernel(
    n_grp,
    n_blk,
    image_hbm,
    text_hbm,
    image_ids,
    text_ids,
    sharpness,
    offset,
    adjoint,
    grad_image,
    grad_text,
    raw,
    hat,
    buf,
    ids,
    own_ids,
    inverse,
    total,
    load_sem,
    send_sem,
    id_send_sem,
    wrap_sem,
    wrap_id_sem,
    detour_sem,
    ready_sem,
    recv_sem,
    id_recv_sem,
):
    rows = hat.shape[1]
    piece = rows // WAVES
    g = lax.axis_index("grp")
    k = lax.axis_index("blk")
    j = lax.rem(k, RUN)

    loads = [
        pltpu.make_async_copy(text_hbm, raw.at[0], load_sem.at[0]),
        pltpu.make_async_copy(image_hbm, raw.at[1], load_sem.at[1]),
    ]
    for load in loads:
        load.start()

    def device(dg, dk):
        return (lax.rem(g + dg + n_grp, n_grp), lax.rem(k + dk + n_blk, n_blk))

    next_grp = [device(step, 0)[0] for step in (1, -1)]
    next_blk = [device(0, step)[1] for step in (1, -1)]

    barrier = pltpu.get_barrier_semaphore()

    def greet(target):
        pl.semaphore_signal(barrier, inc=1, device_id=target, device_id_type=MESH)

    for target in (device(0, -1), device(1, 0), device(-1, 0)):
        greet(target)

    @pl.when(j != RUN - 1)
    def _():
        greet(device(0, 1))

    even = lax.rem(j, 2) == 0

    @pl.when(even & (j >= 2))
    def _():
        greet(device(0, -2))

    @pl.when(jnp.logical_not(even) & (j <= RUN - 3))
    def _():
        greet(device(0, 2))

    def wrap_target(stream, owner, sender):
        step = 1 - 2 * stream
        return (0 if owner < SPAN else step, step * sender)

    def wrap_links(stream):
        links = [(distance, distance) for distance in range(1, SLOTS - 1)]
        links += [(owner, sender) for which, owner, sender, _, _ in DETOURS if which == stream]
        return sorted({(wrap_target(stream, *link), link[1]) for link in links})

    def others(stream):
        return [link for link in wrap_links(stream) if link[0] != (0, 1 - 2 * stream)]

    @pl.when(j == 0)
    def _():
        for (dg, dk), _ in others(0):
            greet(device(-dg, -dk))

    far_sends = sum([(RUN - j == sender).astype(jnp.int32) for _, sender in others(0)])
    far_sends += jnp.where(j == RUN - 1, len(others(1)), 0) - jnp.where(j == 0, 1, 0)
    ready_count = sum([(j + 1 == sender).astype(jnp.int32) for _, sender in wrap_links(1)])
    for (dg, dk), sender in others(1):

        @pl.when(j + 1 == sender)
        def _():
            greet(device(dg, dk))

    def wrap_distance(stream):
        to_edge = RUN - j if stream == 0 else j + 1
        return to_edge, (to_edge >= 2) & (to_edge <= 6)

    skips = jnp.where(even, j != RUN - 2, j != 1).astype(jnp.int32)
    barrier_count = 4 + skips + far_sends

    @pl.when(j == RUN - 1)
    def _():
        pl.semaphore_wait(barrier, barrier_count)
        for (dg, dk), _ in wrap_links(1):
            pl.semaphore_signal(
                ready_sem, inc=1, device_id=device(-dg, -dk), device_id_type=MESH
            )

    for stream, own in ((0, text_ids), (1, image_ids)):
        loads[stream].wait()
        for c in range(WAVES):
            part = pl.ds(c * piece, piece)
            wide = raw[stream, part, :].astype(jnp.float32)
            inv = lax.rsqrt(jnp.sum(wide * wide, axis=-1, keepdims=True) + EPSILON)
            inverse[stream, part, :] = jnp.broadcast_to(inv, (piece, 128))
            unit = (wide * inv).astype(jnp.bfloat16)
            hat[stream, part, :] = unit
            buf[stream, c, pl.ds(0, piece), :] = unit
            at = c * piece
            line = own[at // 128 : at // 128 + 1, :].astype(jnp.float32)
            line = line[:, at % 128 : at % 128 + piece]
            ids[stream, 0, c] = jnp.concatenate([line] * (128 // piece), axis=1)

    @pl.when(j != RUN - 1)
    def _():
        pl.semaphore_wait(barrier, barrier_count)

    def pick(stream, pair):
        return pair[stream] if isinstance(stream, int) else jnp.where(stream == 0, pair[0], pair[1])

    def route(stream, s, reach):
        place = pick(stream, (j, RUN - 1 - j))
        entry = lax.rem(place, 2) == 0
        fresh = (s == 0) | (s == SPAN)
        if reach == 2:
            goes = entry & (place != RUN - 2) & (fresh | (s == 1) | (s == SPAN + 1))
            return (g, pick(stream, [device(0, step)[1] for step in (2, -2)])), goes
        hop = s == SPAN - 1
        target = (
            jnp.where(hop, pick(stream, next_grp), g),
            jnp.where(hop, k, pick(stream, next_blk)),
        )
        goes = jnp.where(place == RUN - 1, s == 0, entry | fresh)
        return target, (s < SLOTS - 1) & (hop | goes)

    def chunk(stream, s, c):
        at = s * piece
        if not isinstance(at, int):
            at = pl.multiple_of(at, piece)
        return buf.at[stream, c, pl.ds(at, piece)]

    def remote(src, dst, send, recv, target):
        return pltpu.make_async_remote_copy(
            src_ref=src,
            dst_ref=dst,
            send_sem=send,
            recv_sem=recv,
            device_id=target,
            device_id_type=MESH,
        )

    def block_copy(stream, s, c, reach, target):
        return remote(
            chunk(stream, s, c),
            chunk(stream, s + reach, c),
            send_sem.at[reach - 1, stream, s],
            recv_sem.at[stream, s + reach, c],
            target,
        )

    def id_copy(stream, s, reach, target):
        return remote(
            ids.at[stream, s],
            ids.at[stream, s + reach],
            id_send_sem.at[reach - 1, stream, s],
            id_recv_sem.at[stream, s + reach],
            target,
        )

    def forward(stream, s, c):
        for reach in (2, 1):
            target, goes = route(stream, s, reach)

            @pl.when(goes)
            def _():
                @pl.when(c == 0)
                def _():
                    id_copy(stream, s, reach, target).start()

                block_copy(stream, s, c, reach, target).start()

    def receive(stream, s, c):
        target = (g, pick(stream, next_blk))

        @pl.when(c == 0)
        def _():
            id_copy(stream, s - 1, 1, target).wait_recv()

        block_copy(stream, s - 1, c, 1, target).wait_recv()

    def wrap_route(stream):
        to_edge, far = wrap_distance(stream)
        same = to_edge < SPAN
        slot = jnp.where(same, to_edge, to_edge + 1)
        step = 1 - 2 * stream
        return far, slot, device(jnp.where(same, 0, step), step * to_edge)

    def wrap_id_copy(stream):
        _, slot, target = wrap_route(stream)
        return remote(
            ids.at[stream, 0],
            ids.at[stream, slot],
            wrap_id_sem.at[stream],
            id_recv_sem.at[stream, slot],
            target,
        )

    def wrap(stream, c, far):
        _, slot, target = wrap_route(stream)

        @pl.when(far)
        def _():
            remote(
                chunk(stream, 0, c),
                chunk(stream, slot, c),
                wrap_sem.at[stream],
                recv_sem.at[stream, slot, c],
                target,
            ).start()

    def wrap_early(stream):
        to_edge, far = wrap_distance(stream)

        @pl.when(far)
        def _():
            wrap_id_copy(stream).start()

        for c in range(WAVES):
            now = far & (to_edge < PATIENT[stream])
            for which, owner, _, _, waves in DETOURS:
                if which == stream and c in waves:
                    now = now & (to_edge != owner)
            wrap(stream, c, now)

    def wrap_late(other, s, c):
        for stream in range(2):
            to_edge, far = wrap_distance(stream)
            now = far & (to_edge >= PATIENT[stream]) & (other == 1 - stream) & (s == SPAN - 1)
            for which, owner, _, _, waves in DETOURS:
                if which == stream:
                    kept = functools.reduce(jnp.logical_and, [c != wave for wave in waves])
                    now = now & ((to_edge != owner) | kept)
            wrap(stream, c, now)

    def detour_copy(n, c):
        stream, owner, sender, s, _ = DETOURS[n]
        slot = owner if owner < SPAN else owner + 1
        return remote(
            chunk(stream, s, c),
            chunk(stream, slot, c),
            detour_sem.at[n],
            recv_sem.at[stream, slot, c],
            device(*wrap_target(stream, owner, sender)),
        )

    def detour(stream, s, c):
        for n, (which, _, sender, slot, waves) in enumerate(DETOURS):
            place = RUN - sender if which == 0 else sender - 1
            now = functools.reduce(jnp.logical_or, [c == wave for wave in waves])

            @pl.when((stream == which) & (s == slot) & (j == place) & now)
            def _():
                detour_copy(n, c).start()

    for c in range(WAVES):
        forward(0, 0, c)

        @pl.when(j != 0)
        def _():
            forward(1, 0, c)

    wrap_early(0)

    def cross():
        pl.semaphore_wait(ready_sem, ready_count)
        for c in range(WAVES):

            @pl.when(j == 0)
            def _():
                forward(1, 0, c)

        wrap_early(1)

    row = lax.broadcasted_iota(jnp.int32, (128, 128), 0)
    lane = lax.broadcasted_iota(jnp.int32, (128, 128), 1)
    for stream, own in ((0, text_ids), (1, image_ids)):
        for half in range(rows // 128):
            line = jnp.broadcast_to(own[half : half + 1, :].astype(jnp.float32), (128, 128))
            column = jnp.sum(jnp.where(row == lane, line, 0.0), axis=-1, keepdims=True)
            own_ids[stream, pl.ds(half * 128, 128), :] = jnp.broadcast_to(column, (128, 128))
        total[stream] = jnp.zeros(total.shape[1:], jnp.float32)

    scale = jnp.exp(jnp.full((1, 128), sharpness[0], jnp.float32))[:, :1]
    shift = offset[0]
    weight = -(adjoint[0] * scale / rows)
    group = SPAN * piece
    turn = lax.broadcasted_iota(jnp.int32, (1, 128), 1) // piece

    def compute(stream, c, half):
        mine = 1 - stream
        visitors = buf[stream, c, pl.ds(pl.multiple_of(half * group, group), group), :]
        grid = lax.dot_general(
            hat[mine], visitors, (((1,), (1,)), ((), ())), preferred_element_type=jnp.float32
        )
        logit = scale * grid + shift
        column = own_ids[mine, :, :]
        parts = []
        for at in range(0, group, 128):
            s = half * SPAN + at // piece
            line = ids[stream, s, c]
            for other in range(1, 128 // piece):
                line = jnp.where(turn == other, ids[stream, s + other, c], line)
            match = column == jnp.broadcast_to(line, (rows, 128))
            here = logit[:, at : at + 128]
            signed = jnp.where(match, here, -here)
            parts.append(jnp.where(match, weight, -weight) * (1.0 / (1.0 + jnp.exp(signed))))
        coef = jnp.concatenate(parts, axis=1).astype(jnp.bfloat16)
        total[mine] += jnp.dot(coef, visitors, preferred_element_type=jnp.float32)

    words = []
    line = lax.rem(g, LINE)
    turn_at = 2 * j + lax.div(k, RUN)
    for i in range(len(ORDER[0])):
        word = jnp.int32(0)
        for row in reversed(range(LINE)):
            entries = [ORDER[row * 2 * RUN + place][i] for place in range(2 * RUN)]
            entry = jnp.int32(entries[0])
            for place in range(1, 2 * RUN):
                if entries[place] != entries[place - 1]:
                    entry = jnp.where(turn_at >= place, entries[place], entry)
            word = entry if row == LINE - 1 else jnp.where(line == row, entry, word)
        words.append(word)

    def step(i, carry):
        word = words[0]
        for other in range(1, len(words)):
            word = jnp.where(i == other, words[other], word)

        @pl.when(lax.rem(word, 64) == 1)
        def _():
            cross()

        for _ in range(4):
            entry = lax.rem(word, 64)
            word = lax.div(word, 64)
            stream = lax.div(entry, 32)
            s = lax.rem(lax.div(entry, 4), 8)
            c = lax.rem(entry, 4)

            @pl.when(entry > 1)
            def _():
                receive(stream, s, c)
                forward(stream, s, c)
                wrap_late(stream, s, c)
                detour(stream, s, c)

        @pl.when(word > 0)
        def _():
            product = word - 1
            compute(lax.div(product, 8), lax.div(lax.rem(product, 8), 2), lax.rem(product, 2))

        return carry

    lax.fori_loop(0, len(words), step, 0)

    for stream, out in ((1, grad_image), (0, grad_text)):
        for c in range(WAVES):
            part = pl.ds(c * piece, piece)
            inv = inverse[stream, part, :][:, :1]
            unit = raw[stream, part, :].astype(jnp.float32) * inv
            grad = total[stream, part, :]
            along = jnp.sum(unit * grad, axis=-1, keepdims=True)
            out[part, :] = inv * (grad - unit * along)

    for stream in range(2):
        for s in range(SLOTS - 1):
            for reach in (2, 1):
                target, goes = route(stream, s, reach)

                @pl.when(goes)
                def _():
                    id_copy(stream, s, reach, target).wait_send()
                    remote(
                        hat.at[stream],
                        hat.at[stream],
                        send_sem.at[reach - 1, stream, s],
                        recv_sem.at[stream, s + 1, 0],
                        target,
                    ).wait_send()

        far, slot, target = wrap_route(stream)

        @pl.when(far)
        def _():
            wrap_id_copy(stream).wait_send()

        for distance in range(2, SLOTS - 1):
            away = [len(d[4]) for d in DETOURS if d[0] == stream and d[1] == distance]
            amount = rows - piece * sum(away)
            if amount:

                @pl.when(wrap_distance(stream)[0] == distance)
                def _():
                    part = hat.at[stream, pl.ds(0, amount)]
                    remote(
                        part, part, wrap_sem.at[stream], recv_sem.at[stream, slot, 0], target
                    ).wait_send()

    for n, (stream, _, sender, _, waves) in enumerate(DETOURS):

        @pl.when(j == (RUN - sender if stream == 0 else sender - 1))
        def _():
            part = hat.at[stream, pl.ds(0, piece * len(waves))]
            target = device(0, 1 - 2 * stream)
            remote(
                part, part, detour_sem.at[n], recv_sem.at[stream, 1, 0], target
            ).wait_send()


def body(n_grp, n_blk, image_emb, text_emb, image_pair_index, text_ids, sharpness, offset, adjoint):
    rows, width = image_emb.shape
    vmem = pl.BlockSpec(memory_space=pltpu.VMEM)
    smem = pl.BlockSpec(memory_space=pltpu.SMEM)
    hbm = pl.BlockSpec(memory_space=pltpu.HBM)
    flops = 4 * SLOTS * 2 * rows * rows * width
    return pl.pallas_call(
        functools.partial(kernel, n_grp, n_blk),
        out_shape=(
            jax.ShapeDtypeStruct((rows, width), jnp.float32),
            jax.ShapeDtypeStruct((rows, width), jnp.float32),
        ),
        in_specs=[hbm, hbm, vmem, vmem, smem, smem, smem],
        out_specs=(vmem, vmem),
        scratch_shapes=[
            pltpu.VMEM((2, rows, width), jnp.bfloat16),
            pltpu.VMEM((2, rows, width), jnp.bfloat16),
            pltpu.VMEM((2, WAVES, SLOTS * rows // WAVES, width), jnp.bfloat16),
            pltpu.VMEM((2, SLOTS, WAVES, 1, 128), jnp.float32),
            pltpu.VMEM((2, rows, 128), jnp.float32),
            pltpu.VMEM((2, rows, 128), jnp.float32),
            pltpu.VMEM((2, rows, width), jnp.float32),
            pltpu.SemaphoreType.DMA((2,)),
            pltpu.SemaphoreType.DMA((2, 2, SLOTS)),
            pltpu.SemaphoreType.DMA((2, 2, SLOTS)),
            pltpu.SemaphoreType.DMA((2,)),
            pltpu.SemaphoreType.DMA((2,)),
            pltpu.SemaphoreType.DMA((max(1, len(DETOURS)),)),
            pltpu.SemaphoreType.REGULAR,
            pltpu.SemaphoreType.DMA((2, SLOTS, WAVES)),
            pltpu.SemaphoreType.DMA((2, SLOTS)),
        ],
        compiler_params=pltpu.CompilerParams(
            collective_id=0, has_side_effects=True, vmem_limit_bytes=60 * 1024 * 1024
        ),
        cost_estimate=pl.CostEstimate(
            flops=flops, bytes_accessed=12 * rows * width, transcendentals=2 * SLOTS * rows * rows
        ),
    )(
        image_emb,
        text_emb,
        image_pair_index.reshape(rows // 128, 128),
        text_ids.reshape(rows // 128, 128),
        sharpness,
        offset,
        adjoint,
    )


def solution(mesh):
    both = ("grp", "blk")
    return jax.shard_map(
        functools.partial(body, mesh.shape["grp"], mesh.shape["blk"]),
        mesh=mesh,
        in_specs=(P(both, None), P(both, None), P(both), P(both), P(), P(), P()),
        out_specs=(P(both, None), P(both, None)),
        check_vma=False,
    )
```

time: 102 us -> 103 us (level)
  the two profiles are of different devices: /device:TPU:377 before, /device:TPU:480 now
where the time goes in v5:
time: 103 us; the launch traced here: 102 us
  Pallas kernels  96.4 us (94%)
  local copies, waits for them, and re-layouts  3.47 us (3%)
  between operations  2.58 us (3%)
    pallas_call x1, Pallas kernels, body(): pl.pallas_call(functools.partial(kernel, n_grp, n_blk), out_shape=(jax.Sh...  96.4 us
    unnamed x4, local copies, waits for them, and re-layouts  3.47 us

profile of v5, /device:TPU:480, one launch (start us, length us, event | category | flops | bytes accessed | tf_op | source)
XLA Modules:
  0.0 102.5 jit_solution(4341794932294475753)
XLA Ops:
  2.6 96.4 %shard_map.86 = (f32[256,1152]{1,0:T(8,128)}, f32[256,1152]{1,0:T(8,128)}) custom-call(bf16[256,1152]{1,0:T(8,128)(2,1)} %image_hbm.1, bf16[256,1152]{1,0:T(8,128)(2,1)} %text_hbm.1, s32[2,128]{1,0:T(2,128)} %bitcast.2, s32[2,128]{1,0:T(2,128)} %bitcast.3, f32[1]{0:T(128)S(6)} %copy.11.sharpness, f32[1]{0:T(128)S(6)} %copy.12.offset, f32[1]{0:T(128)S(6)} %copy.13.adjoint), custom_call_target="tpu_custom_call" | custom-call | flops 4831838208 | bytes 3538944 | tf_op jit(solution)/shard_map/pallas_call | solution.py:1105
  99.0 0.0 copy-start
  99.0 2.5 %copy.14 = f32[256,1152]{1,0:T(8,128)} copy(f32[256,1152]{1,0:T(8,128)} %get-tuple-element.4) | data formatting | bytes 2359296
  101.5 0.0 copy-done
  101.5 1.0 copy.15
Async XLA Ops:
  99.0 2.5 %copy-start = (f32[256,1152]{1,0:T(8,128)S(1)}, f32[256,1152]{1,0:T(8,128)}, u32[]{:S(2)}) copy-start(f32[256,1152]{1,0:T(8,128)} %get-tuple-element.5) | copy-start | bytes 3538948
